TPU v7x, 32 devices: a whole 2x2x4 slice. The times are simulated.
32 devices in a mesh: dp: 16 (over z, y, x), seq: 2 (over core).
Axes of the slice: x: 2, y: 2, z: 4, core: 2. Of those that a mesh axis runs over, the one named last changes fastest.
Arguments:
- inputs: bfloat16 [16, 256, 1024], P('dp', 'seq'), may hold values from -6 to 6
- segments: int32 [16, 256], P('dp', 'seq'), may hold values from 0 to 2, as said below
- cotangent: bfloat16 [16, 256, 1024], P('dp', 'seq'), may hold values from -6 to 6
- ln1_gain: bfloat16 [1024], P(('dp', 'seq')), may hold values from 0.5 to 1.5
- w_qkv: bfloat16 [3145728], P(('dp', 'seq')), may hold values from -0.1875 to 0.1875
- w_attn_out: bfloat16 [1048576], P(('dp', 'seq')), may hold values from -1 to 1
- ln2_gain: bfloat16 [1024], P(('dp', 'seq')), may hold values from 0.5 to 1.5
- w_in: bfloat16 [5373952], P(('dp', 'seq')), may hold values from -0.1875 to 0.1875
- w_mlp_out: bfloat16 [2686976], P(('dp', 'seq')), may hold values from -0.125 to 0.125
Outputs:
- output: bfloat16 [16, 256, 1024], P('dp', 'seq')
- input_grad: float32 [16, 256, 1024], P('dp', 'seq')
- ln1_gain_grad: float32 [1024], P(('dp', 'seq'))
- w_qkv_grad: float32 [3145728], P(('dp', 'seq'))
- w_attn_out_grad: float32 [1048576], P(('dp', 'seq'))
- ln2_gain_grad: float32 [1024], P(('dp', 'seq'))
- w_in_grad: float32 [5373952], P(('dp', 'seq'))
- w_mlp_out_grad: float32 [2686976], P(('dp', 'seq'))
Inputs may be any that keep to these rules, and one draw needn't show every extreme that they name: `segments`: along a packed sequence the numbers never fall, and 0, 1 and 2 all occur in each.
All inputs are finite; a program needn't handle non-finite values.
Results may differ from a plain program's by a relative error of at most 0.022.
Values may be sent and summed in bfloat16 or wider, within the bound.
A program may use at most 192 MiB of HBM per device.

v0:
```python
import math

import jax
import jax.numpy as jnp
from jax import lax
from jax.sharding import PartitionSpec as P

HEADS = 16
HD = 64
FF = 2624


EPSILON = 1e-05
ROPE_BASE = 160000.0


def rope_tables(places):
    freqs = 1.0 / ROPE_BASE ** (jnp.arange(0, HD, 2, dtype=jnp.float32) / HD)
    angles = places[:, None] * freqs[None, :]
    angles = jnp.concatenate([angles, angles], axis=1)
    return (jnp.cos(angles), jnp.sin(angles))


def rotate(values_in, cosines, sines):
    halfway = values_in.shape[-1] // 2
    turned = jnp.concatenate([-values_in[..., halfway:], values_in[..., :halfway]], axis=-1)
    return values_in * cosines[:, None, :] + turned * sines[:, None, :]


def rotate_back(grads_in, cosines, sines):
    halfway = grads_in.shape[-1] // 2
    scaled = grads_in * sines[:, None, :]
    turned = jnp.concatenate([scaled[..., halfway:], -scaled[..., :halfway]], axis=-1)
    return grads_in * cosines[:, None, :] + turned


def norm_forward(values_in, gain):
    centred = values_in - jnp.mean(values_in, axis=-1, keepdims=True)
    inv_spread = lax.rsqrt(jnp.mean(centred * centred, axis=-1, keepdims=True) + EPSILON)
    unit_rows = centred * inv_spread
    return (unit_rows * gain, unit_rows, inv_spread)


def norm_back(grad_rows, unit_rows, inv_spread, gain):
    gain_grad = jnp.sum(grad_rows * unit_rows, axis=0)
    scaled = grad_rows * gain
    inner_mean = jnp.mean(scaled, axis=-1, keepdims=True)
    cross_mean = jnp.mean(scaled * unit_rows, axis=-1, keepdims=True)
    return (gain_grad, inv_spread * (scaled - inner_mean - unit_rows * cross_mean))


def matmul_tn(left, right):
    return lax.dot_general(
        left, right, (((0,), (0,)), ((), ())), preferred_element_type=jnp.float32
    )


def matmul_nt(left, right):
    return lax.dot_general(
        left, right, (((1,), (1,)), ((), ())), preferred_element_type=jnp.float32
    )


def masked_scores(query, key_block, seg_query, seg_block):
    scores = (
        jnp.einsum("qhd,khd->hqk", query, key_block, preferred_element_type=jnp.float32) * 0.125
    )
    same_doc = seg_query[:, None] == seg_block[None, :]
    return jnp.where(same_doc[None], scores, -1e30)


def gated(inner, gate):
    return jax.nn.gelu(inner, approximate=False) * gate


def per_device(inputs, segments, cotangent, ln1_gain, w_qkv, w_attn_out, ln2_gain, w_in, w_mlp_out):
    tok_rows = inputs.shape[1]
    model_width = inputs.shape[2]
    seq_devices = lax.axis_size("seq")
    dp_devices = lax.axis_size("dp")
    tokens_in = inputs[0].astype(jnp.float32)
    seg_send = segments.astype(jnp.bfloat16)
    seg_query = seg_send[0]
    gathered_attn = (
        lax.all_gather(ln1_gain, ("dp", "seq"), axis=0, tiled=True),
        lax.all_gather(w_qkv, ("dp", "seq"), axis=0, tiled=True),
        lax.all_gather(w_attn_out, ("dp", "seq"), axis=0, tiled=True),
    )
    gain_one = gathered_attn[0].astype(jnp.float32)
    qkv_mat = gathered_attn[1].reshape(model_width, 3 * model_width)
    proj_mat = gathered_attn[2].reshape(model_width, model_width)
    places = (lax.axis_index("seq") * tok_rows + jnp.arange(tok_rows, dtype=jnp.int32)).astype(
        jnp.float32
    )
    cosines, sines = rope_tables(places)
    normed_one, unit_one, spread_one = norm_forward(tokens_in, gain_one)
    normed_one_low = normed_one.astype(jnp.bfloat16)
    qkv_rows = jnp.dot(normed_one_low, qkv_mat, preferred_element_type=jnp.float32)
    query = rotate(qkv_rows[:, :model_width].reshape(tok_rows, HEADS, HD), cosines, sines).astype(
        jnp.bfloat16
    )
    key_rot = rotate(
        qkv_rows[:, model_width : 2 * model_width].reshape(tok_rows, HEADS, HD), cosines, sines
    ).astype(jnp.bfloat16)
    value_rows = qkv_rows[:, 2 * model_width :].astype(jnp.bfloat16)
    key_send = key_rot.reshape(1, tok_rows, model_width)
    value_send = value_rows.reshape(1, tok_rows, model_width)
    fwd_init = (
        jnp.full((HEADS, tok_rows), -1e30, jnp.float32),
        jnp.zeros((HEADS, tok_rows), jnp.float32),
        jnp.zeros((tok_rows, HEADS, HD), jnp.float32),
    )
    key_piece = lax.all_gather(key_send, "seq", axis=1, tiled=True)
    value_piece = lax.all_gather(value_send, "seq", axis=1, tiled=True)
    seg_piece = lax.all_gather(seg_send, "seq", axis=1, tiled=True)
    span = key_piece.shape[1]
    step_rows = math.gcd(span, 512)

    def one_block(block_id, inner_state):
        top_score, total, accum = inner_state
        begin = block_id * step_rows
        key_block = lax.dynamic_slice_in_dim(key_piece[0], begin, step_rows, 0).reshape(
            step_rows, HEADS, HD
        )
        value_block = lax.dynamic_slice_in_dim(value_piece[0], begin, step_rows, 0).reshape(
            step_rows, HEADS, HD
        )
        seg_block = lax.dynamic_slice_in_dim(seg_piece[0], begin, step_rows, 0)
        scores = masked_scores(query, key_block, seg_query, seg_block)
        new_top = jnp.maximum(top_score, jnp.max(scores, axis=-1))
        fading = jnp.exp(top_score - new_top)
        weights = jnp.exp(scores - new_top[..., None])
        total = total * fading + jnp.sum(weights, axis=-1)
        accum = accum * fading.T[:, :, None] + jnp.einsum(
            "hqk,khd->qhd",
            weights.astype(jnp.bfloat16),
            value_block,
            preferred_element_type=jnp.float32,
        )
        return (new_top, total, accum)

    fwd_state = lax.fori_loop(0, span // step_rows, one_block, fwd_init)
    run_top, run_total, run_accum = fwd_state
    log_total = run_top + jnp.log(run_total)
    attended = (run_accum / run_total.T[:, :, None]).astype(jnp.bfloat16)
    attended_rows = attended.reshape(tok_rows, model_width)
    middle = tokens_in + jnp.dot(attended_rows, proj_mat, preferred_element_type=jnp.float32)
    gathered_mlp = (
        lax.all_gather(ln2_gain, ("dp", "seq"), axis=0, tiled=True),
        lax.all_gather(w_in, ("dp", "seq"), axis=0, tiled=True),
        lax.all_gather(w_mlp_out, ("dp", "seq"), axis=0, tiled=True),
    )
    gain_two = gathered_mlp[0].astype(jnp.float32)
    in_mat = gathered_mlp[1].reshape(model_width, 2 * FF)
    down_mat = gathered_mlp[2].reshape(FF, model_width)
    normed_two, unit_two, spread_two = norm_forward(middle, gain_two)
    normed_two_low = normed_two.astype(jnp.bfloat16)
    upper = jnp.dot(normed_two_low, in_mat, preferred_element_type=jnp.float32)
    inner = upper[:, :FF]
    gate = upper[:, FF:]
    hidden_low = gated(inner, gate).astype(jnp.bfloat16)
    output = (middle + jnp.dot(hidden_low, down_mat, preferred_element_type=jnp.float32)).astype(
        jnp.bfloat16
    )
    gathered_mlp = (
        lax.all_gather(ln2_gain, ("dp", "seq"), axis=0, tiled=True),
        lax.all_gather(w_in, ("dp", "seq"), axis=0, tiled=True),
        lax.all_gather(w_mlp_out, ("dp", "seq"), axis=0, tiled=True),
    )
    gain_two = gathered_mlp[0].astype(jnp.float32)
    in_mat = gathered_mlp[1].reshape(model_width, 2 * FF)
    down_mat = gathered_mlp[2].reshape(FF, model_width)
    grad_low = cotangent[0]
    grad_rows = grad_low.astype(jnp.float32)
    d_hidden = matmul_nt(grad_low, down_mat)
    grad_down = matmul_tn(hidden_low, grad_low)
    gated_value, pull = jax.vjp(gated, inner, gate)
    d_inner, d_gate = pull(d_hidden)
    d_upper_low = jnp.concatenate([d_inner, d_gate], axis=1).astype(jnp.bfloat16)
    grad_in = matmul_tn(normed_two_low, d_upper_low)
    d_normed_two = matmul_nt(d_upper_low, in_mat)
    grad_gain_two, d_middle_part = norm_back(d_normed_two, unit_two, spread_two, gain_two)
    d_middle = grad_rows + d_middle_part
    mlp_parts = tuple(
        (g.reshape(dp_devices, seq_devices, -1) for g in (grad_gain_two, grad_in, grad_down))
    )
    mlp_mid = (
        lax.psum_scatter(
            mlp_parts[0].astype(jnp.bfloat16), "seq", scatter_dimension=1, tiled=True
        ).astype(jnp.float32),
        lax.psum_scatter(
            mlp_parts[1].astype(jnp.bfloat16), "seq", scatter_dimension=1, tiled=True
        ).astype(jnp.float32),
        lax.psum_scatter(
            mlp_parts[2].astype(jnp.bfloat16), "seq", scatter_dimension=1, tiled=True
        ).astype(jnp.float32),
    )
    mlp_shards = (
        lax.psum_scatter(
            mlp_mid[0].astype(jnp.bfloat16), "dp", scatter_dimension=0, tiled=True
        ).astype(jnp.float32),
        lax.psum_scatter(
            mlp_mid[1].astype(jnp.bfloat16), "dp", scatter_dimension=0, tiled=True
        ).astype(jnp.float32),
        lax.psum_scatter(
            mlp_mid[2].astype(jnp.bfloat16), "dp", scatter_dimension=0, tiled=True
        ).astype(jnp.float32),
    )
    gathered_attn = (
        lax.all_gather(ln1_gain, ("dp", "seq"), axis=0, tiled=True),
        lax.all_gather(w_qkv, ("dp", "seq"), axis=0, tiled=True),
        lax.all_gather(w_attn_out, ("dp", "seq"), axis=0, tiled=True),
    )
    gain_one = gathered_attn[0].astype(jnp.float32)
    qkv_mat = gathered_attn[1].reshape(model_width, 3 * model_width)
    proj_mat = gathered_attn[2].reshape(model_width, model_width)
    d_branch_low = d_middle.astype(jnp.bfloat16)
    grad_proj = matmul_tn(attended_rows, d_branch_low)
    d_attended = matmul_nt(d_branch_low, proj_mat).astype(jnp.bfloat16).reshape(tok_rows, HEADS, HD)
    delta_rows = jnp.einsum(
        "qhd,qhd->hq", d_attended.astype(jnp.float32), attended.astype(jnp.float32)
    )
    back_init = (
        jnp.zeros((tok_rows, HEADS, HD), jnp.float32),
        jnp.zeros((tok_rows * seq_devices, 2 * model_width), jnp.float32),
    )
    attend_key_piece = lax.all_gather(key_send, "seq", axis=1, tiled=True)
    attend_value_piece = lax.all_gather(value_send, "seq", axis=1, tiled=True)
    attend_seg_piece = lax.all_gather(seg_send, "seq", axis=1, tiled=True)
    span = attend_key_piece.shape[1]
    attend_step_rows = math.gcd(span, 512)

    def one_block(block_id, inner_state):
        grad_query, grad_kv = inner_state
        begin = block_id * attend_step_rows
        key_block = lax.dynamic_slice_in_dim(
            attend_key_piece[0], begin, attend_step_rows, 0
        ).reshape(attend_step_rows, HEADS, HD)
        value_block = lax.dynamic_slice_in_dim(
            attend_value_piece[0], begin, attend_step_rows, 0
        ).reshape(attend_step_rows, HEADS, HD)
        seg_block = lax.dynamic_slice_in_dim(attend_seg_piece[0], begin, attend_step_rows, 0)
        scores = masked_scores(query, key_block, seg_query, seg_block)
        probs = jnp.exp(scores - log_total[..., None])
        probs_low = probs.astype(jnp.bfloat16)
        value_grad = jnp.einsum(
            "hqk,qhd->khd", probs_low, d_attended, preferred_element_type=jnp.float32
        )
        d_probs = jnp.einsum(
            "qhd,khd->hqk", d_attended, value_block, preferred_element_type=jnp.float32
        )
        d_scores = (probs * (d_probs - delta_rows[..., None])).astype(jnp.bfloat16)
        grad_query = (
            grad_query
            + jnp.einsum("hqk,khd->qhd", d_scores, key_block, preferred_element_type=jnp.float32)
            * 0.125
        )
        key_grad = (
            jnp.einsum("hqk,qhd->khd", d_scores, query, preferred_element_type=jnp.float32) * 0.125
        )
        block_grads = jnp.concatenate(
            [
                key_grad.reshape(attend_step_rows, model_width),
                value_grad.reshape(attend_step_rows, model_width),
            ],
            axis=1,
        )
        grad_kv = lax.dynamic_update_slice_in_dim(grad_kv, block_grads, begin, 0)
        return (grad_query, grad_kv)

    back_state = lax.fori_loop(0, span // attend_step_rows, one_block, back_init)
    kv_grads = lax.psum_scatter(
        back_state[1].astype(jnp.bfloat16), "seq", scatter_dimension=0, tiled=True
    ).astype(jnp.float32)
    d_query = rotate_back(back_state[0], cosines, sines).reshape(tok_rows, model_width)
    d_key = rotate_back(
        kv_grads[:, :model_width].reshape(tok_rows, HEADS, HD), cosines, sines
    ).reshape(tok_rows, model_width)
    d_qkv_low = jnp.concatenate([d_query, d_key, kv_grads[:, model_width:]], axis=1).astype(
        jnp.bfloat16
    )
    grad_qkv = matmul_tn(normed_one_low, d_qkv_low)
    d_normed_one = matmul_nt(d_qkv_low, qkv_mat)
    grad_gain_one, d_input_part = norm_back(d_normed_one, unit_one, spread_one, gain_one)
    input_grad = d_middle + d_input_part
    attn_parts = tuple(
        (g.reshape(dp_devices, seq_devices, -1) for g in (grad_gain_one, grad_qkv, grad_proj))
    )
    attn_mid = (
        lax.psum_scatter(
            attn_parts[0].astype(jnp.bfloat16), "seq", scatter_dimension=1, tiled=True
        ).astype(jnp.float32),
        lax.psum_scatter(
            attn_parts[1].astype(jnp.bfloat16), "seq", scatter_dimension=1, tiled=True
        ).astype(jnp.float32),
        lax.psum_scatter(
            attn_parts[2].astype(jnp.bfloat16), "seq", scatter_dimension=1, tiled=True
        ).astype(jnp.float32),
    )
    attn_shards = (
        lax.psum_scatter(
            attn_mid[0].astype(jnp.bfloat16), "dp", scatter_dimension=0, tiled=True
        ).astype(jnp.float32),
        lax.psum_scatter(
            attn_mid[1].astype(jnp.bfloat16), "dp", scatter_dimension=0, tiled=True
        ).astype(jnp.float32),
        lax.psum_scatter(
            attn_mid[2].astype(jnp.bfloat16), "dp", scatter_dimension=0, tiled=True
        ).astype(jnp.float32),
    )
    return (
        output.reshape(1, tok_rows, model_width),
        input_grad.reshape(1, tok_rows, model_width),
        attn_shards[0].reshape(-1),
        attn_shards[1].reshape(-1),
        attn_shards[2].reshape(-1),
        mlp_shards[0].reshape(-1),
        mlp_shards[1].reshape(-1),
        mlp_shards[2].reshape(-1),
    )


def solution(mesh):
    placed = (
        P("dp", "seq", None),
        P("dp", "seq"),
        P("dp", "seq", None),
        P(("dp", "seq")),
        P(("dp", "seq")),
        P(("dp", "seq")),
        P(("dp", "seq")),
        P(("dp", "seq")),
        P(("dp", "seq")),
    )
    return jax.shard_map(
        per_device,
        mesh=mesh,
        in_specs=placed,
        out_specs=(
            P("dp", "seq", None),
            P("dp", "seq", None),
            P(("dp", "seq")),
            P(("dp", "seq")),
            P(("dp", "seq")),
            P(("dp", "seq")),
            P(("dp", "seq")),
            P(("dp", "seq")),
        ),
        check_vma=False,
    )
```

profile of v0, /device:TPU:0, one launch (start us, length us, event | category | flops | bytes accessed | tf_op | source)
XLA Modules:
  0.0 1159.9 jit_solution(5142067568363791124)
XLA Ops:
  8.0 0.7 all-gather.13.cloned.1.call-update
  10.0 0.8 dynamic-update-slice
  10.9 0.8 dynamic-update-slice.1
  11.7 42.0 %all-reduce.8 = (bf16[1024]{0:T(1024)(128)(2,1)S(1)}, bf16[1024]{0:T(1024)(128)(2,1)S(1)}) all-reduce(bf16[1024]{0:T(1024)(128)(2,1)S(1)} %dynamic-update-slice, bf16[1024]{0:T(1024)(128)(2,1)S(1)} %dynamic-update-slice.1), channel_id=1, replica_groups=mesh['dp'=16,'seq'=2] {'dp','seq'}, use_global_device_ids=true, to_apply=%add | all-reduce | flops 2048 | bytes 8192
  53.8 0.7 broadcast_multiply_fusion.3
  54.6 1.0 copy.66
  55.6 1.8 all_gather.38
  57.8 12.3 %all-gather.9.cloned.1.call-done = bf16[1048576]{0:T(1024)(128)(2,1)} async-done(((bf16[32768]{0:T(1024)(128)(2,1)}), bf16[1048576]{0:T(1024)(128)(2,1)}) %all-gather.9.cloned.1.call-update) | async-done | bytes 2097168 | tf_op jit(solution)/shard_map/all_gather | solution.py:87
  70.1 4.2 reshape.331
  74.3 63.3 %all-gather.13.cloned.1.call-done = bf16[2686976]{0:T(1024)(128)(2,1)} async-done(((bf16[83968]{0:T(1024)(128)(2,1)}), bf16[2686976]{0:T(1024)(128)(2,1)}) %all-gather.13.cloned.1.call-update) | async-done | bytes 5373968 | tf_op jit(solution)/shard_map/all_gather | solution.py:151
  137.6 9.2 reshape.333
  146.8 62.1 %all-gather.7.cloned.1.call-done = bf16[3145728]{0:T(1024)(128)(2,1)} async-done(((bf16[98304]{0:T(1024)(128)(2,1)}), bf16[3145728]{0:T(1024)(128)(2,1)}) %all-gather.7.cloned.1.call-update) | async-done | bytes 6291472 | tf_op jit(solution)/shard_map/all_gather | solution.py:86
  208.9 10.4 reshape.324
  219.3 3.9 fusion.46
  223.2 2.2 all-gather.1
  225.9 1.0 copy.68
  226.9 1.2 add_convert_fusion.1
  228.1 2.2 all-gather
  233.2 1.0 copy-done
  235.0 62.8 %all-gather.11.cloned.1.call-done = bf16[5373952]{0:T(1024)(128)(2,1)} async-done(((bf16[167936]{0:T(1024)(128)(2,1)}), bf16[5373952]{0:T(1024)(128)(2,1)}) %all-gather.11.cloned.1.call-update) | async-done | bytes 10747920 | tf_op jit(solution)/shard_map/all_gather | solution.py:150
  297.9 19.9 %reshape.332 = bf16[1024,5248]{1,0:T(8,128)(2,1)} reshape(bf16[5373952]{0:T(1024)(128)(2,1)} %all-gather.11.cloned.1.call-done) | data formatting | bytes 21495808 | tf_op jit(solution)/shard_map/reshape | solution.py:154
  317.7 5.9 fusion.71
  323.6 7.9 add_convert_fusion
  331.6 1.3 multiply_convert_fusion.1
  332.9 5.7 multiply_reduce_fusion
  338.9 1.5 convolution_convert_fusion.5
  340.4 1.8 copy.73
  342.2 1.1 fusion.43
  343.4 1.6 convolution_convert_fusion.4
  345.0 1.0 multiply_convert_fusion
  346.0 0.9 copy-done.3
  347.4 1.4 copy.95
  349.0 1.6 convolution_convert_fusion.3
  350.7 2.8 convert_element_type.164
  353.5 4.1 copy.78
  357.7 1.0 copy-done.5
  358.7 4.0 convolution_convert_fusion.1
  362.7 8.7 convert_element_type.170
  371.4 6.4 copy.84
  377.9 1.1 copy-done.4
  379.0 1.5 broadcast_multiply_fusion
  380.7 1.1 fusion.75
  383.0 5.2 convolution_convert_fusion.2
  388.2 12.9 %convert_element_type.162 = bf16[16,2,98304]{2,1,0:T(2,128)(2,1)} reshape(bf16[1024,3072]{1,0:T(8,128)(2,1)} %convolution_convert_fusion.2) | data formatting | bytes 12582912 | tf_op jit(solution)/shard_map/convert_element_type | solution.py:294
  401.1 8.9 copy.76
  410.1 1.0 copy-done.9
  411.1 8.6 convolution_convert_fusion
  419.7 14.3 %convert_element_type.168 = bf16[16,2,167936]{2,1,0:T(2,128)(2,1)} reshape(bf16[1024,5248]{1,0:T(8,128)(2,1)} %convolution_convert_fusion) | data formatting | bytes 21495808 | tf_op jit(solution)/shard_map/convert_element_type | solution.py:192
  434.0 11.1 copy.82
  446.5 5.8 fusion.33
  453.3 4.8 copy.79
  458.1 8.9 copy.85
  467.0 6.8 copy.77
  473.9 10.8 copy.83
  485.9 4.2 fusion.15
  490.9 1.0 fusion.32
  492.6 77.5 %all-reduce.9 = (bf16[16,1,32]{2,1,0:T(2,128)(2,1)S(1)}, bf16[16,1,32]{2,1,0:T(2,128)(2,1)S(1)}) all-reduce(bf16[16,1,32]{2,1,0:T(2,128)(2,1)S(1)} %copy.75, bf16[16,1,32]{2,1,0:T(2,128)(2,1)S(1)} %copy.81), channel_id=6, replica_groups=mesh['dp'=16,'seq'=2] {'dp'}, use_global_device_ids=true, to_apply=%region_13.14.clone | all-reduce | flops 1024 | bytes 4096
  570.1 1.1 fusion.64
  571.2 1.1 fusion.66
  572.4 569.7 %all-reduce.13.cloned.1.call-done = (bf16[16,1,98304]{2,1,0:T(2,128)(2,1)}, bf16[16,1,32768]{2,1,0:T(2,128)(2,1)}, bf16[16,1,167936]{2,1,0:T(2,128)(2,1)}, bf16[16,1,83968]{2,1,0:T(2,128)(2,1)}) async-done(((bf16[16,1,98304]{2,1,0:T(2,128)(2,1)}, bf16[16,1,32768]{2,1,0:T(2,128)(2,1)}, bf16[16,1,167936]{2,1,0:T(2,128)(2,1)}, bf16[16,1,83968]{2,1,0:T(2,128)(2,1)}), (bf16[16,1,98304]{2,1,0:T(2,128)(2,1)}, ...) | async-done | bytes 12255248
  1142.1 2.8 dynamic-slice_convert_fusion.1
  1144.8 2.3 dynamic-slice_convert_fusion.3
  1147.1 2.7 dynamic-slice_convert_fusion.2
  1149.8 3.0 dynamic-slice_convert_fusion
  (150 shorter events, 14.1 us)
Async XLA Ops:
  7.2 48.4 %copy-start.29 = (s32[1,128]{1,0:T(1,128)S(1)}, s32[1,128]{1,0:T(1,128)}, u32[]{:S(2)}) copy-start(s32[1,128]{1,0:T(1,128)} %param.10) | copy-start | bytes 1540
  7.2 50.2 %copy-start.2 = (bf16[1,128,1024]{2,1,0:T(8,128)(2,1)S(1)}, bf16[1,128,1024]{2,1,0:T(8,128)(2,1)}, u32[]{:S(2)}) copy-start(bf16[1,128,1024]{2,1,0:T(8,128)(2,1)} %param.9) | copy-start | bytes 786436
  7.2 62.9 %all-gather.9.cloned.1.call-start = ((), (), s32[]{:S(2)}) async-start(), calls=%async_computation.8 | async-start | bytes 2162688 | tf_op jit(solution)/shard_map/all_gather | solution.py:87
  7.9 129.7 %all-gather.13.cloned.1.call-start = ((), (), s32[]{:S(2)}) async-start(), calls=%async_computation.10 | async-start | bytes 5541888 | tf_op jit(solution)/shard_map/all_gather | solution.py:151
  8.7 200.2 %all-gather.7.cloned.1.call-start = ((), (), s32[]{:S(2)}) async-start(), calls=%async_computation.7 | async-start | bytes 6488064 | tf_op jit(solution)/shard_map/all_gather | solution.py:86
  9.4 288.5 %all-gather.11.cloned.1.call-start = ((), (), s32[]{:S(2)}) async-start(), calls=%async_computation.9 | async-start | bytes 11083776 | tf_op jit(solution)/shard_map/all_gather | solution.py:150
  10.0 370.7 %reduce-scatter.22.cloned.1.call-start = ((), (), s32[]{:S(2)}) async-start(), calls=%async_computation.17 | async-start | bytes 1572864
  57.7 161.6 %copy-start.24 = (f32[128]{0:T(128)}, f32[128]{0:T(128)S(1)}, u32[]{:S(2)}) copy-start(f32[128]{0:T(128)S(1)} %add_rsqrt_fusion.1) | copy-start | bytes 1540
  225.6 7.0 copy-start.13
  225.9 1.1 copy-start.15
  230.5 0.8 copy-start.6
  230.9 1.0 copy-start.10
  232.6 1.6 copy-start
  233.2 1.6 copy-start.12
  235.0 103.6 %copy-start.26 = (f32[128]{0:T(128)}, f32[128]{0:T(128)S(1)}, u32[]{:S(2)}) copy-start(f32[128]{0:T(128)S(1)} %add_rsqrt_fusion) | copy-start | bytes 1540
  317.7 5.9 copy-start.16
  317.7 15.2 %slice-start = ((s8[10747904]{0:T(1024)(128)(4,1)}), s8[4194304]{0:T(1024)(128)(4,1)S(1)}, s32[]{:S(2)}) async-start(s8[10747904]{0:T(1024)(128)(4,1)} %bitcast.135), calls=%async_computation.19 | async-start | bytes 8388608
  323.6 9.3 slice-start.1
  323.6 9.3 slice-start.2
  332.9 5.7 copy-start.8
  332.9 6.0 copy-start.1
  343.4 1.6 copy-start.7
  343.4 1.6 copy-start.14
  345.0 2.0 copy-start.11
  346.0 1.0 copy-start.3
  348.8 104.5 %reduce-scatter.14.cloned.1.call-start = ((), (), s32[]{:S(2)}) async-start(), calls=%async_computation.13 | async-start | bytes 3145728 | tf_op jit(solution)/shard_map/reduce_scatter | solution.py:296
  357.6 1.1 copy-start.5
  357.6 1.2 copy-start.17
  357.6 100.5 %reduce-scatter.20.cloned.1.call-start = ((), (), s32[]{:S(2)}) async-start(), calls=%async_computation.16 | async-start | bytes 8060928 | tf_op jit(solution)/shard_map/reduce_scatter | solution.py:194
  377.8 1.2 copy-start.4
  377.8 1.2 copy-start.23
  377.8 89.2 %reduce-scatter.12.cloned.1.call-start = ((), (), s32[]{:S(2)}) async-start(), calls=%async_computation.12 | async-start | bytes 9437184 | tf_op jit(solution)/shard_map/reduce_scatter | solution.py:293
  380.7 1.8 copy-start.18
  382.3 0.7 copy-start.25
  382.5 5.7 copy-start.20
  410.0 1.1 copy-start.9
  410.0 1.1 copy-start.27
  410.0 63.8 %reduce-scatter.18.cloned.1.call-start = ((), (), s32[]{:S(2)}) async-start(), calls=%async_computation.15 | async-start | bytes 16121856 | tf_op jit(solution)/shard_map/reduce_scatter | solution.py:191
  445.1 0.7 copy-start.28
  445.1 1.4 copy-start.19
  445.1 1.4 copy-start.21
  445.1 45.0 %reduce-scatter.16.cloned.1.call-start = ((), (), s32[]{:S(2)}) async-start(), calls=%async_computation.14 | async-start | bytes 12288 | tf_op jit(solution)/shard_map/reduce_scatter | solution.py:188
  446.4 45.5 %reduce-scatter.10.cloned.1.call-start = ((), (), s32[]{:S(2)}) async-start(), calls=%async_computation.11 | async-start | bytes 12288 | tf_op jit(solution)/shard_map/reduce_scatter | solution.py:290
  453.0 689.0 %all-reduce.13.cloned.1.call-start = ((), (), s32[]{:S(2)}) async-start(), calls=%async_computation.18 | async-start | bytes 49020928
  484.7 0.7 copy-start.30
  485.9 4.9 copy-start.22
Sparse Core Ops, SparseCore 0:
  10.9 59.1 all-gather.8
  72.9 64.6 all-gather.12
  140.5 68.3 all-gather.6
  211.6 86.1 all-gather.10
  348.9 7.0 reduce-scatter.21
  358.2 10.7 reduce-scatter.13
  378.0 12.0 reduce-scatter.19
  410.2 13.4 reduce-scatter.11
  445.2 17.9 reduce-scatter.17
  465.9 8.6 reduce-scatter.15
  477.3 8.5 reduce-scatter.9
  492.2 649.8 all-reduce.12
where the time goes:
time: 1170 us; the launch traced here: 1160 us
  waiting for transfers between devices  773 us (66%)
  local copies, waits for them, and re-layouts  164 us (14%)
  blocking collectives  126 us (11%)
  matrix products  60.4 us (5%)
  other arithmetic  20.7 us (2%)
  between operations  15 us (1%)
    unnamed x14, waiting for transfers between devices  572 us
    unnamed x2, blocking collectives  120 us
    all_gather x1, waiting for transfers between devices, per_device(): lax.all_gather(w_mlp_out, ('dp', 'seq'), axis=0, tiled=True)  63.3 us
    all_gather x1, waiting for transfers between devices, per_device(): lax.all_gather(w_in, ('dp', 'seq'), axis=0, tiled=True)  62.8 us
    all_gather x1, waiting for transfers between devices, per_device(): lax.all_gather(w_qkv, ('dp', 'seq'), axis=0, tiled=True)  62.1 us
    convert_element_type x2, local copies, waits for them, and re-layouts, per_device(): mlp_parts[1].astype(jnp.bfloat16)  25.4 us
  transfers between devices with their start and end apart: 12, of which 5 were waited for; matrix products, arithmetic and copies ran while one was open for 15% of the time, Pallas kernels for 0%

commit v1 on v0

--- a/solution.py
+++ b/solution.py
@@ -1,8 +1,11 @@
+import functools
 import math
 
 import jax
 import jax.numpy as jnp
 from jax import lax
+from jax.experimental import pallas as pl
+from jax.experimental.pallas import tpu as pltpu
 from jax.sharding import PartitionSpec as P
 
 HEADS = 16
@@ -73,7 +76,7 @@
     return jax.nn.gelu(inner, approximate=False) * gate
 
 
-def per_device(inputs, segments, cotangent, ln1_gain, w_qkv, w_attn_out, ln2_gain, w_in, w_mlp_out):
+def general_device(inputs, segments, cotangent, ln1_gain, w_qkv, w_attn_out, ln2_gain, w_in, w_mlp_out):
     tok_rows = inputs.shape[1]
     model_width = inputs.shape[2]
     seq_devices = lax.axis_size("seq")
@@ -320,7 +323,801 @@
     )
 
 
+MESH_IDS = pl.DeviceIdType.MESH
+TOK = 128
+WIDTH = 1024
+PART = FF // 32
+PAD = 96
+HID = 8 * PAD
+QKV = 3 * 256
+BF = jnp.bfloat16
+F32 = jnp.float32
+
+
+def dot_nn(a, b):
+    return lax.dot_general(a, b, (((1,), (0,)), ((), ())), preferred_element_type=F32)
+
+
+def turned(u, low_half):
+    return jnp.where(low_half, pltpu.roll(u, 96, axis=1), pltpu.roll(u, 32, axis=1))
+
+
+def layer_kernel(
+    n_sems,
+    x_ref,
+    cot_in,
+    seg_in,
+    cos_ref,
+    sin_ref,
+    wq_in,
+    wo_in,
+    wi_in,
+    wd_in,
+    out_ref,
+    ig_ref,
+    gq_ref,
+    go_ref,
+    gi_ref,
+    gd_ref,
+    seg_buf,
+    n1,
+    n2,
+    cot,
+    db,
+    wq,
+    wo,
+    wi,
+    wd,
+    unit1,
+    inv1,
+    unit2,
+    inv2,
+    middle,
+    dmid,
+    q_buf,
+    k_buf,
+    v_buf,
+    probs,
+    att,
+    datt,
+    up_a,
+    up_b,
+    hidden,
+    d_up,
+    dqkv,
+    ps,
+    ps_in,
+    ps_far,
+    ps_back,
+    gq,
+    go,
+    gi,
+    gd,
+    rq1,
+    rq2,
+    rq3,
+    ro1,
+    ro2,
+    ro3,
+    ri1,
+    ri2,
+    ri3,
+    rd1,
+    rd2,
+    rd3,
+    send_sems,
+    recv_sems,
+):
+    dp, c = lax.axis_index("dp"), lax.axis_index("seq")
+    x, y, z = lax.rem(dp, 2), lax.rem(dp // 2, 2), dp // 4
+    zh, zp = z // 2, lax.rem(z, 2)
+    role = zp * 2 + c
+
+    def device(X, Y, Z, C):
+        return (Z * 4 + Y * 2 + X, C)
+
+    core_dev = device(x, y, z, 1 - c)
+    pair_dev = device(x, y, zh * 2 + 1 - zp, c)
+    diag_dev = device(x, y, zh * 2 + 1 - zp, 1 - c)
+    half_dev = device(x, y, (1 - zh) * 2 + zp, c)
+    x_dev = device(1 - x, y, z, c)
+    y_dev = device(x, 1 - y, z, c)
+
+    barrier = pltpu.get_barrier_semaphore()
+    for dev in (core_dev, pair_dev, diag_dev, half_dev, x_dev, y_dev):
+        pl.semaphore_signal(barrier, inc=1, device_id=dev, device_id_type=MESH_IDS)
+    pl.semaphore_wait(barrier, 6)
+
+    sent = []
+
+    def copy_to(src, dst, dev, keep=True):
+        i = n_sems[0]
+        n_sems[0] += 1
+        cp = pltpu.make_async_remote_copy(
+            src_ref=src,
+            dst_ref=dst,
+            send_sem=send_sems.at[i],
+            recv_sem=recv_sems.at[i],
+            device_id=dev,
+            device_id_type=MESH_IDS,
+        )
+        if keep:
+            sent.append(cp)
+        return cp
+
+    def go_copy(src, dst, dev):
+        cp = copy_to(src, dst, dev)
+        cp.start()
+        return cp
+
+
+    others = (
+        (core_dev, zp * 2 + 1 - c),
+        (pair_dev, (1 - zp) * 2 + c),
+        (diag_dev, (1 - zp) * 2 + 1 - c),
+    )
+
+    def spread(own, buf):
+        cps = [go_copy(own.at[r], buf.at[z, y, x, c], dev) for dev, r in others]
+        buf[z, y, x, c] = own[role]
+        return cps
+
+    class Gather:
+        def __init__(self, buf, kind, cols):
+            self.buf, self.kind = buf, kind
+            self.halves = (pl.ds(0, cols // 2), pl.ds(cols // 2, cols // 2))
+
+        def own(self, which, cut):
+            b = self.buf
+            if self.kind == "rows":
+                return b.at[pl.ds(2 * which, 2), y, x, :, :, cut]
+            if self.kind == "down":
+                return b.at[which, y, x, :, cut]
+            return b.at[y, x, :, :, cut]
+
+        def line(self, which, cut, first):
+            b = self.buf
+            if self.kind == "rows":
+                at = pl.ds(2 * which, 2)
+                return b.at[at, y, :, :, :, cut] if first == 0 else b.at[at, :, x, :, :, cut]
+            if self.kind == "down":
+                return b.at[which, y, :, :, cut] if first == 0 else b.at[which, :, x, :, cut]
+            return b.at[y, :, :, :, cut] if first == 0 else b.at[:, x, :, :, cut]
+
+        def same(self, ref, dev):
+            return go_copy(ref, ref, dev)
+
+        def first(self):
+            self.across = [self.same(self.own(zh, cut), half_dev) for cut in self.halves]
+            self.a = [
+                self.same(self.own(zh, cut), dev) for cut, dev in zip(self.halves, (x_dev, y_dev))
+            ]
+
+        def second(self):
+            self.b = []
+            for i, dev in enumerate((y_dev, x_dev)):
+                self.a[i].wait_recv()
+                self.b.append(self.same(self.line(zh, self.halves[i], i), dev))
+
+        def third(self):
+            self.a2 = []
+            for i, dev in enumerate((x_dev, y_dev)):
+                self.across[i].wait_recv()
+                self.a2.append(self.same(self.own(1 - zh, self.halves[i]), dev))
+
+        def fourth(self):
+            self.b2 = []
+            for i, dev in enumerate((y_dev, x_dev)):
+                self.a2[i].wait_recv()
+                self.b2.append(self.same(self.line(1 - zh, self.halves[i], i), dev))
+
+        def done(self):
+            for cp in self.b + self.b2:
+                cp.wait_recv()
+
+    class GatherOut(Gather):
+        def first(self):
+            self.s0 = copy_to(wo_in, self.buf.at[y, x, c], core_dev, keep=False)
+
+            @pl.when(c != zh)
+            def _():
+                self.s0.start()
+                self.s0.wait_send()
+
+            self.s1 = copy_to(self.buf.at[y, x], self.buf.at[y, x], half_dev, keep=False)
+
+            @pl.when(c == zh)
+            def _():
+                self.buf[y, x, c] = wo_in[...]
+                self.s0.wait_recv()
+                self.s1.start()
+                self.s1.wait_send()
+
+        def third(self):
+            @pl.when(c != zh)
+            def _():
+                self.s1.wait_recv()
+
+            self.a = [
+                self.same(self.own(0, cut), dev) for cut, dev in zip(self.halves, (x_dev, y_dev))
+            ]
+
+        def fourth(self):
+            self.b = []
+            for i, dev in enumerate((y_dev, x_dev)):
+                self.a[i].wait_recv()
+                self.b.append(self.same(self.line(0, self.halves[i], i), dev))
+
+        def done(self):
+            for cp in self.b:
+                cp.wait_recv()
+
+
+    class Share:
+        def __init__(self, buf):
+            self.buf = buf
+            self.to_core = go_copy(buf.at[zp, c], buf.at[zp, c], core_dev)
+            self.to_pair = go_copy(buf.at[zp, c], buf.at[zp, c], pair_dev)
+
+        def forward(self):
+            self.to_pair.wait_recv()
+            self.fwd = go_copy(self.buf.at[1 - zp, c], self.buf.at[1 - zp, c], core_dev)
+
+        def done(self):
+            self.to_core.wait_recv()
+            self.fwd.wait_recv()
+
+    class Reduce:
+        def __init__(self, i):
+            self.i = i
+            self.mine = go_copy(ps.at[i, :, 1 - c], ps_in.at[i], core_dev)
+
+        def cross(self):
+            i = self.i
+            self.mine.wait_recv()
+            ps_far[i] = (ps[i, 1 - zp, c].astype(F32) + ps_in[i, 1 - zp].astype(F32)).astype(BF)
+            self.far = go_copy(ps_far.at[i], ps_back.at[i], pair_dev)
+
+        def total(self):
+            i = self.i
+            near = ps[i, zp, c].astype(F32) + ps_in[i, zp].astype(F32)
+            self.far.wait_recv()
+            return near + ps_back[i].astype(F32)
+
+
+    def add_into(pairs):
+        for target, extra in pairs:
+            t, e = target, extra
+            t[...] = (t[...].astype(F32) + e[...].astype(F32)).astype(BF)
+
+    class Scatter:
+        def __init__(self, buf, kind, cols, r1, r2, r3):
+            self.buf, self.kind, self.r1, self.r2, self.r3 = buf, kind, r1, r2, r3
+            self.halves = (pl.ds(0, cols // 2), pl.ds(cols // 2, cols // 2))
+
+        def row(self, i, at, cut):
+            b = self.buf
+            if self.kind == "rows":
+                return b.at[:, at, :, :, :, cut] if i == 0 else b.at[:, :, at, :, :, cut]
+            if self.kind == "down":
+                return b.at[:, at, :, :, cut] if i == 0 else b.at[:, :, at, :, cut]
+            return b.at[at, :, :, :, cut] if i == 0 else b.at[:, at, :, :, cut]
+
+        def spot(self, Y, X, cut):
+            b = self.buf
+            if self.kind == "rows":
+                return b.at[:, Y, X, :, :, cut]
+            if self.kind == "down":
+                return b.at[:, Y, X, :, cut]
+            return b.at[Y, X, :, :, cut]
+
+        def first(self):
+            self.c1 = []
+            for i, (at, dev) in enumerate(((1 - y, y_dev), (1 - x, x_dev))):
+                self.c1.append(go_copy(self.row(i, at, self.halves[i]), self.r1.at[i], dev))
+
+        def second(self):
+            self.c2 = []
+            for i, dev in enumerate((x_dev, y_dev)):
+                self.c1[i].wait_recv()
+                at = y if i == 0 else x
+                mine = self.row(i, at, self.halves[i])
+                got = self.r1.at[i]
+
+                def body(j, carry, mine=mine, got=got):
+                    add_into([(mine.at[j], got.at[j])])
+                    return carry
+
+                lax.fori_loop(0, got.shape[0], body, 0)
+                there = (y, 1 - x) if i == 0 else (1 - y, x)
+                self.c2.append(
+                    go_copy(self.spot(*there, self.halves[i]), self.r2.at[i], dev)
+                )
+
+        def third(self):
+            for i in range(2):
+                self.c2[i].wait_recv()
+                mine = self.spot(y, x, self.halves[i])
+                got = self.r2.at[i]
+
+                def body(j, carry, mine=mine, got=got):
+                    add_into([(mine.at[j], got.at[j])])
+                    return carry
+
+                lax.fori_loop(0, got.shape[0], body, 0)
+            self.over()
+
+        def over(self):
+            b = self.buf
+            src = (
+                b.at[pl.ds(2 * (1 - zh), 2), y, x]
+                if self.kind == "rows"
+                else b.at[1 - zh, y, x]
+            )
+            self.c3 = go_copy(src, self.r3, half_dev)
+
+    class ScatterRows(Scatter):
+        def fourth(self, out):
+            self.c3.wait_recv()
+            self.out = out
+            for i in range(2):
+                add_into([(self.buf.at[2 * zh + i, y, x], self.r3.at[i])])
+            self.c4 = []
+            for dev, r in others:
+                src = self.buf.at[2 * zh + r // 2, y, x, lax.rem(r, 2)]
+                self.c4.append(go_copy(src, out.at[role], dev))
+            out[role] = self.buf[z, y, x, c]
+
+        def done(self):
+            for cp in self.c4:
+                cp.wait_recv()
+
+    class ScatterDown(Scatter):
+        def fourth(self, out):
+            self.c3.wait_recv()
+            out[...] = self.buf[zh, y, x].astype(F32) + self.r3[...].astype(F32)
+
+    class ScatterOut(Scatter):
+        def over(self):
+            self.c3 = copy_to(self.buf.at[y, x], self.r3, half_dev, keep=False)
+
+            @pl.when(c != zh)
+            def _():
+                self.c3.start()
+                self.c3.wait_send()
+
+        def fourth(self, out):
+            self.c4 = copy_to(self.r3.at[1 - c], out, core_dev, keep=False)
+
+            @pl.when(c == zh)
+            def _():
+                self.c3.wait_recv()
+                for i in range(2):
+                    add_into([(self.r3.at[i], self.buf.at[y, x, i])])
+                self.c4.start()
+                out[...] = self.r3[c]
+                self.c4.wait_send()
+
+            @pl.when(c != zh)
+            def _():
+                self.c4.wait_recv()
+
+    s_q = spread(wq_in, wq)
+    seg_buf[zp, c] = seg_in[...]
+    s_seg = [go_copy(seg_buf.at[zp, c], seg_buf.at[zp, c], dev) for dev, _ in others]
+
+    tokens = x_ref[...].astype(F32)
+    centred = tokens - jnp.mean(tokens, axis=-1, keepdims=True)
+    inv = lax.rsqrt(jnp.mean(centred * centred, axis=-1, keepdims=True) + EPSILON)
+    unit = centred * inv
+    unit1[...] = unit
+    inv1[...] = jnp.broadcast_to(inv, (TOK, 128))
+    n1[zp, c] = unit.astype(BF)
+    share_n1 = Share(n1)
+
+    g_q = Gather(wq, "rows", QKV)
+    g_i = Gather(wi, "rows", 2 * HID)
+    g_d = Gather(wd, "down", WIDTH)
+    g_o = GatherOut(wo, "out", WIDTH)
+
+    for cp in s_q:
+        cp.wait_recv()
+    g_q.first()
+    s_i = spread(wi_in, wi)
+    g_o.first()
+    g_q.second()
+    share_n1.forward()
+    g_q.third()
+    for cp in s_i:
+        cp.wait_recv()
+    g_i.first()
+    cot[zp, c] = cot_in[...]
+    share_cot = Share(cot)
+    g_o.third()
+    g_q.fourth()
+    g_o.fourth()
+    wd[zh, y, x] = wd_in[...]
+    share_n1.done()
+    for cp in s_seg:
+        cp.wait_recv()
+    g_q.done()
+
+    lanes = lax.broadcasted_iota(jnp.int32, (1, 128), 1)
+    low_half = lax.rem(lanes, 64) < 32
+    first_head = lanes < 64
+
+    def qkv_step(s, carry):
+        rows = n1[s].reshape(256, WIDTH)
+        for part, dst in enumerate((q_buf, k_buf, v_buf)):
+            for j in range(2):
+                at = part * 256 + j * 128
+                w = wq[:, :, :, :, :, pl.ds(at, 128)].reshape(WIDTH, 128)
+                u = dot_nn(rows, w)
+                if part < 2:
+                    u = u * cos_ref[...] + turned(u, low_half) * sin_ref[...]
+                dst[s, j] = u.astype(BF)
+        return carry
+
+    lax.fori_loop(0, 2, qkv_step, 0)
+    g_i.second()
+    share_cot.forward()
+
+    def only(head, u):
+        return jnp.where(first_head if head == 0 else ~first_head, u, jnp.zeros_like(u))
+
+    def attend(i, carry):
+        s, j = i // 2, lax.rem(i, 2)
+        q, k, v = q_buf[s, j], k_buf[s, j], v_buf[s, j]
+        seg_row = jnp.concatenate([seg_buf[s, 0, 0:1], seg_buf[s, 1, 0:1]], axis=1)
+        seg_col = jnp.broadcast_to(seg_row, (128, 256)).T[:, 0:1]
+        same = seg_col == seg_row
+        heads = []
+        for h in range(2):
+            scores = matmul_nt(only(h, q), k) * 0.125
+            scores = jnp.where(same, scores, -1e30)
+            weights = jnp.exp(scores - jnp.max(scores, axis=-1, keepdims=True))
+            p = weights * (1.0 / jnp.sum(weights, axis=-1, keepdims=True))
+            probs[i, h] = p
+            heads.append(dot_nn(p.astype(BF), v))
+        att[s, j] = jnp.where(first_head, heads[0], heads[1]).astype(BF)
+        return carry
+
+    lax.fori_loop(0, 4, attend, 0)
+    g_o.done()
+
+    def att_rows(s):
+        return jnp.concatenate([att[s, 0], att[s, 1]], axis=1)
+
+    def branch(s, carry):
+        w = wo[...].reshape(256, WIDTH)
+        ps[0, s] = dot_nn(att_rows(s), w).astype(BF).reshape(2, TOK, WIDTH)
+        return carry
+
+    lax.fori_loop(0, 2, branch, 0)
+    red = Reduce(0)
+    red.cross()
+    g_i.third()
+    g_d.first()
+    share_cot.done()
+    mid = x_ref[...].astype(F32) + red.total()
+    middle[...] = mid
+    centred = mid - jnp.mean(mid, axis=-1, keepdims=True)
+    inv = lax.rsqrt(jnp.mean(centred * centred, axis=-1, keepdims=True) + EPSILON)
+    unit = centred * inv
+    unit2[...] = unit
+    inv2[...] = jnp.broadcast_to(inv, (TOK, 128))
+    n2[zp, c] = unit.astype(BF)
+    share_n2 = Share(n2)
+    g_i.fourth()
+    g_d.second()
+    share_n2.forward()
+    g_d.third()
+    share_n2.done()
+    g_i.done()
+    g_d.fourth()
+
+    def upper(j, carry):
+        at = pl.multiple_of(j * 256, 256)
+        for s in range(2):
+            rows = n2[s].reshape(256, WIDTH)
+            inner = dot_nn(rows, wi[:, :, :, :, :, pl.ds(at, 256)].reshape(WIDTH, 256))
+            gate = dot_nn(
+                rows,
+                wi[:, :, :, :, :, pl.ds(pl.multiple_of(HID + at, 256), 256)].reshape(WIDTH, 256),
+            )
+            cdf = 0.5 * (1.0 + lax.erf(inner * math.sqrt(0.5)))
+            slope = cdf + inner * jnp.exp(-0.5 * inner * inner) * (1.0 / math.sqrt(2 * math.pi))
+            bent = inner * cdf
+            up_a[s, :, pl.ds(at, 256)] = gate * slope
+            up_b[s, :, pl.ds(at, 256)] = bent
+            hidden[s, :, pl.ds(at, 256)] = (bent * gate).astype(BF)
+        return carry
+
+    lax.fori_loop(0, HID // 256, upper, 0)
+
+    def down_grad(i, carry):
+        lhs = hidden[:, :, pl.ds(pl.multiple_of(i * 384, 384), 384)].reshape(512, 384)
+        for j in range(2):
+            rhs = cot[:, :, :, pl.ds(j * 512, 512)].reshape(512, 512)
+            gd[i, :, :, :, pl.ds(j * 512, 512)] = (
+                matmul_tn(lhs, rhs).astype(BF).reshape(2, 2, PAD, 512)
+            )
+        return carry
+
+    lax.fori_loop(0, 2, down_grad, 0)
+    r_d = ScatterDown(gd, "down", WIDTH, rd1, rd2, rd3)
+    r_d.first()
+    g_d.done()
+
+    def hidden_grad(i, carry):
+        w = wd[i].reshape(384, WIDTH)
+        at = pl.multiple_of(i * 384, 384)
+        for s in range(2):
+            dh = matmul_nt(cot[s].reshape(256, WIDTH), w)
+            d_up[s, :, pl.ds(at, 384)] = (dh * up_a[s, :, pl.ds(at, 384)]).astype(BF)
+            d_up[s, :, pl.ds(pl.multiple_of(HID + at, 384), 384)] = (
+                dh * up_b[s, :, pl.ds(at, 384)]
+            ).astype(BF)
+        return carry
+
+    lax.fori_loop(0, 2, hidden_grad, 0)
+
+    def normed_two_grad(i, carry):
+        w = wi[i].reshape(256, 2 * HID)
+        at = pl.multiple_of(i * 256, 256)
+        for s in range(2):
+            ps[1, s, :, :, pl.ds(at, 256)] = (
+                matmul_nt(d_up[s], w).astype(BF).reshape(2, TOK, 256)
+            )
+        return carry
+
+    lax.fori_loop(0, 4, normed_two_grad, 0)
+    red = Reduce(1)
+    r_d.second()
+
+    def in_grad(i, carry):
+        lhs = n2[:, :, :, pl.ds(pl.multiple_of(i * 256, 256), 256)].reshape(512, 256)
+        for j in range(3):
+            rhs = d_up[:, :, pl.ds(j * 512, 512)].reshape(512, 512)
+            gi[i, :, :, :, :, pl.ds(j * 512, 512)] = (
+                matmul_tn(lhs, rhs).astype(BF).reshape(2, 2, 2, 32, 512)
+            )
+        return carry
+
+    lax.fori_loop(0, 4, in_grad, 0)
+    red.cross()
+    r_i = ScatterRows(gi, "rows", 2 * HID, ri1, ri2, ri3)
+    r_i.first()
+
+    e = red.total()
+    n = unit2[...]
+    d_middle = cot_in[...].astype(F32) + inv2[:, 0:1] * (
+        e
+        - jnp.mean(e, axis=-1, keepdims=True)
+        - n * jnp.mean(e * n, axis=-1, keepdims=True)
+    )
+    dmid[...] = d_middle
+    db[zp, c] = d_middle.astype(BF)
+    share_db = Share(db)
+    r_d.third()
+
+    def down(i, carry):
+        w = wd[...].reshape(HID, WIDTH)
+        ps[2, i] = dot_nn(hidden[i], w).astype(BF).reshape(2, TOK, WIDTH)
+        return carry
+
+    lax.fori_loop(0, 2, down, 0)
+    red_out = Reduce(2)
+    share_db.forward()
+    red_out.cross()
+    r_i.second()
+    r_d.fourth(gd_ref)
+    share_db.done()
+
+    def attended_grad(s, carry):
+        rows = db[s].reshape(256, WIDTH)
+        da = matmul_nt(rows, wo[...].reshape(256, WIDTH)).astype(BF)
+        datt[s, 0] = da[:, 0:128]
+        datt[s, 1] = da[:, 128:256]
+        return carry
+
+    lax.fori_loop(0, 2, attended_grad, 0)
+
+    def attend_back(i, carry):
+        s, j = i // 2, lax.rem(i, 2)
+        q, k, v, da = q_buf[s, j], k_buf[s, j], v_buf[s, j], datt[s, j]
+        dq, dk, dv = [], [], []
+        for h in range(2):
+            p = probs[i, h]
+            dprob = matmul_nt(only(h, da), v)
+            delta = jnp.sum(p * dprob, axis=-1, keepdims=True)
+            ds = (p * (dprob - delta)).astype(BF)
+            dq.append(dot_nn(ds, k))
+            dk.append(matmul_tn(ds, q))
+            dv.append(matmul_tn(p.astype(BF), da))
+        for part, pieces in enumerate((dq, dk, dv)):
+            u = jnp.where(first_head, pieces[0], pieces[1])
+            if part < 2:
+                u = u * 0.125
+                u = u * cos_ref[...] - turned(u, low_half) * sin_ref[...]
+            dqkv[part, j, s] = u.astype(BF)
+        return carry
+
+    lax.fori_loop(0, 4, attend_back, 0)
+    r_i.third()
+
+    def first_grads(i, carry):
+        w = wq[i].reshape(256, QKV)
+        at = pl.multiple_of(i * 256, 256)
+        for s in range(2):
+            rows = jnp.concatenate([dqkv[p, j, s] for p in range(3) for j in range(2)], axis=1)
+            ps[3, s, :, :, pl.ds(at, 256)] = (
+                matmul_nt(rows, w).astype(BF).reshape(2, TOK, 256)
+            )
+        return carry
+
+    lax.fori_loop(0, 4, first_grads, 0)
+    red_in = Reduce(3)
+
+    def qkv_grad(i, carry):
+        lhs = n1[:, :, :, pl.ds(pl.multiple_of(i * 256, 256), 256)].reshape(512, 256)
+        for p in range(3):
+            for j in range(2):
+                rhs = dqkv[p, j].reshape(512, 128)
+                gq[i, :, :, :, :, pl.ds(p * 256 + j * 128, 128)] = (
+                    matmul_tn(lhs, rhs).astype(BF).reshape(2, 2, 2, 32, 128)
+                )
+        return carry
+
+    lax.fori_loop(0, 4, qkv_grad, 0)
+    r_q = ScatterRows(gq, "rows", QKV, rq1, rq2, rq3)
+    r_q.first()
+
+    lhs = att
+    for j in range(2):
+        for half in range(2):
+            rhs = db[:, :, :, pl.ds(half * 512, 512)].reshape(512, 512)
+            go[j, :, :, :, pl.ds(half * 512, 512)] = (
+                matmul_tn(lhs[:, j].reshape(512, 128), rhs).astype(BF).reshape(2, 2, 32, 512)
+            )
+    r_o = ScatterOut(go, "out", WIDTH, ro1, ro2, ro3)
+    r_o.first()
+    red_in.cross()
+    r_i.fourth(gi_ref)
+    out_ref[...] = (middle[...] + red_out.total()).astype(BF)
+    r_q.second()
+    r_o.second()
+    e = red_in.total()
+    n = unit1[...]
+    ig_ref[...] = dmid[...] + inv1[:, 0:1] * (
+        e
+        - jnp.mean(e, axis=-1, keepdims=True)
+        - n * jnp.mean(e * n, axis=-1, keepdims=True)
+    )
+    r_q.third()
+    r_o.third()
+    r_q.fourth(gq_ref)
+    r_o.fourth(go_ref)
+    r_i.done()
+    r_q.done()
+    for cp in sent:
+        cp.wait_send()
+
+
+def block_device(inputs, segments, cotangent, ln1_gain, w_qkv, w_attn_out, ln2_gain, w_in, w_mlp_out):
+    gain_one = ln1_gain.astype(F32)[:, None]
+    gain_two = ln2_gain.astype(F32)[:, None]
+    qkv_own = w_qkv.reshape(32, 3 * WIDTH).astype(F32)
+    in_own = w_in.reshape(32, 2 * FF).astype(F32)
+    wq_in = (
+        (qkv_own * gain_one)
+        .astype(BF)
+        .reshape(32, 3, 2, 2, 256)
+        .transpose(3, 2, 0, 1, 4)
+        .reshape(4, 32, QKV)
+    )
+    wi_in = (in_own * gain_two).astype(BF).reshape(32, 2, 2, 2, 2, 2, 2, PART)
+    wi_in = jnp.pad(wi_in, ((0, 0),) * 7 + ((0, PAD - PART),))
+    wi_in = wi_in.transpose(3, 6, 0, 1, 2, 4, 5, 7).reshape(4, 32, 2 * HID)
+    wd_in = jnp.pad(w_mlp_out.reshape(PART, WIDTH), ((0, PAD - PART), (0, 0)))
+    wo_in = w_attn_out.reshape(32, WIDTH)
+    seg = jnp.broadcast_to(segments.astype(F32), (8, TOK))
+    cosines, sines = rope_tables(jnp.arange(2 * TOK, dtype=jnp.int32).astype(F32))
+    signs = jnp.where(jnp.arange(HD) < HD // 2, -1.0, 1.0).astype(F32)
+    cosines = jnp.tile(cosines, (1, 2))
+    sines = jnp.tile(sines * signs, (1, 2))
+
+    vm = pltpu.VMEM
+    group = (2, 2, TOK, WIDTH)
+    rows = (4, 2, 2, 2, 32)
+    outs = pl.pallas_call(
+        functools.partial(layer_kernel, [0]),
+        out_shape=(
+            jax.ShapeDtypeStruct((TOK, WIDTH), BF),
+            jax.ShapeDtypeStruct((TOK, WIDTH), F32),
+            jax.ShapeDtypeStruct((4, 32, QKV), BF),
+            jax.ShapeDtypeStruct((32, WIDTH), BF),
+            jax.ShapeDtypeStruct((4, 32, 2 * HID), BF),
+            jax.ShapeDtypeStruct((PAD, WIDTH), F32),
+        ),
+        in_specs=[pl.BlockSpec(memory_space=vm)] * 9,
+        out_specs=(pl.BlockSpec(memory_space=vm),) * 6,
+        scratch_shapes=[
+            vm((2, 2, 8, TOK), F32),
+            vm(group, BF),
+            vm(group, BF),
+            vm(group, BF),
+            vm(group, BF),
+            vm(rows + (QKV,), BF),
+            vm((2, 2, 2, 32, WIDTH), BF),
+            vm(rows + (2 * HID,), BF),
+            vm((2, 2, 2, PAD, WIDTH), BF),
+            vm((TOK, WIDTH), F32),
+            vm((TOK, 128), F32),
+            vm((TOK, WIDTH), F32),
+            vm((TOK, 128), F32),
+            vm((TOK, WIDTH), F32),
+            vm((TOK, WIDTH), F32),
+            vm((2, 2, 256, 128), BF),
+            vm((2, 2, 256, 128), BF),
+            vm((2, 2, 256, 128), BF),
+            vm((4, 2, 256, 256), F32),
+            vm((2, 2, 256, 128), BF),
+            vm((2, 2, 256, 128), BF),
+            vm((2, 256, HID), F32),
+            vm((2, 256, HID), F32),
+            vm((2, 256, HID), BF),
+            vm((2, 256, 2 * HID), BF),
+            vm((3, 2, 2, 256, 128), BF),
+            vm((4,) + group, BF),
+            vm((4, 2, TOK, WIDTH), BF),
+            vm((4, TOK, WIDTH), BF),
+            vm((4, TOK, WIDTH), BF),
+            vm(rows + (QKV,), BF),
+            vm((2, 2, 2, 32, WIDTH), BF),
+            vm(rows + (2 * HID,), BF),
+            vm((2, 2, 2, PAD, WIDTH), BF),
+            vm((2, 4, 2, 2, 32, QKV // 2), BF),
+            vm((2, 4, 2, 32, QKV // 2), BF),
+            vm((2, 2, 32, QKV), BF),
+            vm((2, 2, 2, 32, WIDTH // 2), BF),
+            vm((2, 2, 32, WIDTH // 2), BF),
+            vm((2, 32, WIDTH), BF),
+            vm((2, 4, 2, 2, 32, HID), BF),
+            vm((2, 4, 2, 32, HID), BF),
+            vm((2, 2, 32, 2 * HID), BF),
+            vm((2, 2, 2, PAD, WIDTH // 2), BF),
+            vm((2, 2, PAD, WIDTH // 2), BF),
+            vm((PAD, WIDTH), BF),
+            pltpu.SemaphoreType.DMA((N_COPIES,)),
+            pltpu.SemaphoreType.DMA((N_COPIES,)),
+        ],
+        compiler_params=pltpu.CompilerParams(
+            collective_id=0, has_side_effects=True, vmem_limit_bytes=60 * 2**20
+        ),
+    )(inputs[0], cotangent[0], seg, cosines, sines, wq_in, wo_in, wi_in, wd_in)
+    output, input_grad, gq, go, gi, gd = outs
+
+    raw_q = gq.astype(F32).reshape(2, 2, 32, 3, 256).transpose(2, 3, 1, 0, 4).reshape(32, 3 * WIDTH)
+    raw_i = gi.astype(F32).reshape(2, 2, 32, 2, 2, 2, 2, PAD)[..., :PART]
+    raw_i = raw_i.transpose(2, 3, 4, 0, 5, 6, 1, 7).reshape(32, 2 * FF)
+    return (
+        output[None],
+        input_grad[None],
+        jnp.sum(raw_q * qkv_own, axis=1),
+        (raw_q * gain_one).reshape(-1),
+        go.astype(F32).reshape(-1),
+        jnp.sum(raw_i * in_own, axis=1),
+        (raw_i * gain_two).reshape(-1),
+        gd[:PART].reshape(-1),
+    )
+
+
+N_COPIES = 160
+
+
 def solution(mesh):
+    block = dict(mesh.shape) == {"dp": 16, "seq": 2}
     placed = (
         P("dp", "seq", None),
         P("dp", "seq"),
@@ -333,7 +1130,7 @@
         P(("dp", "seq")),
     )
     return jax.shard_map(
-        per_device,
+        block_device if block else general_device,
         mesh=mesh,
         in_specs=placed,
         out_specs=(

time: 1170 us -> 183 us (0.16)
  waiting for transfers between devices: 773 us -> 0 us
  Pallas kernels: 0 us -> 158 us
  local copies, waits for them, and re-layouts: 164 us -> 17.7 us
  blocking collectives: 126 us -> 0 us
  matrix products: 60.4 us -> 0 us
  other arithmetic: 20.7 us -> 6.05 us
  between operations: 15 us -> 0.88 us
    unnamed x14 -> x0, waiting for transfers between devices: 572 us -> none
    all_gather x4 -> x0, waiting for transfers between devices: 200 us -> none  [the longest x1 63.3 us: per_device(): lax.all_gather(w_mlp_out, ('dp', 'seq'), axis=0, tiled=True)]
    pallas_call x0 -> x1, Pallas kernels: none -> 158 us  [block_device(): pl.pallas_call(functools.partial(layer_kernel, [0]), out_shape=(jax.Shape...]
    unnamed x2 -> x0, blocking collectives: 120 us -> none
    convert_element_type x13 -> x2, local copies, waits for them, and re-layouts: 72.4 us -> 3.22 us  [the longest x1 2.05 us: block_device(): in_own = w_in.reshape(32, 2 * FF).astype(F32)]
    dot_general x18 -> x0, matrix products: 60.4 us -> none  [the longest x4 20.9 us: matmul_nt(): lax.dot_general(left, right, (((1,), (1,)), ((), ())), preferred_element_...]
    reshape x4 -> x7, local copies, waits for them, and re-layouts: 43.7 us -> 5.94 us  [the longest x1 1.75 us: block_device(): raw_i = raw_i.transpose(2, 3, 4, 0, 5, 6, 1, 7).reshape(32, 2 * FF)]
    reduce_scatter x6 -> x0, local copies, waits for them, and re-layouts: 32.7 us -> none  [the longest x1 10.8 us: per_device(): lax.psum_scatter(mlp_parts[1].astype(jnp.bfloat16), 'seq', scatter_dimens...]
  transfers between devices with their start and end apart: 12 -> 0, of which waited for: 5 -> 0; matrix products, arithmetic and copies ran while one was open for 15% -> 0% of each run, Pallas kernels for 0% -> 0%
where the time goes in v1:
time: 183 us; the launch traced here: 182 us
  Pallas kernels  158 us (86%)
  local copies, waits for them, and re-layouts  17.7 us (10%)
  other arithmetic  6.05 us (3%)
    pallas_call x1, Pallas kernels, block_device(): pl.pallas_call(functools.partial(layer_kernel, [0]), out_shape=(jax.Shape...  158 us

profile of v1, /device:TPU:0, one launch (start us, length us, event | category | flops | bytes accessed | tf_op | source)
XLA Modules:
  0.0 182.3 jit_solution(8867036316974069318)
XLA Ops:
  0.6 0.0 copy-start.9
  0.6 1.2 reshape.180
  1.8 0.0 copy-done.9
  1.8 0.2 fusion.1
  2.0 0.1 copy.17
  2.2 0.0 copy-start.2
  2.2 0.9 reshape.169.wq_in
  3.1 0.1 copy-done.2
  3.1 0.0 copy-start.8
  3.1 2.0 %reshape.181 = f32[32,2,2,2,2,2,2,82]{7,6,5,4,3,2,1,0:T(2,128)S(1)} reshape(bf16[167936]{0:T(1024)(128)(2,1)S(1)} %copy-done.2) | data formatting | bytes 1007616 | tf_op jit(solution)/shard_map/convert_element_type | solution.py:1011
  5.2 0.0 copy-done.8
  5.2 0.6 multiply_convert_fusion
  5.8 0.6 pad_bitcast_fusion
  6.4 0.3 copy.18
  6.7 1.3 reshape.171.wi_in
  8.0 0.1 broadcast_multiply_fusion
  8.1 0.1 fusion.4
  8.2 0.8 copy.19.cos_ref
  9.0 0.0 copy-start.5
  9.0 0.8 copy.20.sin_ref
  9.8 0.2 copy-done.5
  9.9 0.1 reshape.172
  10.0 0.0 copy-start.7
  10.0 0.7 pad.9.wd_in
  10.7 0.1 copy-done.7
  10.9 0.0 copy-start.10
  10.9 0.7 reshape.170.wo_in
  11.5 0.0 copy-done.10
  11.5 0.6 broadcast_in_dim.27.seg_in
  12.1 157.7 %shard_map.152 = (bf16[128,1024]{1,0:T(8,128)(2,1)}, f32[128,1024]{1,0:T(8,128)}, bf16[4,32,768]{2,1,0:T(8,128)(2,1)}, bf16[32,1024]{1,0:T(8,128)(2,1)}, bf16[4,...) custom-call(bf16[128,1024]{1,0:T(8,128)(2,1)} %bitcast.37, bf16[128,1024]{1,0:T(8,128)(2,1)} %bitcast.38, ...), custom_call_target="tpu_custom_call" | custom-call | tf_op jit(solution)/shard_map/pallas_call | solution.py:1033
  169.9 1.1 reshape.184
  171.0 1.0 fusion
  172.0 0.2 copy.24
  172.2 0.1 broadcast_bitcast_fusion
  172.3 0.1 copy.25
  172.4 0.0 copy-start.1
  172.4 0.8 mul.99
  173.2 0.3 copy-done.1
  173.5 0.5 reshape.177
  174.0 1.5 multiply_reduce_fusion
  175.5 0.8 convert_bitcast_fusion
  176.3 1.8 reshape.178
  178.0 0.1 mul.101
  178.2 0.0 copy-start.3
  178.2 0.9 mul.103
  179.1 0.1 copy-done.3
  179.3 0.0 copy-start.6
  179.3 0.0 copy-start.4
  179.3 0.8 reshape.179
  180.1 0.0 copy-start
  180.1 0.0 copy-done.6
  180.2 0.7 copy.26
  180.8 0.0 copy-done.4
  180.8 0.7 copy.33
  181.5 0.0 copy-done
  181.5 0.8 copy.34
  (11 shorter events, 0.1 us)
Async XLA Ops:
  0.6 1.2 copy-start.9
  2.2 1.0 copy-start.2
  3.1 2.1 %copy-start.8 = (bf16[32]{0:T(256)(128)(2,1)S(1)}, bf16[32]{0:T(256)(128)(2,1)}, u32[]{:S(2)}) copy-start(bf16[32]{0:T(256)(128)(2,1)} %param.15) | copy-start | bytes 196
  9.0 0.9 copy-start.5
  10.0 0.8 copy-start.7
  10.9 0.7 copy-start.10
  172.4 1.1 copy-start.1
  178.2 1.0 copy-start.3
  179.3 0.8 copy-start.6
  179.3 1.5 copy-start.4
  180.1 1.4 copy-start

commit v2 on v1

--- a/solution.py
+++ b/solution.py
@@ -3,6 +3,7 @@
 
 import jax
 import jax.numpy as jnp
+import numpy as np
 from jax import lax
 from jax.experimental import pallas as pl
 from jax.experimental.pallas import tpu as pltpu
@@ -342,6 +343,163 @@
     return jnp.where(low_half, pltpu.roll(u, 96, axis=1), pltpu.roll(u, 32, axis=1))
 
 
+def column(gain_ref):
+    square = jnp.broadcast_to(gain_ref[...].astype(F32), (32, 32))
+    rows = lax.broadcasted_iota(jnp.int32, (32, 32), 0)
+    cols = lax.broadcasted_iota(jnp.int32, (32, 32), 1)
+    return jnp.sum(jnp.where(rows == cols, square, 0.0), axis=1, keepdims=True)
+
+
+def owner(r, k):
+    return k // 4 * 16 + r // 2 * 8 + k // 2 % 2 * 4 + k % 2 * 2 + r % 2
+
+
+def runs(places):
+    found = []
+    for lane, place in enumerate(places):
+        if place is None:
+            continue
+        tile, shift = place[0], (place[1] - lane) % 128
+        if found and found[-1][:2] == (tile, shift) and found[-1][3] == lane:
+            found[-1] = found[-1][:3] + (lane + 1,)
+        else:
+            found.append((tile, shift, lane, lane + 1))
+    return found
+
+
+def in_moves(r, u):
+    places = []
+    for at in range(u * 128, u * 128 + 128):
+        gate, rest = divmod(at, HID)
+        k, i = divmod(rest, PAD)
+        col = gate * FF + PART * owner(r, k) + i
+        places.append(divmod(col, 128) if i < PART else None)
+    return runs(places)
+
+
+def out_moves(t):
+    spots = {owner(r, k): (r, k) for r in range(4) for k in range(8)}
+    places = []
+    for col in range(t * 128, t * 128 + 128):
+        gate, rest = divmod(col, FF)
+        device, i = divmod(rest, PART)
+        r, k = spots[device]
+        u, lane = divmod(gate * HID + k * PAD + i, 128)
+        places.append(((r, u), lane))
+    return runs(places)
+
+
+def moved(moves, load):
+    lanes = lax.broadcasted_iota(jnp.int32, (1, 128), 1)
+    out = jnp.zeros((32, 128), F32)
+    for tile, shift, low, high in moves:
+        piece = load(tile)
+        if shift:
+            piece = pltpu.roll(piece, 128 - shift, axis=1)
+        out = jnp.where((lanes >= low) & (lanes < high), piece, out)
+    return out
+
+
+def finish_kernel(
+    gq_in,
+    go_in,
+    gi_in,
+    gd_in,
+    out_in,
+    ig_in,
+    gain1_in,
+    gain2_in,
+    wq_flat,
+    wi_flat,
+    out_ref,
+    ig_ref,
+    gain1_ref,
+    gq_ref,
+    go_ref,
+    gain2_ref,
+    gi_ref,
+    gd_ref,
+    lines,
+    gq_raw,
+    go_raw,
+    gi_raw,
+    gd_raw,
+    wq_raw,
+    wi_raw,
+    gq_own,
+    go_own,
+    gi_own,
+    gd_own,
+    ig_raw,
+    out_raw,
+    sems,
+):
+    count = [0]
+
+    def start(src, dst):
+        cp = pltpu.make_async_copy(src, dst, sems.at[count[0]])
+        count[0] += 1
+        cp.start()
+        return cp
+
+    gi_here = start(gi_in, gi_raw)
+    wi_here = start(wi_flat, wi_raw)
+    gq_here = start(gq_in, gq_raw)
+    wq_here = start(wq_flat, wq_raw)
+    gd_here = start(gd_in, gd_raw)
+    go_here = start(go_in, go_raw)
+    ig_here = start(ig_in, ig_raw)
+    out_here = start(out_in, out_raw)
+    written = []
+    rows = lax.broadcasted_iota(jnp.int32, (32, 32), 0)
+    cols = lax.broadcasted_iota(jnp.int32, (32, 32), 1)
+
+    def line(total):
+        total = jnp.sum(total, axis=1, keepdims=True)
+        return jnp.sum(jnp.where(rows == cols, total, 0.0), axis=0, keepdims=True)
+
+    in_rows = 2 * FF // TOK
+    gain = column(gain2_in)
+    total = jnp.zeros((32, 128), F32)
+    wi_here.wait()
+    lines[...] = wi_raw[...].astype(F32)
+    gi_here.wait()
+    for j in range(in_rows):
+        g = moved(out_moves(j), lambda t: gi_raw[t[0], :, pl.ds(t[1] * 128, 128)].astype(F32))
+        total = total + g * lines[pl.ds(j, 32, stride=in_rows), :]
+        gi_own[pl.ds(j, 32, stride=in_rows), :] = g * gain
+    written.append(start(gi_own, gi_ref))
+    ig_here.wait()
+    written.append(start(ig_raw, ig_ref))
+    out_here.wait()
+    written.append(start(out_raw, out_ref))
+    gain2_ref[...] = line(total)
+    qkv_rows = 3 * WIDTH // TOK
+    gain = column(gain1_in)
+    total = jnp.zeros((32, 128), F32)
+    wq_here.wait()
+    lines[0 : 32 * qkv_rows] = wq_raw[...].astype(F32)
+    gq_here.wait()
+    for j in range(qkv_rows):
+        part, cut = divmod(j, 8)
+        r = (cut // 2 % 2) * 2 + cut // 4
+        g = gq_raw[r, :, pl.ds(part * 256 + cut % 2 * 128, 128)].astype(F32)
+        total = total + g * lines[pl.ds(j, 32, stride=qkv_rows), :]
+        gq_own[pl.ds(j, 32, stride=qkv_rows), :] = g * gain
+    written.append(start(gq_own, gq_ref))
+    gain1_ref[...] = line(total)
+    gd_here.wait()
+    for j in range(8):
+        gd_own[pl.ds(j, PART, stride=8), :] = gd_raw[0:PART, pl.ds(j * 128, 128)]
+    written.append(start(gd_own, gd_ref))
+    go_here.wait()
+    for j in range(8):
+        go_own[pl.ds(j, 32, stride=8), :] = go_raw[:, pl.ds(j * 128, 128)].astype(F32)
+    written.append(start(go_own, go_ref))
+    for cp in written:
+        cp.wait()
+
+
 def layer_kernel(
     n_sems,
     x_ref,
@@ -349,10 +507,12 @@
     seg_in,
     cos_ref,
     sin_ref,
-    wq_in,
-    wo_in,
-    wi_in,
-    wd_in,
+    gain1_in,
+    gain2_in,
+    wq_flat,
+    wo_flat,
+    wi_flat,
+    wd_flat,
     out_ref,
     ig_ref,
     gq_ref,
@@ -405,8 +565,20 @@
     rd1,
     rd2,
     rd3,
+    wq_in,
+    wo_in,
+    wi_in,
+    lines,
+    wide,
+    out_vm,
+    ig_vm,
+    gq_vm,
+    go_vm,
+    gi_vm,
+    gd_vm,
     send_sems,
     recv_sems,
+    local_sems,
 ):
     dp, c = lax.axis_index("dp"), lax.axis_index("seq")
     x, y, z = lax.rem(dp, 2), lax.rem(dp // 2, 2), dp // 4
@@ -426,7 +598,6 @@
     barrier = pltpu.get_barrier_semaphore()
     for dev in (core_dev, pair_dev, diag_dev, half_dev, x_dev, y_dev):
         pl.semaphore_signal(barrier, inc=1, device_id=dev, device_id_type=MESH_IDS)
-    pl.semaphore_wait(barrier, 6)
 
     sent = []
 
@@ -445,6 +616,18 @@
             sent.append(cp)
         return cp
 
+    local = []
+
+    def emit(i, src, dst):
+        cp = pltpu.make_async_copy(src, dst, local_sems.at[i])
+        cp.start()
+        local.append(cp)
+
+    def settle():
+        for cp in sent:
+            cp.wait_send()
+        del sent[:]
+
     def go_copy(src, dst, dev):
         cp = copy_to(src, dst, dev)
         cp.start()
@@ -459,53 +642,49 @@
 
     def spread(own, buf):
         cps = [go_copy(own.at[r], buf.at[z, y, x, c], dev) for dev, r in others]
-        buf[z, y, x, c] = own[role]
         return cps
 
     class Gather:
-        def __init__(self, buf, kind, cols):
-            self.buf, self.kind = buf, kind
+        def __init__(self, buf, cols):
+            self.buf = buf
             self.halves = (pl.ds(0, cols // 2), pl.ds(cols // 2, cols // 2))
-
-        def own(self, which, cut):
-            b = self.buf
-            if self.kind == "rows":
-                return b.at[pl.ds(2 * which, 2), y, x, :, :, cut]
-            if self.kind == "down":
-                return b.at[which, y, x, :, cut]
-            return b.at[y, x, :, :, cut]
-
-        def line(self, which, cut, first):
-            b = self.buf
-            if self.kind == "rows":
-                at = pl.ds(2 * which, 2)
-                return b.at[at, y, :, :, :, cut] if first == 0 else b.at[at, :, x, :, :, cut]
-            if self.kind == "down":
-                return b.at[which, y, :, :, cut] if first == 0 else b.at[which, :, x, :, cut]
-            return b.at[y, :, :, :, cut] if first == 0 else b.at[:, x, :, :, cut]
+            self.per_half = buf.shape[0] // 2
+
+        def of(self, which):
+            return pl.ds(self.per_half * which, self.per_half)
+
+        def spot(self, which, cut):
+            return self.buf.at[(self.of(which), y, x) + (slice(None),) * (len(self.buf.shape) - 4) + (cut,)]
+
+        def line(self, which, cut, i):
+            rest = (slice(None),) * (len(self.buf.shape) - 4) + (cut,)
+            at = (y, slice(None)) if i == 0 else (slice(None), x)
+            return self.buf.at[(self.of(which),) + at + rest]
 
         def same(self, ref, dev):
             return go_copy(ref, ref, dev)
 
-        def first(self):
-            self.across = [self.same(self.own(zh, cut), half_dev) for cut in self.halves]
+        def across(self):
+            self.over = [self.same(self.spot(zh, cut), half_dev) for cut in self.halves]
+
+        def own_first(self):
             self.a = [
-                self.same(self.own(zh, cut), dev) for cut, dev in zip(self.halves, (x_dev, y_dev))
+                self.same(self.spot(zh, cut), dev) for cut, dev in zip(self.halves, (x_dev, y_dev))
             ]
 
-        def second(self):
+        def own_second(self):
             self.b = []
             for i, dev in enumerate((y_dev, x_dev)):
                 self.a[i].wait_recv()
                 self.b.append(self.same(self.line(zh, self.halves[i], i), dev))
 
-        def third(self):
+        def far_first(self):
             self.a2 = []
             for i, dev in enumerate((x_dev, y_dev)):
-                self.across[i].wait_recv()
-                self.a2.append(self.same(self.own(1 - zh, self.halves[i]), dev))
-
-        def fourth(self):
+                self.over[i].wait_recv()
+                self.a2.append(self.same(self.spot(1 - zh, self.halves[i]), dev))
+
+        def far_second(self):
             self.b2 = []
             for i, dev in enumerate((y_dev, x_dev)):
                 self.a2[i].wait_recv()
@@ -515,15 +694,19 @@
             for cp in self.b + self.b2:
                 cp.wait_recv()
 
-    class GatherOut(Gather):
-        def first(self):
+    class GatherOut:
+        def __init__(self, buf, cols):
+            self.buf = buf
+            self.halves = (pl.ds(0, cols // 2), pl.ds(cols // 2, cols // 2))
+
+        def start(self):
             self.s0 = copy_to(wo_in, self.buf.at[y, x, c], core_dev, keep=False)
 
             @pl.when(c != zh)
             def _():
                 self.s0.start()
-                self.s0.wait_send()
-
+
+        def across(self):
             self.s1 = copy_to(self.buf.at[y, x], self.buf.at[y, x], half_dev, keep=False)
 
             @pl.when(c == zh)
@@ -531,41 +714,60 @@
                 self.buf[y, x, c] = wo_in[...]
                 self.s0.wait_recv()
                 self.s1.start()
-                self.s1.wait_send()
-
-        def third(self):
+
+        def first(self):
             @pl.when(c != zh)
             def _():
                 self.s1.wait_recv()
 
-            self.a = [
-                self.same(self.own(0, cut), dev) for cut, dev in zip(self.halves, (x_dev, y_dev))
-            ]
-
-        def fourth(self):
+            self.a = []
+            for cut, dev in zip(self.halves, (x_dev, y_dev)):
+                ref = self.buf.at[y, x, :, :, cut]
+                self.a.append(go_copy(ref, ref, dev))
+
+        def second(self):
             self.b = []
             for i, dev in enumerate((y_dev, x_dev)):
                 self.a[i].wait_recv()
-                self.b.append(self.same(self.line(0, self.halves[i], i), dev))
+                cut = self.halves[i]
+                ref = self.buf.at[y, :, :, :, cut] if i == 0 else self.buf.at[:, x, :, :, cut]
+                self.b.append(go_copy(ref, ref, dev))
 
         def done(self):
             for cp in self.b:
                 cp.wait_recv()
 
+        def end(self):
+            @pl.when(c != zh)
+            def _():
+                self.s0.wait_send()
+
+            @pl.when(c == zh)
+            def _():
+                self.s1.wait_send()
+
+
+    pieces = [pl.ds(i * (TOK // PIECES), TOK // PIECES) for i in range(PIECES)]
 
     class Share:
         def __init__(self, buf):
             self.buf = buf
+            self.to_pair = [
+                go_copy(buf.at[zp, c, cut], buf.at[zp, c, cut], pair_dev) for cut in pieces
+            ]
             self.to_core = go_copy(buf.at[zp, c], buf.at[zp, c], core_dev)
-            self.to_pair = go_copy(buf.at[zp, c], buf.at[zp, c], pair_dev)
 
         def forward(self):
-            self.to_pair.wait_recv()
-            self.fwd = go_copy(self.buf.at[1 - zp, c], self.buf.at[1 - zp, c], core_dev)
+            self.fwd = []
+            for cp, cut in zip(self.to_pair, pieces):
+                cp.wait_recv()
+                ref = self.buf.at[1 - zp, c, cut]
+                self.fwd.append(go_copy(ref, ref, core_dev))
 
         def done(self):
             self.to_core.wait_recv()
-            self.fwd.wait_recv()
+            for cp in self.fwd:
+                cp.wait_recv()
 
     class Reduce:
         def __init__(self, i):
@@ -575,93 +777,85 @@
         def cross(self):
             i = self.i
             self.mine.wait_recv()
-            ps_far[i] = (ps[i, 1 - zp, c].astype(F32) + ps_in[i, 1 - zp].astype(F32)).astype(BF)
-            self.far = go_copy(ps_far.at[i], ps_back.at[i], pair_dev)
+            self.far = []
+            for cut in pieces:
+                ps_far[i, cut] = (
+                    ps[i, 1 - zp, c, cut].astype(F32) + ps_in[i, 1 - zp, cut].astype(F32)
+                ).astype(BF)
+                self.far.append(go_copy(ps_far.at[i, cut], ps_back.at[i, cut], pair_dev))
 
         def total(self):
             i = self.i
             near = ps[i, zp, c].astype(F32) + ps_in[i, zp].astype(F32)
-            self.far.wait_recv()
+            for cp in self.far:
+                cp.wait_recv()
             return near + ps_back[i].astype(F32)
 
 
-    def add_into(pairs):
-        for target, extra in pairs:
-            t, e = target, extra
-            t[...] = (t[...].astype(F32) + e[...].astype(F32)).astype(BF)
+    def add_into(target, extra):
+        target[...] = (target[...].astype(F32) + extra[...].astype(F32)).astype(BF)
+
+    def add_all(mine, got):
+        n = got.shape[0]
+        if n == 1:
+            add_into(mine.at[0], got.at[0])
+            return
+
+        def body(j, carry):
+            add_into(mine.at[j], got.at[j])
+            return carry
+
+        lax.fori_loop(0, n, body, 0)
 
     class Scatter:
-        def __init__(self, buf, kind, cols, r1, r2, r3):
-            self.buf, self.kind, self.r1, self.r2, self.r3 = buf, kind, r1, r2, r3
+        def __init__(self, buf, cols, r1, r2, r3):
+            self.buf, self.r1, self.r2, self.r3 = buf, r1, r2, r3
             self.halves = (pl.ds(0, cols // 2), pl.ds(cols // 2, cols // 2))
-
-        def row(self, i, at, cut):
-            b = self.buf
-            if self.kind == "rows":
-                return b.at[:, at, :, :, :, cut] if i == 0 else b.at[:, :, at, :, :, cut]
-            if self.kind == "down":
-                return b.at[:, at, :, :, cut] if i == 0 else b.at[:, :, at, :, cut]
-            return b.at[at, :, :, :, cut] if i == 0 else b.at[:, at, :, :, cut]
-
-        def spot(self, Y, X, cut):
-            b = self.buf
-            if self.kind == "rows":
-                return b.at[:, Y, X, :, :, cut]
-            if self.kind == "down":
-                return b.at[:, Y, X, :, cut]
-            return b.at[Y, X, :, :, cut]
-
-        def first(self):
-            self.c1 = []
-            for i, (at, dev) in enumerate(((1 - y, y_dev), (1 - x, x_dev))):
-                self.c1.append(go_copy(self.row(i, at, self.halves[i]), self.r1.at[i], dev))
-
-        def second(self):
-            self.c2 = []
+            self.per_half = buf.shape[0] // 2
+            self.rest = (slice(None),) * (len(buf.shape) - 4)
+            self.c1, self.c2 = {}, {}
+
+        def of(self, which):
+            return pl.ds(self.per_half * which, self.per_half)
+
+        def line(self, i, which, other):
+            if i == 0:
+                at = (1 - y if other else y, slice(None))
+            else:
+                at = (slice(None), 1 - x if other else x)
+            return self.buf.at[(self.of(which),) + at + self.rest + (self.halves[i],)]
+
+        def spot(self, i, which, other):
+            Y, X = (y, x) if not other else ((y, 1 - x) if i == 0 else (1 - y, x))
+            return self.buf.at[(self.of(which), Y, X) + self.rest + (self.halves[i],)]
+
+        def first(self, far):
+            which = 1 - zh if far else zh
+            self.c1[far] = [
+                go_copy(self.line(i, which, True), self.r1.at[i, far], dev)
+                for i, dev in enumerate((y_dev, x_dev))
+            ]
+
+        def second(self, far):
+            which = 1 - zh if far else zh
+            self.c2[far] = []
             for i, dev in enumerate((x_dev, y_dev)):
-                self.c1[i].wait_recv()
-                at = y if i == 0 else x
-                mine = self.row(i, at, self.halves[i])
-                got = self.r1.at[i]
-
-                def body(j, carry, mine=mine, got=got):
-                    add_into([(mine.at[j], got.at[j])])
-                    return carry
-
-                lax.fori_loop(0, got.shape[0], body, 0)
-                there = (y, 1 - x) if i == 0 else (1 - y, x)
-                self.c2.append(
-                    go_copy(self.spot(*there, self.halves[i]), self.r2.at[i], dev)
-                )
-
-        def third(self):
+                self.c1[far][i].wait_recv()
+                add_all(self.line(i, which, False), self.r1.at[i, far])
+                self.c2[far].append(go_copy(self.spot(i, which, True), self.r2.at[i, far], dev))
+
+        def third(self, far):
+            which = 1 - zh if far else zh
             for i in range(2):
-                self.c2[i].wait_recv()
-                mine = self.spot(y, x, self.halves[i])
-                got = self.r2.at[i]
-
-                def body(j, carry, mine=mine, got=got):
-                    add_into([(mine.at[j], got.at[j])])
-                    return carry
-
-                lax.fori_loop(0, got.shape[0], body, 0)
-            self.over()
-
-        def over(self):
-            b = self.buf
-            src = (
-                b.at[pl.ds(2 * (1 - zh), 2), y, x]
-                if self.kind == "rows"
-                else b.at[1 - zh, y, x]
-            )
-            self.c3 = go_copy(src, self.r3, half_dev)
+                self.c2[far][i].wait_recv()
+                add_all(self.spot(i, which, False), self.r2.at[i, far])
+            if far:
+                self.c3 = go_copy(self.buf.at[self.of(which), y, x], self.r3, half_dev)
 
     class ScatterRows(Scatter):
         def fourth(self, out):
             self.c3.wait_recv()
-            self.out = out
-            for i in range(2):
-                add_into([(self.buf.at[2 * zh + i, y, x], self.r3.at[i])])
+            add_all(self.buf.at[self.of(zh), y, x], self.r3)
             self.c4 = []
             for dev, r in others:
                 src = self.buf.at[2 * zh + r // 2, y, x, lax.rem(r, 2)]
@@ -675,16 +869,45 @@
     class ScatterDown(Scatter):
         def fourth(self, out):
             self.c3.wait_recv()
-            out[...] = self.buf[zh, y, x].astype(F32) + self.r3[...].astype(F32)
-
-    class ScatterOut(Scatter):
-        def over(self):
+            out[...] = self.buf[zh, y, x].astype(F32) + self.r3[0].astype(F32)
+
+    class ScatterOut:
+        def __init__(self, buf, cols, r1, r2, r3):
+            self.buf, self.r1, self.r2, self.r3 = buf, r1, r2, r3
+            self.halves = (pl.ds(0, cols // 2), pl.ds(cols // 2, cols // 2))
+
+        def line(self, i, other):
+            cut = self.halves[i]
+            if i == 0:
+                return self.buf.at[1 - y if other else y, :, :, :, cut]
+            return self.buf.at[:, 1 - x if other else x, :, :, cut]
+
+        def spot(self, i, other):
+            Y, X = (y, x) if not other else ((y, 1 - x) if i == 0 else (1 - y, x))
+            return self.buf.at[Y, X, :, :, self.halves[i]]
+
+        def first(self):
+            self.c1 = [
+                go_copy(self.line(i, True), self.r1.at[i], dev)
+                for i, dev in enumerate((y_dev, x_dev))
+            ]
+
+        def second(self):
+            self.c2 = []
+            for i, dev in enumerate((x_dev, y_dev)):
+                self.c1[i].wait_recv()
+                add_all(self.line(i, False), self.r1.at[i])
+                self.c2.append(go_copy(self.spot(i, True), self.r2.at[i], dev))
+
+        def third(self):
+            for i in range(2):
+                self.c2[i].wait_recv()
+                add_all(self.spot(i, False), self.r2.at[i])
             self.c3 = copy_to(self.buf.at[y, x], self.r3, half_dev, keep=False)
 
             @pl.when(c != zh)
             def _():
                 self.c3.start()
-                self.c3.wait_send()
 
         def fourth(self, out):
             self.c4 = copy_to(self.r3.at[1 - c], out, core_dev, keep=False)
@@ -692,19 +915,19 @@
             @pl.when(c == zh)
             def _():
                 self.c3.wait_recv()
-                for i in range(2):
-                    add_into([(self.r3.at[i], self.buf.at[y, x, i])])
+                add_all(self.r3, self.buf.at[y, x])
                 self.c4.start()
                 out[...] = self.r3[c]
-                self.c4.wait_send()
-
+
+        def done(self):
             @pl.when(c != zh)
             def _():
                 self.c4.wait_recv()
-
-    s_q = spread(wq_in, wq)
-    seg_buf[zp, c] = seg_in[...]
-    s_seg = [go_copy(seg_buf.at[zp, c], seg_buf.at[zp, c], dev) for dev, _ in others]
+                self.c3.wait_send()
+
+            @pl.when(c == zh)
+            def _():
+                self.c4.wait_send()
 
     tokens = x_ref[...].astype(F32)
     centred = tokens - jnp.mean(tokens, axis=-1, keepdims=True)
@@ -713,34 +936,68 @@
     unit1[...] = unit
     inv1[...] = jnp.broadcast_to(inv, (TOK, 128))
     n1[zp, c] = unit.astype(BF)
-    share_n1 = Share(n1)
-
-    g_q = Gather(wq, "rows", QKV)
-    g_i = Gather(wi, "rows", 2 * HID)
-    g_d = Gather(wd, "down", WIDTH)
-    g_o = GatherOut(wo, "out", WIDTH)
-
+    qkv_rows = 3 * WIDTH // TOK
+    lines[0 : 32 * qkv_rows] = wq_flat[...].astype(F32)
+    gain = column(gain1_in)
+    for j in range(qkv_rows):
+        part, cut = divmod(j, 8)
+        r = (cut // 2 % 2) * 2 + cut // 4
+        w = lines[pl.ds(j, 32, stride=qkv_rows), :] * gain
+        wq_in[r, :, pl.ds(part * 256 + cut % 2 * 128, 128)] = w.astype(BF)
+    seg_buf[zp, c] = jnp.broadcast_to(seg_in[...].astype(F32), (8, TOK))
+    wq[z, y, x, c] = wq_in[role]
+    cot[zp, c] = cot_in[...]
+    lines2 = wide
+    lines2[0 : 8 * PART] = wd_flat[...].astype(F32)
+    lines2[8 * PART : 8 * PAD] = jnp.zeros((8 * (PAD - PART), TOK), F32)
+    for j in range(8):
+        wd[zh, y, x, :, pl.ds(j * 128, 128)] = lines2[pl.ds(j, PAD, stride=8), :].astype(BF)
+
+    g_q, g_i, g_d = Gather(wq, QKV), Gather(wi, 2 * HID), Gather(wd, WIDTH)
+    g_o = GatherOut(wo, WIDTH)
+
+    pl.semaphore_wait(barrier, 6)
+    s_q = spread(wq_in, wq)
+    g_d.own_first()
+    wide[0:256] = wo_flat[...].astype(F32)
+    for j in range(8):
+        wo_in[:, pl.ds(j * 128, 128)] = wide[pl.ds(j, 32, stride=8), :].astype(BF)
+    g_o.start()
+    s_seg = [go_copy(seg_buf.at[zp, c], seg_buf.at[zp, c], dev) for dev, _ in others]
+    in_rows = 2 * FF // TOK
+    lines[...] = wi_flat[...].astype(F32)
+    gain = column(gain2_in)
+    for j in range(in_rows):
+        wide[pl.ds(j * 32, 32), :] = lines[pl.ds(j, 32, stride=in_rows), :] * gain
+    for r in range(4):
+        for u in range(2 * HID // TOK):
+            tile = moved(in_moves(r, u), lambda t: wide[pl.ds(t * 32, 32), :])
+            wi_in[r, :, pl.ds(u * 128, 128)] = tile.astype(BF)
+    wi[z, y, x, c] = wi_in[role]
     for cp in s_q:
         cp.wait_recv()
-    g_q.first()
+    g_o.across()
+    g_q.across()
+    g_q.own_first()
+    g_d.own_second()
     s_i = spread(wi_in, wi)
-    g_o.first()
-    g_q.second()
-    share_n1.forward()
-    g_q.third()
+    share_n1 = Share(n1)
+    g_q.own_second()
+    g_d.across()
+    g_q.far_first()
     for cp in s_i:
         cp.wait_recv()
-    g_i.first()
-    cot[zp, c] = cot_in[...]
-    share_cot = Share(cot)
-    g_o.third()
-    g_q.fourth()
-    g_o.fourth()
-    wd[zh, y, x] = wd_in[...]
+    g_i.across()
+    g_i.own_first()
+    g_q.far_second()
+    g_o.first()
+    share_n1.forward()
     share_n1.done()
+    g_o.second()
     for cp in s_seg:
         cp.wait_recv()
     g_q.done()
+    g_i.own_second()
 
     lanes = lax.broadcasted_iota(jnp.int32, (1, 128), 1)
     low_half = lax.rem(lanes, 64) < 32
@@ -759,8 +1016,6 @@
         return carry
 
     lax.fori_loop(0, 2, qkv_step, 0)
-    g_i.second()
-    share_cot.forward()
 
     def only(head, u):
         return jnp.where(first_head if head == 0 else ~first_head, u, jnp.zeros_like(u))
@@ -796,9 +1051,8 @@
     lax.fori_loop(0, 2, branch, 0)
     red = Reduce(0)
     red.cross()
-    g_i.third()
-    g_d.first()
-    share_cot.done()
+    g_d.far_first()
+    g_i.far_first()
     mid = x_ref[...].astype(F32) + red.total()
     middle[...] = mid
     centred = mid - jnp.mean(mid, axis=-1, keepdims=True)
@@ -808,13 +1062,12 @@
     inv2[...] = jnp.broadcast_to(inv, (TOK, 128))
     n2[zp, c] = unit.astype(BF)
     share_n2 = Share(n2)
-    g_i.fourth()
-    g_d.second()
+    g_i.far_second()
     share_n2.forward()
-    g_d.third()
+    share_cot = Share(cot)
     share_n2.done()
+    g_d.far_second()
     g_i.done()
-    g_d.fourth()
 
     def upper(j, carry):
         at = pl.multiple_of(j * 256, 256)
@@ -834,6 +1087,8 @@
         return carry
 
     lax.fori_loop(0, HID // 256, upper, 0)
+    share_cot.forward()
+    share_cot.done()
 
     def down_grad(i, carry):
         lhs = hidden[:, :, pl.ds(pl.multiple_of(i * 384, 384), 384)].reshape(512, 384)
@@ -845,8 +1100,8 @@
         return carry
 
     lax.fori_loop(0, 2, down_grad, 0)
-    r_d = ScatterDown(gd, "down", WIDTH, rd1, rd2, rd3)
-    r_d.first()
+    r_d = ScatterDown(gd, WIDTH, rd1, rd2, rd3)
+    r_d.first(1)
     g_d.done()
 
     def hidden_grad(i, carry):
@@ -873,9 +1128,9 @@
 
     lax.fori_loop(0, 4, normed_two_grad, 0)
     red = Reduce(1)
-    r_d.second()
-
-    def in_grad(i, carry):
+
+    def in_grad(k, carry):
+        i = k
         lhs = n2[:, :, :, pl.ds(pl.multiple_of(i * 256, 256), 256)].reshape(512, 256)
         for j in range(3):
             rhs = d_up[:, :, pl.ds(j * 512, 512)].reshape(512, 512)
@@ -884,10 +1139,13 @@
             )
         return carry
 
-    lax.fori_loop(0, 4, in_grad, 0)
+    lax.fori_loop(2 * (1 - zh), 2 * (1 - zh) + 2, in_grad, 0)
+    r_i = ScatterRows(gi, 2 * HID, ri1, ri2, ri3)
+    r_i.first(1)
     red.cross()
-    r_i = ScatterRows(gi, "rows", 2 * HID, ri1, ri2, ri3)
-    r_i.first()
+    lax.fori_loop(2 * zh, 2 * zh + 2, in_grad, 0)
+    r_d.second(1)
+    r_d.first(0)
 
     e = red.total()
     n = unit2[...]
@@ -899,7 +1157,6 @@
     dmid[...] = d_middle
     db[zp, c] = d_middle.astype(BF)
     share_db = Share(db)
-    r_d.third()
 
     def down(i, carry):
         w = wd[...].reshape(HID, WIDTH)
@@ -907,11 +1164,10 @@
         return carry
 
     lax.fori_loop(0, 2, down, 0)
+    share_db.forward()
+    r_d.third(1)
+    r_i.second(1)
     red_out = Reduce(2)
-    share_db.forward()
-    red_out.cross()
-    r_i.second()
-    r_d.fourth(gd_ref)
     share_db.done()
 
     def attended_grad(s, carry):
@@ -922,6 +1178,16 @@
         return carry
 
     lax.fori_loop(0, 2, attended_grad, 0)
+
+    lhs = att
+    for j in range(2):
+        for half in range(2):
+            rhs = db[:, :, :, pl.ds(half * 512, 512)].reshape(512, 512)
+            go[j, :, :, :, pl.ds(half * 512, 512)] = (
+                matmul_tn(lhs[:, j].reshape(512, 128), rhs).astype(BF).reshape(2, 2, 32, 512)
+            )
+    r_o = ScatterOut(go, WIDTH, ro1, ro2, ro3)
+    r_o.first()
 
     def attend_back(i, carry):
         s, j = i // 2, lax.rem(i, 2)
@@ -943,8 +1209,25 @@
             dqkv[part, j, s] = u.astype(BF)
         return carry
 
+    r_d.second(0)
+    red_out.cross()
     lax.fori_loop(0, 4, attend_back, 0)
-    r_i.third()
+    r_i.third(1)
+
+    def qkv_grad(i, carry):
+        lhs = n1[:, :, :, pl.ds(pl.multiple_of(i * 256, 256), 256)].reshape(512, 256)
+        for p in range(3):
+            for j in range(2):
+                rhs = dqkv[p, j].reshape(512, 128)
+                gq[i, :, :, :, :, pl.ds(p * 256 + j * 128, 128)] = (
+                    matmul_tn(lhs, rhs).astype(BF).reshape(2, 2, 2, 32, 128)
+                )
+        return carry
+
+    lax.fori_loop(2 * (1 - zh), 2 * (1 - zh) + 2, qkv_grad, 0)
+    r_q = ScatterRows(gq, QKV, rq1, rq2, rq3)
+    r_q.first(1)
+    lax.fori_loop(2 * zh, 2 * zh + 2, qkv_grad, 0)
 
     def first_grads(i, carry):
         w = wq[i].reshape(256, QKV)
@@ -959,73 +1242,56 @@
     lax.fori_loop(0, 4, first_grads, 0)
     red_in = Reduce(3)
 
-    def qkv_grad(i, carry):
-        lhs = n1[:, :, :, pl.ds(pl.multiple_of(i * 256, 256), 256)].reshape(512, 256)
-        for p in range(3):
-            for j in range(2):
-                rhs = dqkv[p, j].reshape(512, 128)
-                gq[i, :, :, :, :, pl.ds(p * 256 + j * 128, 128)] = (
-                    matmul_tn(lhs, rhs).astype(BF).reshape(2, 2, 2, 32, 128)
-                )
-        return carry
-
-    lax.fori_loop(0, 4, qkv_grad, 0)
-    r_q = ScatterRows(gq, "rows", QKV, rq1, rq2, rq3)
-    r_q.first()
-
-    lhs = att
-    for j in range(2):
-        for half in range(2):
-            rhs = db[:, :, :, pl.ds(half * 512, 512)].reshape(512, 512)
-            go[j, :, :, :, pl.ds(half * 512, 512)] = (
-                matmul_tn(lhs[:, j].reshape(512, 128), rhs).astype(BF).reshape(2, 2, 32, 512)
-            )
-    r_o = ScatterOut(go, "out", WIDTH, ro1, ro2, ro3)
-    r_o.first()
+    r_q.second(1)
+    r_i.first(0)
     red_in.cross()
-    r_i.fourth(gi_ref)
-    out_ref[...] = (middle[...] + red_out.total()).astype(BF)
-    r_q.second()
     r_o.second()
+    r_q.third(1)
+    r_q.first(0)
+    r_d.third(0)
+    r_d.fourth(gd_vm)
+    emit(2, gd_vm, gd_ref)
     e = red_in.total()
     n = unit1[...]
-    ig_ref[...] = dmid[...] + inv1[:, 0:1] * (
+    ig_vm[...] = dmid[...] + inv1[:, 0:1] * (
         e
         - jnp.mean(e, axis=-1, keepdims=True)
         - n * jnp.mean(e * n, axis=-1, keepdims=True)
     )
-    r_q.third()
+    emit(1, ig_vm, ig_ref)
+    out_vm[...] = (middle[...] + red_out.total()).astype(BF)
+    emit(0, out_vm, out_ref)
+    r_i.second(0)
+    r_q.second(0)
     r_o.third()
-    r_q.fourth(gq_ref)
-    r_o.fourth(go_ref)
+    settle()
+    r_i.third(0)
+    r_i.fourth(gi_vm)
+    r_o.fourth(go_vm)
+    r_q.third(0)
+    r_q.fourth(gq_vm)
     r_i.done()
+    emit(3, gi_vm, gi_ref)
+    r_o.done()
+    emit(4, go_vm, go_ref)
     r_q.done()
-    for cp in sent:
-        cp.wait_send()
+    emit(5, gq_vm, gq_ref)
+    g_o.end()
+    settle()
+    for cp in local:
+        cp.wait()
 
 
 def block_device(inputs, segments, cotangent, ln1_gain, w_qkv, w_attn_out, ln2_gain, w_in, w_mlp_out):
-    gain_one = ln1_gain.astype(F32)[:, None]
-    gain_two = ln2_gain.astype(F32)[:, None]
-    qkv_own = w_qkv.reshape(32, 3 * WIDTH).astype(F32)
-    in_own = w_in.reshape(32, 2 * FF).astype(F32)
-    wq_in = (
-        (qkv_own * gain_one)
-        .astype(BF)
-        .reshape(32, 3, 2, 2, 256)
-        .transpose(3, 2, 0, 1, 4)
-        .reshape(4, 32, QKV)
-    )
-    wi_in = (in_own * gain_two).astype(BF).reshape(32, 2, 2, 2, 2, 2, 2, PART)
-    wi_in = jnp.pad(wi_in, ((0, 0),) * 7 + ((0, PAD - PART),))
-    wi_in = wi_in.transpose(3, 6, 0, 1, 2, 4, 5, 7).reshape(4, 32, 2 * HID)
-    wd_in = jnp.pad(w_mlp_out.reshape(PART, WIDTH), ((0, PAD - PART), (0, 0)))
-    wo_in = w_attn_out.reshape(32, WIDTH)
-    seg = jnp.broadcast_to(segments.astype(F32), (8, TOK))
-    cosines, sines = rope_tables(jnp.arange(2 * TOK, dtype=jnp.int32).astype(F32))
-    signs = jnp.where(jnp.arange(HD) < HD // 2, -1.0, 1.0).astype(F32)
-    cosines = jnp.tile(cosines, (1, 2))
-    sines = jnp.tile(sines * signs, (1, 2))
+    places = np.arange(2 * TOK, dtype=np.float32)
+    freqs = (1.0 / ROPE_BASE ** (np.arange(0, HD, 2, dtype=np.float64) / HD)).astype(np.float32)
+    angles = np.tile(places[:, None] * freqs[None, :], (1, 4))
+    signs = np.where(np.arange(2 * HD) % HD < HD // 2, -1.0, 1.0).astype(np.float32)
+    cosines = jnp.asarray(np.cos(angles))
+    sines = jnp.asarray(np.sin(angles) * signs)
+    gain_one, gain_two = ln1_gain[None], ln2_gain[None]
+    wq_flat, wo_flat = w_qkv.reshape(-1, TOK), w_attn_out.reshape(-1, TOK)
+    wi_flat, wd_flat = w_in.reshape(-1, TOK), w_mlp_out.reshape(-1, TOK)
 
     vm = pltpu.VMEM
     group = (2, 2, TOK, WIDTH)
@@ -1040,8 +1306,8 @@
             jax.ShapeDtypeStruct((4, 32, 2 * HID), BF),
             jax.ShapeDtypeStruct((PAD, WIDTH), F32),
         ),
-        in_specs=[pl.BlockSpec(memory_space=vm)] * 9,
-        out_specs=(pl.BlockSpec(memory_space=vm),) * 6,
+        in_specs=[pl.BlockSpec(memory_space=vm)] * 11,
+        out_specs=(pl.BlockSpec(memory_space=pl.ANY),) * 6,
         scratch_shapes=[
             vm((2, 2, 8, TOK), F32),
             vm(group, BF),
@@ -1077,43 +1343,91 @@
             vm((2, 2, 2, 32, WIDTH), BF),
             vm(rows + (2 * HID,), BF),
             vm((2, 2, 2, PAD, WIDTH), BF),
-            vm((2, 4, 2, 2, 32, QKV // 2), BF),
-            vm((2, 4, 2, 32, QKV // 2), BF),
+            vm((2, 2, 2, 2, 2, 32, QKV // 2), BF),
+            vm((2, 2, 2, 2, 32, QKV // 2), BF),
             vm((2, 2, 32, QKV), BF),
             vm((2, 2, 2, 32, WIDTH // 2), BF),
             vm((2, 2, 32, WIDTH // 2), BF),
             vm((2, 32, WIDTH), BF),
-            vm((2, 4, 2, 2, 32, HID), BF),
-            vm((2, 4, 2, 32, HID), BF),
+            vm((2, 2, 2, 2, 2, 32, HID), BF),
+            vm((2, 2, 2, 2, 32, HID), BF),
             vm((2, 2, 32, 2 * HID), BF),
-            vm((2, 2, 2, PAD, WIDTH // 2), BF),
-            vm((2, 2, PAD, WIDTH // 2), BF),
-            vm((PAD, WIDTH), BF),
+            vm((2, 2, 1, 2, PAD, WIDTH // 2), BF),
+            vm((2, 2, 1, PAD, WIDTH // 2), BF),
+            vm((1, PAD, WIDTH), BF),
+            vm((4, 32, QKV), BF),
+            vm((32, WIDTH), BF),
+            vm((4, 32, 2 * HID), BF),
+            vm((64 * FF // TOK, TOK), F32),
+            vm((64 * FF // TOK, TOK), F32),
+            vm((TOK, WIDTH), BF),
+            vm((TOK, WIDTH), F32),
+            vm((4, 32, QKV), BF),
+            vm((32, WIDTH), BF),
+            vm((4, 32, 2 * HID), BF),
+            vm((PAD, WIDTH), F32),
             pltpu.SemaphoreType.DMA((N_COPIES,)),
             pltpu.SemaphoreType.DMA((N_COPIES,)),
+            pltpu.SemaphoreType.DMA((6,)),
         ],
         compiler_params=pltpu.CompilerParams(
             collective_id=0, has_side_effects=True, vmem_limit_bytes=60 * 2**20
         ),
-    )(inputs[0], cotangent[0], seg, cosines, sines, wq_in, wo_in, wi_in, wd_in)
+    )(
+        inputs[0],
+        cotangent[0],
+        segments,
+        cosines,
+        sines,
+        gain_one,
+        gain_two,
+        wq_flat,
+        wo_flat,
+        wi_flat,
+        wd_flat,
+    )
     output, input_grad, gq, go, gi, gd = outs
-
-    raw_q = gq.astype(F32).reshape(2, 2, 32, 3, 256).transpose(2, 3, 1, 0, 4).reshape(32, 3 * WIDTH)
-    raw_i = gi.astype(F32).reshape(2, 2, 32, 2, 2, 2, 2, PAD)[..., :PART]
-    raw_i = raw_i.transpose(2, 3, 4, 0, 5, 6, 1, 7).reshape(32, 2 * FF)
-    return (
-        output[None],
-        input_grad[None],
-        jnp.sum(raw_q * qkv_own, axis=1),
-        (raw_q * gain_one).reshape(-1),
-        go.astype(F32).reshape(-1),
-        jnp.sum(raw_i * in_own, axis=1),
-        (raw_i * gain_two).reshape(-1),
-        gd[:PART].reshape(-1),
-    )
-
-
-N_COPIES = 160
+    final = pl.pallas_call(
+        finish_kernel,
+        out_shape=(
+            jax.ShapeDtypeStruct((TOK, WIDTH), BF),
+            jax.ShapeDtypeStruct((TOK, WIDTH), F32),
+            jax.ShapeDtypeStruct((1, 32), F32),
+            jax.ShapeDtypeStruct(wq_flat.shape, F32),
+            jax.ShapeDtypeStruct(wo_flat.shape, F32),
+            jax.ShapeDtypeStruct((1, 32), F32),
+            jax.ShapeDtypeStruct(wi_flat.shape, F32),
+            jax.ShapeDtypeStruct(wd_flat.shape, F32),
+        ),
+        in_specs=[pl.BlockSpec(memory_space=pl.ANY)] * 6
+        + [pl.BlockSpec(memory_space=vm)] * 2
+        + [pl.BlockSpec(memory_space=pl.ANY)] * 2,
+        out_specs=tuple(
+            pl.BlockSpec(memory_space=vm if i in (2, 5) else pl.ANY) for i in range(8)
+        ),
+        scratch_shapes=[
+            vm(wi_flat.shape, F32),
+            vm((4, 32, QKV), BF),
+            vm((32, WIDTH), BF),
+            vm((4, 32, 2 * HID), BF),
+            vm((PAD, WIDTH), F32),
+            vm(wq_flat.shape, BF),
+            vm(wi_flat.shape, BF),
+            vm(wq_flat.shape, F32),
+            vm(wo_flat.shape, F32),
+            vm(wi_flat.shape, F32),
+            vm(wd_flat.shape, F32),
+            vm((TOK, WIDTH), F32),
+            vm((TOK, WIDTH), BF),
+            pltpu.SemaphoreType.DMA((14,)),
+        ],
+        compiler_params=pltpu.CompilerParams(vmem_limit_bytes=60 * 2**20),
+    )(gq, go, gi, gd, output, input_grad, gain_one, gain_two, wq_flat, wi_flat)
+    return (final[0][None], final[1][None]) + tuple(f.reshape(-1) for f in final[2:])
+
+
+N_COPIES = 116
+PIECES = 2
 
 
 def solution(mesh):

time: 183 us -> 144 us (0.79)
  local copies, waits for them, and re-layouts: 17.7 us -> 0 us
  Pallas kernels: 158 us -> 143 us
  other arithmetic: 6.05 us -> 0 us
    pallas_call x1, Pallas kernels: 158 us -> 139 us  [block_device(): pl.pallas_call(functools.partial(layer_kernel, [0]), out_shape=(jax.Shape...]
    reshape x7 -> x0, local copies, waits for them, and re-layouts: 5.94 us -> none  [the longest x1 1.75 us: block_device(): raw_i = raw_i.transpose(2, 3, 4, 0, 5, 6, 1, 7).reshape(32, 2 * FF)]
    pallas_call x0 -> x1, Pallas kernels: none -> 4.19 us  [block_device(): pl.pallas_call(finish_kernel, out_shape=(jax.ShapeDtypeStruct((TOK, WIDTH...]
    unnamed x28 -> x0, local copies, waits for them, and re-layouts: 3.41 us -> none
    convert_element_type x2 -> x0, local copies, waits for them, and re-layouts: 3.22 us -> none  [the longest x1 2.05 us: block_device(): in_own = w_in.reshape(32, 2 * FF).astype(F32)]
    reduce_sum x2 -> x0, other arithmetic: 2.53 us -> none  [the longest x1 1.51 us: block_device(): jnp.sum(raw_i * in_own, axis=1)]
    transpose x4 -> x0, local copies, waits for them, and re-layouts: 2.12 us -> none  [the longest x1 1.13 us: block_device(): gq.astype(F32).reshape(2, 2, 32, 3, 256).transpose(2, 3, 1, 0, 4)]
    mul x4 -> x0, other arithmetic: 1.91 us -> none  [the longest x1 0.91 us: block_device(): raw_i * gain_two]
where the time goes in v2:
time: 144 us
  Pallas kernels  143 us (99%)
    pallas_call x1, Pallas kernels, block_device(): pl.pallas_call(functools.partial(layer_kernel, [0]), out_shape=(jax.Shape...  139 us
    pallas_call x1, Pallas kernels, block_device(): pl.pallas_call(finish_kernel, out_shape=(jax.ShapeDtypeStruct((TOK, WIDTH...  4.19 us

profile of v2, /device:TPU:0, one launch (start us, length us, event | category | flops | bytes accessed | tf_op | source)
XLA Modules:
  0.0 143.8 jit_solution(15693967407337121912)
XLA Ops:
  0.6 139.0 %shard_map.170 = (bf16[128,1024]{1,0:T(8,128)(2,1)}, f32[128,1024]{1,0:T(8,128)}, bf16[4,32,768]{2,1,0:T(8,128)(2,1)}, bf16[32,1024]{1,0:T(8,128)(2,1)}, bf16[4,...) custom-call(bf16[128,1024]{1,0:T(8,128)(2,1)} %bitcast.20, bf16[128,1024]{1,0:T(8,128)(2,1)} %bitcast.21, s32[1,128]{1,0:T(1,128)} %seg_in.1, ...), custom_call_target="tpu_custom_call" | custom-call | tf_op jit(solution)/shard_map/pallas_call | solution.py:1299
  139.7 4.2 %shard_map.171 = (bf16[128,1024]{1,0:T(8,128)(2,1)}, f32[128,1024]{1,0:T(8,128)}, f32[1,32]{1,0:T(1,128)}, f32[768,128]{1,0:T(8,128)}, f32[256,128]{1,0:T(8,128)...) custom-call(bf16[4,32,768]{2,1,0:T(8,128)(2,1)} %get-tuple-element.22.gq_in, ...), custom_call_target="tpu_custom_call" | custom-call | tf_op jit(solution)/shard_map/pallas_call | solution.py:1390

commit v3 on v2

--- a/solution.py
+++ b/solution.py
@@ -458,23 +458,27 @@
         total = jnp.sum(total, axis=1, keepdims=True)
         return jnp.sum(jnp.where(rows == cols, total, 0.0), axis=0, keepdims=True)
 
+    qkv_rows = 3 * WIDTH // TOK
     in_rows = 2 * FF // TOK
     gain = column(gain2_in)
     total = jnp.zeros((32, 128), F32)
     wi_here.wait()
     lines[...] = wi_raw[...].astype(F32)
+    ig_here.wait()
+    written.append(start(ig_raw, ig_ref))
+    out_here.wait()
+    written.append(start(out_raw, out_ref))
+    gd_here.wait()
+    for j in range(8):
+        gd_own[pl.ds(j, PART, stride=8), :] = gd_raw[0:PART, pl.ds(j * 128, 128)]
+    written.append(start(gd_own, gd_ref))
     gi_here.wait()
     for j in range(in_rows):
         g = moved(out_moves(j), lambda t: gi_raw[t[0], :, pl.ds(t[1] * 128, 128)].astype(F32))
         total = total + g * lines[pl.ds(j, 32, stride=in_rows), :]
         gi_own[pl.ds(j, 32, stride=in_rows), :] = g * gain
     written.append(start(gi_own, gi_ref))
-    ig_here.wait()
-    written.append(start(ig_raw, ig_ref))
-    out_here.wait()
-    written.append(start(out_raw, out_ref))
     gain2_ref[...] = line(total)
-    qkv_rows = 3 * WIDTH // TOK
     gain = column(gain1_in)
     total = jnp.zeros((32, 128), F32)
     wq_here.wait()
@@ -488,10 +492,6 @@
         gq_own[pl.ds(j, 32, stride=qkv_rows), :] = g * gain
     written.append(start(gq_own, gq_ref))
     gain1_ref[...] = line(total)
-    gd_here.wait()
-    for j in range(8):
-        gd_own[pl.ds(j, PART, stride=8), :] = gd_raw[0:PART, pl.ds(j * 128, 128)]
-    written.append(start(gd_own, gd_ref))
     go_here.wait()
     for j in range(8):
         go_own[pl.ds(j, 32, stride=8), :] = go_raw[:, pl.ds(j * 128, 128)].astype(F32)
@@ -501,7 +501,6 @@
 
 
 def layer_kernel(
-    n_sems,
     x_ref,
     cot_in,
     seg_in,
@@ -600,20 +599,22 @@
         pl.semaphore_signal(barrier, inc=1, device_id=dev, device_id_type=MESH_IDS)
 
     sent = []
+    n_sems = [0]
+    free = list(range(N_SENDS))
 
     def copy_to(src, dst, dev, keep=True):
-        i = n_sems[0]
+        i, k = n_sems[0], free.pop(0)
         n_sems[0] += 1
         cp = pltpu.make_async_remote_copy(
             src_ref=src,
             dst_ref=dst,
-            send_sem=send_sems.at[i],
+            send_sem=send_sems.at[k],
             recv_sem=recv_sems.at[i],
             device_id=dev,
             device_id_type=MESH_IDS,
         )
         if keep:
-            sent.append(cp)
+            sent.append((cp, k))
         return cp
 
     local = []
@@ -623,10 +624,11 @@
         cp.start()
         local.append(cp)
 
-    def settle():
-        for cp in sent:
+    def settle(first):
+        for cp, k in sent[:first]:
             cp.wait_send()
-        del sent[:]
+            free.append(k)
+        del sent[:first]
 
     def go_copy(src, dst, dev):
         cp = copy_to(src, dst, dev)
@@ -645,9 +647,9 @@
         return cps
 
     class Gather:
-        def __init__(self, buf, cols):
+        def __init__(self, buf, cols, base=0):
             self.buf = buf
-            self.halves = (pl.ds(0, cols // 2), pl.ds(cols // 2, cols // 2))
+            self.halves = (pl.ds(base, cols // 2), pl.ds(base + cols // 2, cols // 2))
             self.per_half = buf.shape[0] // 2
 
         def of(self, which):
@@ -764,19 +766,28 @@
                 ref = self.buf.at[1 - zp, c, cut]
                 self.fwd.append(go_copy(ref, ref, core_dev))
 
+        def core(self):
+            self.to_core.wait_recv()
+
         def done(self):
-            self.to_core.wait_recv()
             for cp in self.fwd:
                 cp.wait_recv()
 
     class Reduce:
         def __init__(self, i):
             self.i = i
-            self.mine = go_copy(ps.at[i, :, 1 - c], ps_in.at[i], core_dev)
+
+        def far_terms(self):
+            i = self.i
+            self.mine_far = go_copy(ps.at[i, 1 - zp, 1 - c], ps_in.at[i, 1 - zp], core_dev)
+
+        def near_terms(self):
+            i = self.i
+            self.mine_near = go_copy(ps.at[i, zp, 1 - c], ps_in.at[i, zp], core_dev)
 
         def cross(self):
             i = self.i
-            self.mine.wait_recv()
+            self.mine_far.wait_recv()
             self.far = []
             for cut in pieces:
                 ps_far[i, cut] = (
@@ -786,6 +797,7 @@
 
         def total(self):
             i = self.i
+            self.mine_near.wait_recv()
             near = ps[i, zp, c].astype(F32) + ps_in[i, zp].astype(F32)
             for cp in self.far:
                 cp.wait_recv()
@@ -808,9 +820,10 @@
         lax.fori_loop(0, n, body, 0)
 
     class Scatter:
-        def __init__(self, buf, cols, r1, r2, r3):
+        def __init__(self, buf, cols, r1, r2, r3, base=0):
             self.buf, self.r1, self.r2, self.r3 = buf, r1, r2, r3
-            self.halves = (pl.ds(0, cols // 2), pl.ds(cols // 2, cols // 2))
+            self.halves = (pl.ds(base, cols // 2), pl.ds(base + cols // 2, cols // 2))
+            self.cols = pl.ds(base, cols)
             self.per_half = buf.shape[0] // 2
             self.rest = (slice(None),) * (len(buf.shape) - 4)
             self.c1, self.c2 = {}, {}
@@ -850,17 +863,19 @@
                 self.c2[far][i].wait_recv()
                 add_all(self.spot(i, which, False), self.r2.at[i, far])
             if far:
-                self.c3 = go_copy(self.buf.at[self.of(which), y, x], self.r3, half_dev)
+                src = self.buf.at[(self.of(which), y, x) + self.rest + (self.cols,)]
+                self.c3 = go_copy(src, self.r3, half_dev)
 
     class ScatterRows(Scatter):
         def fourth(self, out):
             self.c3.wait_recv()
-            add_all(self.buf.at[self.of(zh), y, x], self.r3)
+            cols = self.cols
+            add_all(self.buf.at[self.of(zh), y, x, :, :, cols], self.r3)
             self.c4 = []
             for dev, r in others:
-                src = self.buf.at[2 * zh + r // 2, y, x, lax.rem(r, 2)]
-                self.c4.append(go_copy(src, out.at[role], dev))
-            out[role] = self.buf[z, y, x, c]
+                src = self.buf.at[2 * zh + r // 2, y, x, lax.rem(r, 2), :, cols]
+                self.c4.append(go_copy(src, out.at[role, :, cols], dev))
+            out[role, :, cols] = self.buf[z, y, x, c, :, cols]
 
         def done(self):
             for cp in self.c4:
@@ -953,52 +968,18 @@
     for j in range(8):
         wd[zh, y, x, :, pl.ds(j * 128, 128)] = lines2[pl.ds(j, PAD, stride=8), :].astype(BF)
 
-    g_q, g_i, g_d = Gather(wq, QKV), Gather(wi, 2 * HID), Gather(wd, WIDTH)
+    g_q, g_d = Gather(wq, QKV), Gather(wd, WIDTH)
+    g_i, g_j = Gather(wi, HID), Gather(wi, HID, HID)
     g_o = GatherOut(wo, WIDTH)
 
-    pl.semaphore_wait(barrier, 6)
-    s_q = spread(wq_in, wq)
-    g_d.own_first()
-    wide[0:256] = wo_flat[...].astype(F32)
-    for j in range(8):
-        wo_in[:, pl.ds(j * 128, 128)] = wide[pl.ds(j, 32, stride=8), :].astype(BF)
-    g_o.start()
-    s_seg = [go_copy(seg_buf.at[zp, c], seg_buf.at[zp, c], dev) for dev, _ in others]
-    in_rows = 2 * FF // TOK
-    lines[...] = wi_flat[...].astype(F32)
-    gain = column(gain2_in)
-    for j in range(in_rows):
-        wide[pl.ds(j * 32, 32), :] = lines[pl.ds(j, 32, stride=in_rows), :] * gain
-    for r in range(4):
-        for u in range(2 * HID // TOK):
-            tile = moved(in_moves(r, u), lambda t: wide[pl.ds(t * 32, 32), :])
-            wi_in[r, :, pl.ds(u * 128, 128)] = tile.astype(BF)
-    wi[z, y, x, c] = wi_in[role]
-    for cp in s_q:
-        cp.wait_recv()
-    g_o.across()
-    g_q.across()
-    g_q.own_first()
-    g_d.own_second()
-    s_i = spread(wi_in, wi)
-    share_n1 = Share(n1)
-    g_q.own_second()
-    g_d.across()
-    g_q.far_first()
-    for cp in s_i:
-        cp.wait_recv()
-    g_i.across()
-    g_i.own_first()
-    g_q.far_second()
-    g_o.first()
-    share_n1.forward()
-    share_n1.done()
-    g_o.second()
-    for cp in s_seg:
-        cp.wait_recv()
-    g_q.done()
-    g_i.own_second()
-
+
+    r_d = ScatterDown(gd, WIDTH, rd1, rd2, rd3)
+    r_i = ScatterRows(gi, HID, ri1.at[0], ri2.at[0], ri3.at[0])
+    r_j = ScatterRows(gi, HID, ri1.at[1], ri2.at[1], ri3.at[1], HID)
+    r_q = ScatterRows(gq, QKV, rq1, rq2, rq3)
+    r_o = ScatterOut(go, WIDTH, ro1, ro2, ro3)
+    on = {}
+    red = [Reduce(i) for i in range(4)]
     lanes = lax.broadcasted_iota(jnp.int32, (1, 128), 1)
     low_half = lax.rem(lanes, 64) < 32
     first_head = lanes < 64
@@ -1014,8 +995,6 @@
                     u = u * cos_ref[...] + turned(u, low_half) * sin_ref[...]
                 dst[s, j] = u.astype(BF)
         return carry
-
-    lax.fori_loop(0, 2, qkv_step, 0)
 
     def only(head, u):
         return jnp.where(first_head if head == 0 else ~first_head, u, jnp.zeros_like(u))
@@ -1037,9 +1016,6 @@
         att[s, j] = jnp.where(first_head, heads[0], heads[1]).astype(BF)
         return carry
 
-    lax.fori_loop(0, 4, attend, 0)
-    g_o.done()
-
     def att_rows(s):
         return jnp.concatenate([att[s, 0], att[s, 1]], axis=1)
 
@@ -1048,30 +1024,9 @@
         ps[0, s] = dot_nn(att_rows(s), w).astype(BF).reshape(2, TOK, WIDTH)
         return carry
 
-    lax.fori_loop(0, 2, branch, 0)
-    red = Reduce(0)
-    red.cross()
-    g_d.far_first()
-    g_i.far_first()
-    mid = x_ref[...].astype(F32) + red.total()
-    middle[...] = mid
-    centred = mid - jnp.mean(mid, axis=-1, keepdims=True)
-    inv = lax.rsqrt(jnp.mean(centred * centred, axis=-1, keepdims=True) + EPSILON)
-    unit = centred * inv
-    unit2[...] = unit
-    inv2[...] = jnp.broadcast_to(inv, (TOK, 128))
-    n2[zp, c] = unit.astype(BF)
-    share_n2 = Share(n2)
-    g_i.far_second()
-    share_n2.forward()
-    share_cot = Share(cot)
-    share_n2.done()
-    g_d.far_second()
-    g_i.done()
-
-    def upper(j, carry):
-        at = pl.multiple_of(j * 256, 256)
-        for s in range(2):
+    def upper_for(s):
+        def upper(j, carry):
+            at = pl.multiple_of(j * 256, 256)
             rows = n2[s].reshape(256, WIDTH)
             inner = dot_nn(rows, wi[:, :, :, :, :, pl.ds(at, 256)].reshape(WIDTH, 256))
             gate = dot_nn(
@@ -1084,11 +1039,9 @@
             up_a[s, :, pl.ds(at, 256)] = gate * slope
             up_b[s, :, pl.ds(at, 256)] = bent
             hidden[s, :, pl.ds(at, 256)] = (bent * gate).astype(BF)
-        return carry
-
-    lax.fori_loop(0, HID // 256, upper, 0)
-    share_cot.forward()
-    share_cot.done()
+            return carry
+
+        lax.fori_loop(0, HID // 256, upper, 0)
 
     def down_grad(i, carry):
         lhs = hidden[:, :, pl.ds(pl.multiple_of(i * 384, 384), 384)].reshape(512, 384)
@@ -1098,11 +1051,6 @@
                 matmul_tn(lhs, rhs).astype(BF).reshape(2, 2, PAD, 512)
             )
         return carry
-
-    lax.fori_loop(0, 2, down_grad, 0)
-    r_d = ScatterDown(gd, WIDTH, rd1, rd2, rd3)
-    r_d.first(1)
-    g_d.done()
 
     def hidden_grad(i, carry):
         w = wd[i].reshape(384, WIDTH)
@@ -1115,60 +1063,32 @@
             ).astype(BF)
         return carry
 
-    lax.fori_loop(0, 2, hidden_grad, 0)
-
-    def normed_two_grad(i, carry):
-        w = wi[i].reshape(256, 2 * HID)
-        at = pl.multiple_of(i * 256, 256)
-        for s in range(2):
-            ps[1, s, :, :, pl.ds(at, 256)] = (
-                matmul_nt(d_up[s], w).astype(BF).reshape(2, TOK, 256)
-            )
-        return carry
-
-    lax.fori_loop(0, 4, normed_two_grad, 0)
-    red = Reduce(1)
-
-    def in_grad(k, carry):
-        i = k
-        lhs = n2[:, :, :, pl.ds(pl.multiple_of(i * 256, 256), 256)].reshape(512, 256)
-        for j in range(3):
-            rhs = d_up[:, :, pl.ds(j * 512, 512)].reshape(512, 512)
-            gi[i, :, :, :, :, pl.ds(j * 512, 512)] = (
-                matmul_tn(lhs, rhs).astype(BF).reshape(2, 2, 2, 32, 512)
-            )
-        return carry
-
-    lax.fori_loop(2 * (1 - zh), 2 * (1 - zh) + 2, in_grad, 0)
-    r_i = ScatterRows(gi, 2 * HID, ri1, ri2, ri3)
-    r_i.first(1)
-    red.cross()
-    lax.fori_loop(2 * zh, 2 * zh + 2, in_grad, 0)
-    r_d.second(1)
-    r_d.first(0)
-
-    e = red.total()
-    n = unit2[...]
-    d_middle = cot_in[...].astype(F32) + inv2[:, 0:1] * (
-        e
-        - jnp.mean(e, axis=-1, keepdims=True)
-        - n * jnp.mean(e * n, axis=-1, keepdims=True)
-    )
-    dmid[...] = d_middle
-    db[zp, c] = d_middle.astype(BF)
-    share_db = Share(db)
+    def normed_two_grad_for(s):
+        def normed_two_grad(i, carry):
+            w = wi[i].reshape(256, 2 * HID)
+            at = pl.multiple_of(i * 256, 256)
+            ps[1, s, :, :, pl.ds(at, 256)] = matmul_nt(d_up[s], w).astype(BF).reshape(2, TOK, 256)
+            return carry
+
+        lax.fori_loop(0, 4, normed_two_grad, 0)
+
+    def in_grad_for(base, first):
+        def in_grad(i, carry):
+            lhs = n2[:, :, :, pl.ds(pl.multiple_of(i * 256, 256), 256)].reshape(512, 256)
+            for j in range(HID // 256):
+                at = base + j * 256
+                rhs = d_up[:, :, pl.ds(at, 256)].reshape(512, 256)
+                gi[i, :, :, :, :, pl.ds(at, 256)] = (
+                    matmul_tn(lhs, rhs).astype(BF).reshape(2, 2, 2, 32, 256)
+                )
+            return carry
+
+        lax.fori_loop(first, first + 2, in_grad, 0)
 
     def down(i, carry):
         w = wd[...].reshape(HID, WIDTH)
         ps[2, i] = dot_nn(hidden[i], w).astype(BF).reshape(2, TOK, WIDTH)
         return carry
-
-    lax.fori_loop(0, 2, down, 0)
-    share_db.forward()
-    r_d.third(1)
-    r_i.second(1)
-    red_out = Reduce(2)
-    share_db.done()
 
     def attended_grad(s, carry):
         rows = db[s].reshape(256, WIDTH)
@@ -1176,18 +1096,6 @@
         datt[s, 0] = da[:, 0:128]
         datt[s, 1] = da[:, 128:256]
         return carry
-
-    lax.fori_loop(0, 2, attended_grad, 0)
-
-    lhs = att
-    for j in range(2):
-        for half in range(2):
-            rhs = db[:, :, :, pl.ds(half * 512, 512)].reshape(512, 512)
-            go[j, :, :, :, pl.ds(half * 512, 512)] = (
-                matmul_tn(lhs[:, j].reshape(512, 128), rhs).astype(BF).reshape(2, 2, 32, 512)
-            )
-    r_o = ScatterOut(go, WIDTH, ro1, ro2, ro3)
-    r_o.first()
 
     def attend_back(i, carry):
         s, j = i // 2, lax.rem(i, 2)
@@ -1209,10 +1117,16 @@
             dqkv[part, j, s] = u.astype(BF)
         return carry
 
-    r_d.second(0)
-    red_out.cross()
-    lax.fori_loop(0, 4, attend_back, 0)
-    r_i.third(1)
+    def first_grads_for(s):
+        rows = jnp.concatenate([dqkv[p, j, s] for p in range(3) for j in range(2)], axis=1)
+
+        def first_grads(i, carry):
+            w = wq[i].reshape(256, QKV)
+            at = pl.multiple_of(i * 256, 256)
+            ps[3, s, :, :, pl.ds(at, 256)] = matmul_nt(rows, w).astype(BF).reshape(2, TOK, 256)
+            return carry
+
+        lax.fori_loop(0, 4, first_grads, 0)
 
     def qkv_grad(i, carry):
         lhs = n1[:, :, :, pl.ds(pl.multiple_of(i * 256, 256), 256)].reshape(512, 256)
@@ -1224,34 +1138,170 @@
                 )
         return carry
 
+    pl.semaphore_wait(barrier, 6)
+    on["s_q"] = spread(wq_in, wq)
+    wide[0:256] = wo_flat[...].astype(F32)
+    for j in range(8):
+        wo_in[:, pl.ds(j * 128, 128)] = wide[pl.ds(j, 32, stride=8), :].astype(BF)
+    on["seg"] = [go_copy(seg_buf.at[zp, c], seg_buf.at[zp, c], dev) for dev, _ in others]
+    g_o.start()
+    g_o.across()
+    in_rows = 2 * FF // TOK
+    lines[...] = wi_flat[...].astype(F32)
+    gain = column(gain2_in)
+    for j in range(in_rows):
+        wide[pl.ds(j * 32, 32), :] = lines[pl.ds(j, 32, stride=in_rows), :] * gain
+    for r in range(4):
+        for u in range(2 * HID // TOK):
+            tile = moved(in_moves(r, u), lambda t: wide[pl.ds(t * 32, 32), :])
+            wi_in[r, :, pl.ds(u * 128, 128)] = tile.astype(BF)
+    wi[z, y, x, c] = wi_in[role]
+    on["s_i"] = spread(wi_in, wi)
+    g_d.own_first()
+    g_d.own_second()
+    for cp in on["s_q"]:
+        cp.wait_recv()
+    g_q.across()
+    g_q.own_first()
+    on["n1"] = Share(n1)
+    g_d.across()
+    for cp in on["seg"]:
+        cp.wait_recv()
+    g_o.first()
+    g_q.own_second()
+    g_o.second()
+    g_q.far_first()
+    for cp in on["s_i"]:
+        cp.wait_recv()
+    g_i.own_first()
+    g_i.across()
+    g_q.far_second()
+    on["cot"] = Share(cot)
+    g_o.done()
+    g_i.own_second()
+    on["n1"].forward()
+    g_j.own_first()
+    on["n1"].done()
+    on["n1"].core()
+    g_q.done()
+    lax.fori_loop(1 - zp, 2 - zp, qkv_step, 0)
+    lax.fori_loop(zp, zp + 1, qkv_step, 0)
+    g_d.far_first()
+    g_j.across()
+    lax.fori_loop(2 * zp, 2 * zp + 2, attend, 0)
+    on["cot"].core()
+    g_i.far_first()
+    lax.fori_loop(2 * (1 - zp), 2 * (1 - zp) + 2, attend, 0)
+    lax.fori_loop(1 - zp, 2 - zp, branch, 0)
+    red[0].far_terms()
+    red[0].cross()
+    g_j.own_second()
+    on["cot"].forward()
+    g_i.far_second()
+    lax.fori_loop(zp, zp + 1, branch, 0)
+    red[0].near_terms()
+    g_j.far_first()
+    mid = x_ref[...].astype(F32) + red[0].total()
+    middle[...] = mid
+    centred = mid - jnp.mean(mid, axis=-1, keepdims=True)
+    inv = lax.rsqrt(jnp.mean(centred * centred, axis=-1, keepdims=True) + EPSILON)
+    unit = centred * inv
+    unit2[...] = unit
+    inv2[...] = jnp.broadcast_to(inv, (TOK, 128))
+    n2[zp, c] = unit.astype(BF)
+    on["n2"] = Share(n2)
+    g_j.far_second()
+    g_d.far_second()
+    g_i.done()
+    on["n2"].forward()
+    g_j.done()
+    on["n2"].core()
+    on["mark"] = len(sent)
+    upper_for(zp)
+    on["cot"].done()
+    on["n2"].done()
+    upper_for(1 - zp)
+    lax.fori_loop(0, 2, down_grad, 0)
+    g_d.done()
+    r_d.first(1)
+    lax.fori_loop(0, 2, hidden_grad, 0)
+    normed_two_grad_for(1 - zp)
+    red[1].far_terms()
+    in_grad_for(HID, 2 * (1 - zh))
+    r_j.first(1)
+    red[1].cross()
+    in_grad_for(0, 2 * (1 - zh))
+    r_i.first(1)
+    normed_two_grad_for(zp)
+    red[1].near_terms()
+    in_grad_for(HID, 2 * zh)
+    r_j.second(1)
+    r_d.first(0)
+    settle(on["mark"])
+    e = red[1].total()
+    n = unit2[...]
+    d_middle = cot_in[...].astype(F32) + inv2[:, 0:1] * (
+        e
+        - jnp.mean(e, axis=-1, keepdims=True)
+        - n * jnp.mean(e * n, axis=-1, keepdims=True)
+    )
+    dmid[...] = d_middle
+    db[zp, c] = d_middle.astype(BF)
+    on["db"] = Share(db)
+    r_d.second(1)
+    lax.fori_loop(1 - zp, 2 - zp, down, 0)
+    red[2].far_terms()
+    r_j.third(1)
+    in_grad_for(0, 2 * zh)
+    r_j.first(0)
+    on["db"].forward()
+    on["db"].core()
+    r_i.second(1)
+    lax.fori_loop(zp, zp + 1, attended_grad, 0)
+    r_d.second(0)
+    red[2].cross()
+    lax.fori_loop(2 * zp, 2 * zp + 2, attend_back, 0)
+    r_i.first(0)
+    on["db"].done()
+    r_d.third(1)
+    lax.fori_loop(1 - zp, 2 - zp, attended_grad, 0)
+    lhs = att
+    for j in range(2):
+        for half in range(2):
+            rhs = db[:, :, :, pl.ds(half * 512, 512)].reshape(512, 512)
+            go[j, :, :, :, pl.ds(half * 512, 512)] = (
+                matmul_tn(lhs[:, j].reshape(512, 128), rhs).astype(BF).reshape(2, 2, 32, 512)
+            )
+    lax.fori_loop(zp, zp + 1, down, 0)
+    red[2].near_terms()
+    r_o.first()
+    lax.fori_loop(2 * (1 - zp), 2 * (1 - zp) + 2, attend_back, 0)
+    lax.fori_loop(2 * zh, 2 * zh + 2, qkv_grad, 0)
     lax.fori_loop(2 * (1 - zh), 2 * (1 - zh) + 2, qkv_grad, 0)
-    r_q = ScatterRows(gq, QKV, rq1, rq2, rq3)
     r_q.first(1)
-    lax.fori_loop(2 * zh, 2 * zh + 2, qkv_grad, 0)
-
-    def first_grads(i, carry):
-        w = wq[i].reshape(256, QKV)
-        at = pl.multiple_of(i * 256, 256)
-        for s in range(2):
-            rows = jnp.concatenate([dqkv[p, j, s] for p in range(3) for j in range(2)], axis=1)
-            ps[3, s, :, :, pl.ds(at, 256)] = (
-                matmul_nt(rows, w).astype(BF).reshape(2, TOK, 256)
-            )
-        return carry
-
-    lax.fori_loop(0, 4, first_grads, 0)
-    red_in = Reduce(3)
-
+    first_grads_for(1 - zp)
+    red[3].far_terms()
+    out_vm[...] = (middle[...] + red[2].total()).astype(BF)
+    emit(0, out_vm, out_ref)
+    r_i.third(1)
+    r_i.second(0)
+    red[3].cross()
+    first_grads_for(zp)
+    red[3].near_terms()
+    r_o.second()
     r_q.second(1)
-    r_i.first(0)
-    red_in.cross()
-    r_o.second()
+    r_d.third(0)
+    r_i.third(0)
+    r_o.third()
+    r_q.first(0)
+    r_i.fourth(gi_vm)
+    r_j.second(0)
     r_q.third(1)
-    r_q.first(0)
-    r_d.third(0)
     r_d.fourth(gd_vm)
     emit(2, gd_vm, gd_ref)
-    e = red_in.total()
+    r_o.fourth(go_vm)
+    r_q.second(0)
+    e = red[3].total()
     n = unit1[...]
     ig_vm[...] = dmid[...] + inv1[:, 0:1] * (
         e
@@ -1259,25 +1309,21 @@
         - n * jnp.mean(e * n, axis=-1, keepdims=True)
     )
     emit(1, ig_vm, ig_ref)
-    out_vm[...] = (middle[...] + red_out.total()).astype(BF)
-    emit(0, out_vm, out_ref)
-    r_i.second(0)
-    r_q.second(0)
-    r_o.third()
-    settle()
-    r_i.third(0)
-    r_i.fourth(gi_vm)
-    r_o.fourth(go_vm)
+    r_j.third(0)
+    r_i.done()
+    emit(3, gi_vm.at[:, :, pl.ds(0, HID)], gi_ref.at[:, :, pl.ds(0, HID)])
+    r_j.fourth(gi_vm)
     r_q.third(0)
     r_q.fourth(gq_vm)
-    r_i.done()
-    emit(3, gi_vm, gi_ref)
+    r_j.done()
+    emit(6, gi_vm.at[:, :, pl.ds(HID, HID)], gi_ref.at[:, :, pl.ds(HID, HID)])
     r_o.done()
     emit(4, go_vm, go_ref)
     r_q.done()
     emit(5, gq_vm, gq_ref)
     g_o.end()
-    settle()
+    assert n_sems[0] == N_COPIES
+    settle(len(sent))
     for cp in local:
         cp.wait()
 
@@ -1297,7 +1343,7 @@
     group = (2, 2, TOK, WIDTH)
     rows = (4, 2, 2, 2, 32)
     outs = pl.pallas_call(
-        functools.partial(layer_kernel, [0]),
+        layer_kernel,
         out_shape=(
             jax.ShapeDtypeStruct((TOK, WIDTH), BF),
             jax.ShapeDtypeStruct((TOK, WIDTH), F32),
@@ -1349,9 +1395,9 @@
             vm((2, 2, 2, 32, WIDTH // 2), BF),
             vm((2, 2, 32, WIDTH // 2), BF),
             vm((2, 32, WIDTH), BF),
-            vm((2, 2, 2, 2, 2, 32, HID), BF),
-            vm((2, 2, 2, 2, 32, HID), BF),
-            vm((2, 2, 32, 2 * HID), BF),
+            vm((2, 2, 2, 2, 2, 2, 32, HID // 2), BF),
+            vm((2, 2, 2, 2, 2, 32, HID // 2), BF),
+            vm((2, 2, 2, 32, HID), BF),
             vm((2, 2, 1, 2, PAD, WIDTH // 2), BF),
             vm((2, 2, 1, PAD, WIDTH // 2), BF),
             vm((1, PAD, WIDTH), BF),
@@ -1366,9 +1412,9 @@
             vm((32, WIDTH), BF),
             vm((4, 32, 2 * HID), BF),
             vm((PAD, WIDTH), F32),
+            pltpu.SemaphoreType.DMA((N_SENDS,)),
             pltpu.SemaphoreType.DMA((N_COPIES,)),
-            pltpu.SemaphoreType.DMA((N_COPIES,)),
-            pltpu.SemaphoreType.DMA((6,)),
+            pltpu.SemaphoreType.DMA((7,)),
         ],
         compiler_params=pltpu.CompilerParams(
             collective_id=0, has_side_effects=True, vmem_limit_bytes=60 * 2**20
@@ -1426,7 +1472,8 @@
     return (final[0][None], final[1][None]) + tuple(f.reshape(-1) for f in final[2:])
 
 
-N_COPIES = 116
+N_COPIES = 142
+N_SENDS = 100
 PIECES = 2
 
 

time: 144 us -> 140 us (0.972)
  Pallas kernels: 143 us -> 138 us
    pallas_call x1, Pallas kernels: 139 us -> 134 us  [block_device(): pl.pallas_call(layer_kernel, out_shape=(jax.ShapeDtypeStruct((TOK, WIDTH)...]
where the time goes in v3:
time: 140 us; the launch traced here: 139 us
  Pallas kernels  138 us (99%)
    pallas_call x1, Pallas kernels, block_device(): pl.pallas_call(layer_kernel, out_shape=(jax.ShapeDtypeStruct((TOK, WIDTH)...  134 us
    pallas_call x1, Pallas kernels, block_device(): pl.pallas_call(finish_kernel, out_shape=(jax.ShapeDtypeStruct((TOK, WIDTH...  4.37 us

profile of v3, /device:TPU:0, one launch (start us, length us, event | category | flops | bytes accessed | tf_op | source)
XLA Modules:
  0.0 139.2 jit_solution(13767771490770862855)
XLA Ops:
  0.6 134.0 %shard_map.170 = (bf16[128,1024]{1,0:T(8,128)(2,1)}, f32[128,1024]{1,0:T(8,128)}, bf16[4,32,768]{2,1,0:T(8,128)(2,1)}, bf16[32,1024]{1,0:T(8,128)(2,1)}, bf16[4,...) custom-call(bf16[128,1024]{1,0:T(8,128)(2,1)} %bitcast.20, bf16[128,1024]{1,0:T(8,128)(2,1)} %bitcast.21, s32[1,128]{1,0:T(1,128)} %seg_in.1, ...), custom_call_target="tpu_custom_call" | custom-call | tf_op jit(solution)/shard_map/pallas_call | solution.py:1345
  134.7 4.4 %shard_map.171 = (bf16[128,1024]{1,0:T(8,128)(2,1)}, f32[128,1024]{1,0:T(8,128)}, f32[1,32]{1,0:T(1,128)}, f32[768,128]{1,0:T(8,128)}, f32[256,128]{1,0:T(8,128)...) custom-call(bf16[4,32,768]{2,1,0:T(8,128)(2,1)} %get-tuple-element.22.gq_in, ...), custom_call_target="tpu_custom_call" | custom-call | tf_op jit(solution)/shard_map/pallas_call | solution.py:1436

commit v4 on v3

--- a/solution.py
+++ b/solution.py
@@ -351,7 +351,7 @@
 
 
 def owner(r, k):
-    return k // 4 * 16 + r // 2 * 8 + k // 2 % 2 * 4 + k % 2 * 2 + r % 2
+    return k // 4 * 16 + (r // 2 + k // 4) % 2 * 8 + k // 2 % 2 * 4 + k % 2 * 2 + r % 2
 
 
 def runs(places):
@@ -408,9 +408,8 @@
     out_in,
     ig_in,
     gain1_in,
-    gain2_in,
+    sums_in,
     wq_flat,
-    wi_flat,
     out_ref,
     ig_ref,
     gain1_ref,
@@ -425,10 +424,8 @@
     gi_raw,
     gd_raw,
     wq_raw,
-    wi_raw,
     gq_own,
     go_own,
-    gi_own,
     gd_own,
     ig_raw,
     out_raw,
@@ -442,10 +439,9 @@
         cp.start()
         return cp
 
-    gi_here = start(gi_in, gi_raw)
-    wi_here = start(wi_flat, wi_raw)
     gq_here = start(gq_in, gq_raw)
     wq_here = start(wq_flat, wq_raw)
+    gi_here = start(gi_in, gi_raw)
     gd_here = start(gd_in, gd_raw)
     go_here = start(go_in, go_raw)
     ig_here = start(ig_in, ig_raw)
@@ -459,26 +455,17 @@
         return jnp.sum(jnp.where(rows == cols, total, 0.0), axis=0, keepdims=True)
 
     qkv_rows = 3 * WIDTH // TOK
-    in_rows = 2 * FF // TOK
-    gain = column(gain2_in)
-    total = jnp.zeros((32, 128), F32)
-    wi_here.wait()
-    lines[...] = wi_raw[...].astype(F32)
     ig_here.wait()
     written.append(start(ig_raw, ig_ref))
     out_here.wait()
     written.append(start(out_raw, out_ref))
+    gi_here.wait()
+    written.append(start(gi_raw, gi_ref))
+    gain2_ref[...] = line(sums_in[...])
     gd_here.wait()
     for j in range(8):
         gd_own[pl.ds(j, PART, stride=8), :] = gd_raw[0:PART, pl.ds(j * 128, 128)]
     written.append(start(gd_own, gd_ref))
-    gi_here.wait()
-    for j in range(in_rows):
-        g = moved(out_moves(j), lambda t: gi_raw[t[0], :, pl.ds(t[1] * 128, 128)].astype(F32))
-        total = total + g * lines[pl.ds(j, 32, stride=in_rows), :]
-        gi_own[pl.ds(j, 32, stride=in_rows), :] = g * gain
-    written.append(start(gi_own, gi_ref))
-    gain2_ref[...] = line(total)
     gain = column(gain1_in)
     total = jnp.zeros((32, 128), F32)
     wq_here.wait()
@@ -486,7 +473,7 @@
     gq_here.wait()
     for j in range(qkv_rows):
         part, cut = divmod(j, 8)
-        r = (cut // 2 % 2) * 2 + cut // 4
+        r = (cut // 2 + cut // 4) % 2 * 2 + cut // 4
         g = gq_raw[r, :, pl.ds(part * 256 + cut % 2 * 128, 128)].astype(F32)
         total = total + g * lines[pl.ds(j, 32, stride=qkv_rows), :]
         gq_own[pl.ds(j, 32, stride=qkv_rows), :] = g * gain
@@ -518,6 +505,7 @@
     go_ref,
     gi_ref,
     gd_ref,
+    sums_ref,
     seg_buf,
     n1,
     n2,
@@ -575,6 +563,8 @@
     go_vm,
     gi_vm,
     gd_vm,
+    gi_own,
+    sums,
     send_sems,
     recv_sems,
     local_sems,
@@ -582,7 +572,8 @@
     dp, c = lax.axis_index("dp"), lax.axis_index("seq")
     x, y, z = lax.rem(dp, 2), lax.rem(dp // 2, 2), dp // 4
     zh, zp = z // 2, lax.rem(z, 2)
-    role = zp * 2 + c
+    kind = lax.rem(zp + zh, 2)
+    role = kind * 2 + c
 
     def device(X, Y, Z, C):
         return (Z * 4 + Y * 2 + X, C)
@@ -590,7 +581,7 @@
     core_dev = device(x, y, z, 1 - c)
     pair_dev = device(x, y, zh * 2 + 1 - zp, c)
     diag_dev = device(x, y, zh * 2 + 1 - zp, 1 - c)
-    half_dev = device(x, y, (1 - zh) * 2 + zp, c)
+    half_dev = device(x, y, 3 - z, c)
     x_dev = device(1 - x, y, z, c)
     y_dev = device(x, 1 - y, z, c)
 
@@ -637,13 +628,13 @@
 
 
     others = (
-        (core_dev, zp * 2 + 1 - c),
-        (pair_dev, (1 - zp) * 2 + c),
-        (diag_dev, (1 - zp) * 2 + 1 - c),
+        (core_dev, kind * 2 + 1 - c, (z, 1 - c)),
+        (pair_dev, (1 - kind) * 2 + c, (zh * 2 + 1 - zp, c)),
+        (diag_dev, (1 - kind) * 2 + 1 - c, (zh * 2 + 1 - zp, 1 - c)),
     )
 
     def spread(own, buf):
-        cps = [go_copy(own.at[r], buf.at[z, y, x, c], dev) for dev, r in others]
+        cps = [go_copy(own.at[r], buf.at[z, y, x, c], dev) for dev, r, _ in others]
         return cps
 
     class Gather:
@@ -872,8 +863,8 @@
             cols = self.cols
             add_all(self.buf.at[self.of(zh), y, x, :, :, cols], self.r3)
             self.c4 = []
-            for dev, r in others:
-                src = self.buf.at[2 * zh + r // 2, y, x, lax.rem(r, 2), :, cols]
+            for dev, _, (there, core) in others:
+                src = self.buf.at[there, y, x, core, :, cols]
                 self.c4.append(go_copy(src, out.at[role, :, cols], dev))
             out[role, :, cols] = self.buf[z, y, x, c, :, cols]
 
@@ -944,30 +935,15 @@
             def _():
                 self.c4.wait_send()
 
-    tokens = x_ref[...].astype(F32)
-    centred = tokens - jnp.mean(tokens, axis=-1, keepdims=True)
-    inv = lax.rsqrt(jnp.mean(centred * centred, axis=-1, keepdims=True) + EPSILON)
-    unit = centred * inv
-    unit1[...] = unit
-    inv1[...] = jnp.broadcast_to(inv, (TOK, 128))
-    n1[zp, c] = unit.astype(BF)
     qkv_rows = 3 * WIDTH // TOK
     lines[0 : 32 * qkv_rows] = wq_flat[...].astype(F32)
     gain = column(gain1_in)
     for j in range(qkv_rows):
         part, cut = divmod(j, 8)
-        r = (cut // 2 % 2) * 2 + cut // 4
+        r = (cut // 2 + cut // 4) % 2 * 2 + cut // 4
         w = lines[pl.ds(j, 32, stride=qkv_rows), :] * gain
         wq_in[r, :, pl.ds(part * 256 + cut % 2 * 128, 128)] = w.astype(BF)
-    seg_buf[zp, c] = jnp.broadcast_to(seg_in[...].astype(F32), (8, TOK))
     wq[z, y, x, c] = wq_in[role]
-    cot[zp, c] = cot_in[...]
-    lines2 = wide
-    lines2[0 : 8 * PART] = wd_flat[...].astype(F32)
-    lines2[8 * PART : 8 * PAD] = jnp.zeros((8 * (PAD - PART), TOK), F32)
-    for j in range(8):
-        wd[zh, y, x, :, pl.ds(j * 128, 128)] = lines2[pl.ds(j, PAD, stride=8), :].astype(BF)
-
     g_q, g_d = Gather(wq, QKV), Gather(wd, WIDTH)
     g_i, g_j = Gather(wi, HID), Gather(wi, HID, HID)
     g_o = GatherOut(wo, WIDTH)
@@ -1140,10 +1116,24 @@
 
     pl.semaphore_wait(barrier, 6)
     on["s_q"] = spread(wq_in, wq)
+    wide[0 : 8 * PART] = wd_flat[...].astype(F32)
+    wide[8 * PART : 8 * PAD] = jnp.zeros((8 * (PAD - PART), TOK), F32)
+    for j in range(8):
+        wd[zh, y, x, :, pl.ds(j * 128, 128)] = wide[pl.ds(j, PAD, stride=8), :].astype(BF)
+    g_d.own_first()
+    tokens = x_ref[...].astype(F32)
+    centred = tokens - jnp.mean(tokens, axis=-1, keepdims=True)
+    inv = lax.rsqrt(jnp.mean(centred * centred, axis=-1, keepdims=True) + EPSILON)
+    unit = centred * inv
+    unit1[...] = unit
+    inv1[...] = jnp.broadcast_to(inv, (TOK, 128))
+    n1[zp, c] = unit.astype(BF)
+    seg_buf[zp, c] = jnp.broadcast_to(seg_in[...].astype(F32), (8, TOK))
+    cot[zp, c] = cot_in[...]
     wide[0:256] = wo_flat[...].astype(F32)
     for j in range(8):
         wo_in[:, pl.ds(j * 128, 128)] = wide[pl.ds(j, 32, stride=8), :].astype(BF)
-    on["seg"] = [go_copy(seg_buf.at[zp, c], seg_buf.at[zp, c], dev) for dev, _ in others]
+    on["seg"] = [go_copy(seg_buf.at[zp, c], seg_buf.at[zp, c], dev) for dev, _, _ in others]
     g_o.start()
     g_o.across()
     in_rows = 2 * FF // TOK
@@ -1157,50 +1147,48 @@
             wi_in[r, :, pl.ds(u * 128, 128)] = tile.astype(BF)
     wi[z, y, x, c] = wi_in[role]
     on["s_i"] = spread(wi_in, wi)
-    g_d.own_first()
     g_d.own_second()
     for cp in on["s_q"]:
         cp.wait_recv()
+    g_q.own_first()
     g_q.across()
-    g_q.own_first()
     on["n1"] = Share(n1)
-    g_d.across()
     for cp in on["seg"]:
         cp.wait_recv()
+    g_d.across()
     g_o.first()
     g_q.own_second()
     g_o.second()
-    g_q.far_first()
     for cp in on["s_i"]:
         cp.wait_recv()
+    g_q.far_first()
+    g_i.across()
+    g_o.done()
+    on["cot"] = Share(cot)
     g_i.own_first()
-    g_i.across()
     g_q.far_second()
-    on["cot"] = Share(cot)
-    g_o.done()
+    g_j.own_first()
+    on["n1"].forward()
     g_i.own_second()
-    on["n1"].forward()
-    g_j.own_first()
     on["n1"].done()
     on["n1"].core()
     g_q.done()
     lax.fori_loop(1 - zp, 2 - zp, qkv_step, 0)
     lax.fori_loop(zp, zp + 1, qkv_step, 0)
+    g_j.own_second()
+    g_j.across()
+    g_i.far_first()
     g_d.far_first()
-    g_j.across()
+    lax.fori_loop(2 * (1 - zp), 2 * (1 - zp) + 2, attend, 0)
+    on["cot"].core()
     lax.fori_loop(2 * zp, 2 * zp + 2, attend, 0)
-    on["cot"].core()
-    g_i.far_first()
-    lax.fori_loop(2 * (1 - zp), 2 * (1 - zp) + 2, attend, 0)
     lax.fori_loop(1 - zp, 2 - zp, branch, 0)
     red[0].far_terms()
     red[0].cross()
-    g_j.own_second()
-    on["cot"].forward()
+    g_j.far_first()
     g_i.far_second()
     lax.fori_loop(zp, zp + 1, branch, 0)
     red[0].near_terms()
-    g_j.far_first()
     mid = x_ref[...].astype(F32) + red[0].total()
     middle[...] = mid
     centred = mid - jnp.mean(mid, axis=-1, keepdims=True)
@@ -1210,15 +1198,16 @@
     inv2[...] = jnp.broadcast_to(inv, (TOK, 128))
     n2[zp, c] = unit.astype(BF)
     on["n2"] = Share(n2)
+    on["cot"].forward()
     g_j.far_second()
+    on["cot"].done()
+    on["n2"].core()
+    g_i.done()
     g_d.far_second()
-    g_i.done()
     on["n2"].forward()
     g_j.done()
-    on["n2"].core()
     on["mark"] = len(sent)
     upper_for(zp)
-    on["cot"].done()
     on["n2"].done()
     upper_for(1 - zp)
     lax.fori_loop(0, 2, down_grad, 0)
@@ -1234,9 +1223,11 @@
     r_i.first(1)
     normed_two_grad_for(zp)
     red[1].near_terms()
-    in_grad_for(HID, 2 * zh)
+    lax.fori_loop(1 - zp, 2 - zp, down, 0)
+    red[2].far_terms()
     r_j.second(1)
     r_d.first(0)
+    r_d.second(1)
     settle(on["mark"])
     e = red[1].total()
     n = unit2[...]
@@ -1248,23 +1239,23 @@
     dmid[...] = d_middle
     db[zp, c] = d_middle.astype(BF)
     on["db"] = Share(db)
-    r_d.second(1)
-    lax.fori_loop(1 - zp, 2 - zp, down, 0)
-    red[2].far_terms()
     r_j.third(1)
+    in_grad_for(HID, 2 * zh)
+    r_d.second(0)
+    r_i.second(1)
+    red[2].cross()
+    on["db"].forward()
+    r_j.first(0)
     in_grad_for(0, 2 * zh)
-    r_j.first(0)
-    on["db"].forward()
-    on["db"].core()
-    r_i.second(1)
-    lax.fori_loop(zp, zp + 1, attended_grad, 0)
-    r_d.second(0)
-    red[2].cross()
-    lax.fori_loop(2 * zp, 2 * zp + 2, attend_back, 0)
-    r_i.first(0)
     on["db"].done()
     r_d.third(1)
+    r_i.first(0)
+    on["db"].core()
+    lax.fori_loop(zp, zp + 1, attended_grad, 0)
     lax.fori_loop(1 - zp, 2 - zp, attended_grad, 0)
+    lax.fori_loop(2 * (1 - zp), 2 * (1 - zp) + 2, attend_back, 0)
+    first_grads_for(1 - zp)
+    red[3].far_terms()
     lhs = att
     for j in range(2):
         for half in range(2):
@@ -1272,35 +1263,31 @@
             go[j, :, :, :, pl.ds(half * 512, 512)] = (
                 matmul_tn(lhs[:, j].reshape(512, 128), rhs).astype(BF).reshape(2, 2, 32, 512)
             )
+    r_i.third(1)
+    lax.fori_loop(2 * zp, 2 * zp + 2, attend_back, 0)
+    lax.fori_loop(2 * zh, 2 * zh + 2, qkv_grad, 0)
+    r_o.first()
+    r_d.third(0)
+    red[3].cross()
+    lax.fori_loop(2 * (1 - zh), 2 * (1 - zh) + 2, qkv_grad, 0)
+    r_q.first(1)
     lax.fori_loop(zp, zp + 1, down, 0)
     red[2].near_terms()
-    r_o.first()
-    lax.fori_loop(2 * (1 - zp), 2 * (1 - zp) + 2, attend_back, 0)
-    lax.fori_loop(2 * zh, 2 * zh + 2, qkv_grad, 0)
-    lax.fori_loop(2 * (1 - zh), 2 * (1 - zh) + 2, qkv_grad, 0)
-    r_q.first(1)
-    first_grads_for(1 - zp)
-    red[3].far_terms()
-    out_vm[...] = (middle[...] + red[2].total()).astype(BF)
-    emit(0, out_vm, out_ref)
-    r_i.third(1)
+    r_o.second()
     r_i.second(0)
-    red[3].cross()
+    r_q.second(1)
+    r_d.fourth(gd_vm)
+    emit(2, gd_vm, gd_ref)
+    r_o.third()
     first_grads_for(zp)
     red[3].near_terms()
-    r_o.second()
-    r_q.second(1)
-    r_d.third(0)
     r_i.third(0)
-    r_o.third()
     r_q.first(0)
+    r_j.second(0)
     r_i.fourth(gi_vm)
-    r_j.second(0)
     r_q.third(1)
-    r_d.fourth(gd_vm)
-    emit(2, gd_vm, gd_ref)
-    r_o.fourth(go_vm)
     r_q.second(0)
+    r_j.third(0)
     e = red[3].total()
     n = unit1[...]
     ig_vm[...] = dmid[...] + inv1[:, 0:1] * (
@@ -1309,18 +1296,29 @@
         - n * jnp.mean(e * n, axis=-1, keepdims=True)
     )
     emit(1, ig_vm, ig_ref)
-    r_j.third(0)
+    out_vm[...] = (middle[...] + red[2].total()).astype(BF)
+    emit(0, out_vm, out_ref)
+    r_o.fourth(go_vm)
+    r_j.fourth(gi_vm)
     r_i.done()
-    emit(3, gi_vm.at[:, :, pl.ds(0, HID)], gi_ref.at[:, :, pl.ds(0, HID)])
-    r_j.fourth(gi_vm)
     r_q.third(0)
-    r_q.fourth(gq_vm)
-    r_j.done()
-    emit(6, gi_vm.at[:, :, pl.ds(HID, HID)], gi_ref.at[:, :, pl.ds(HID, HID)])
     r_o.done()
     emit(4, go_vm, go_ref)
+    r_q.fourth(gq_vm)
     r_q.done()
     emit(5, gq_vm, gq_ref)
+    r_j.done()
+    in_rows = 2 * FF // TOK
+    lines[...] = wi_flat[...].astype(F32)
+    gain = column(gain2_in)
+    total = jnp.zeros((32, 128), F32)
+    for j in range(in_rows):
+        g = moved(out_moves(j), lambda t: gi_vm[t[0], :, pl.ds(t[1] * 128, 128)].astype(F32))
+        total = total + g * lines[pl.ds(j, 32, stride=in_rows), :]
+        gi_own[pl.ds(j, 32, stride=in_rows), :] = g * gain
+    sums[...] = total
+    emit(3, gi_own, gi_ref)
+    emit(6, sums, sums_ref)
     g_o.end()
     assert n_sems[0] == N_COPIES
     settle(len(sent))
@@ -1349,11 +1347,12 @@
             jax.ShapeDtypeStruct((TOK, WIDTH), F32),
             jax.ShapeDtypeStruct((4, 32, QKV), BF),
             jax.ShapeDtypeStruct((32, WIDTH), BF),
-            jax.ShapeDtypeStruct((4, 32, 2 * HID), BF),
+            jax.ShapeDtypeStruct(wi_flat.shape, F32),
             jax.ShapeDtypeStruct((PAD, WIDTH), F32),
+            jax.ShapeDtypeStruct((32, TOK), F32),
         ),
         in_specs=[pl.BlockSpec(memory_space=vm)] * 11,
-        out_specs=(pl.BlockSpec(memory_space=pl.ANY),) * 6,
+        out_specs=(pl.BlockSpec(memory_space=pl.ANY),) * 7,
         scratch_shapes=[
             vm((2, 2, 8, TOK), F32),
             vm(group, BF),
@@ -1412,6 +1411,8 @@
             vm((32, WIDTH), BF),
             vm((4, 32, 2 * HID), BF),
             vm((PAD, WIDTH), F32),
+            vm(wi_flat.shape, F32),
+            vm((32, TOK), F32),
             pltpu.SemaphoreType.DMA((N_SENDS,)),
             pltpu.SemaphoreType.DMA((N_COPIES,)),
             pltpu.SemaphoreType.DMA((7,)),
@@ -1432,7 +1433,7 @@
         wi_flat,
         wd_flat,
     )
-    output, input_grad, gq, go, gi, gd = outs
+    output, input_grad, gq, go, gi, gd, sums = outs
     final = pl.pallas_call(
         finish_kernel,
         out_shape=(
@@ -1447,28 +1448,26 @@
         ),
         in_specs=[pl.BlockSpec(memory_space=pl.ANY)] * 6
         + [pl.BlockSpec(memory_space=vm)] * 2
-        + [pl.BlockSpec(memory_space=pl.ANY)] * 2,
+        + [pl.BlockSpec(memory_space=pl.ANY)],
         out_specs=tuple(
             pl.BlockSpec(memory_space=vm if i in (2, 5) else pl.ANY) for i in range(8)
         ),
         scratch_shapes=[
-            vm(wi_flat.shape, F32),
+            vm(wq_flat.shape, F32),
             vm((4, 32, QKV), BF),
             vm((32, WIDTH), BF),
-            vm((4, 32, 2 * HID), BF),
+            vm(wi_flat.shape, F32),
             vm((PAD, WIDTH), F32),
             vm(wq_flat.shape, BF),
-            vm(wi_flat.shape, BF),
             vm(wq_flat.shape, F32),
             vm(wo_flat.shape, F32),
-            vm(wi_flat.shape, F32),
             vm(wd_flat.shape, F32),
             vm((TOK, WIDTH), F32),
             vm((TOK, WIDTH), BF),
             pltpu.SemaphoreType.DMA((14,)),
         ],
         compiler_params=pltpu.CompilerParams(vmem_limit_bytes=60 * 2**20),
-    )(gq, go, gi, gd, output, input_grad, gain_one, gain_two, wq_flat, wi_flat)
+    )(gq, go, gi, gd, output, input_grad, gain_one, sums, wq_flat)
     return (final[0][None], final[1][None]) + tuple(f.reshape(-1) for f in final[2:])
 
 

time: 140 us -> 135 us (0.964)
  Pallas kernels: 138 us -> 134 us
    pallas_call x1, Pallas kernels: 134 us -> 130 us  [block_device(): pl.pallas_call(layer_kernel, out_shape=(jax.ShapeDtypeStruct((TOK, WIDTH)...]
where the time goes in v4:
time: 135 us
  Pallas kernels  134 us (99%)
    pallas_call x1, Pallas kernels, block_device(): pl.pallas_call(layer_kernel, out_shape=(jax.ShapeDtypeStruct((TOK, WIDTH)...  130 us
    pallas_call x1, Pallas kernels, block_device(): pl.pallas_call(finish_kernel, out_shape=(jax.ShapeDtypeStruct((TOK, WIDTH...  4.33 us

profile of v4, /device:TPU:0, one launch (start us, length us, event | category | flops | bytes accessed | tf_op | source)
XLA Modules:
  0.0 135.1 jit_solution(10236353596047774567)
XLA Ops:
  0.6 130.0 %shard_map.170 = (bf16[128,1024]{1,0:T(8,128)(2,1)}, f32[128,1024]{1,0:T(8,128)}, bf16[4,32,768]{2,1,0:T(8,128)(2,1)}, bf16[32,1024]{1,0:T(8,128)(2,1)}, f32[131...) custom-call(bf16[128,1024]{1,0:T(8,128)(2,1)} %bitcast.19, bf16[128,1024]{1,0:T(8,128)(2,1)} %bitcast.20, ...), custom_call_target="tpu_custom_call" | custom-call | tf_op jit(solution)/shard_map/pallas_call | solution.py:1343
  130.6 4.3 %shard_map.171 = (bf16[128,1024]{1,0:T(8,128)(2,1)}, f32[128,1024]{1,0:T(8,128)}, f32[1,32]{1,0:T(1,128)}, f32[768,128]{1,0:T(8,128)}, f32[256,128]{1,0:T(8,128)...) custom-call(bf16[4,32,768]{2,1,0:T(8,128)(2,1)} %get-tuple-element.23.gq_in, ...), custom_call_target="tpu_custom_call" | custom-call | tf_op jit(solution)/shard_map/pallas_call | solution.py:1437

commit v5 on v4

--- a/solution.py
+++ b/solution.py
@@ -439,13 +439,13 @@
         cp.start()
         return cp
 
+    gi_here = start(gi_in, gi_raw)
+    ig_here = start(ig_in, ig_raw)
+    out_here = start(out_in, out_raw)
+    gd_here = start(gd_in, gd_raw)
     gq_here = start(gq_in, gq_raw)
     wq_here = start(wq_flat, wq_raw)
-    gi_here = start(gi_in, gi_raw)
-    gd_here = start(gd_in, gd_raw)
     go_here = start(go_in, go_raw)
-    ig_here = start(ig_in, ig_raw)
-    out_here = start(out_in, out_raw)
     written = []
     rows = lax.broadcasted_iota(jnp.int32, (32, 32), 0)
     cols = lax.broadcasted_iota(jnp.int32, (32, 32), 1)
@@ -455,12 +455,12 @@
         return jnp.sum(jnp.where(rows == cols, total, 0.0), axis=0, keepdims=True)
 
     qkv_rows = 3 * WIDTH // TOK
+    gi_here.wait()
+    written.append(start(gi_raw, gi_ref))
     ig_here.wait()
     written.append(start(ig_raw, ig_ref))
     out_here.wait()
     written.append(start(out_raw, out_ref))
-    gi_here.wait()
-    written.append(start(gi_raw, gi_ref))
     gain2_ref[...] = line(sums_in[...])
     gd_here.wait()
     for j in range(8):
@@ -1028,16 +1028,18 @@
             )
         return carry
 
-    def hidden_grad(i, carry):
-        w = wd[i].reshape(384, WIDTH)
-        at = pl.multiple_of(i * 384, 384)
-        for s in range(2):
+    def hidden_grad_for(s):
+        def hidden_grad(i, carry):
+            w = wd[i].reshape(384, WIDTH)
+            at = pl.multiple_of(i * 384, 384)
             dh = matmul_nt(cot[s].reshape(256, WIDTH), w)
             d_up[s, :, pl.ds(at, 384)] = (dh * up_a[s, :, pl.ds(at, 384)]).astype(BF)
             d_up[s, :, pl.ds(pl.multiple_of(HID + at, 384), 384)] = (
                 dh * up_b[s, :, pl.ds(at, 384)]
             ).astype(BF)
-        return carry
+            return carry
+
+        lax.fori_loop(0, 2, hidden_grad, 0)
 
     def normed_two_grad_for(s):
         def normed_two_grad(i, carry):
@@ -1120,22 +1122,11 @@
     wide[8 * PART : 8 * PAD] = jnp.zeros((8 * (PAD - PART), TOK), F32)
     for j in range(8):
         wd[zh, y, x, :, pl.ds(j * 128, 128)] = wide[pl.ds(j, PAD, stride=8), :].astype(BF)
-    g_d.own_first()
-    tokens = x_ref[...].astype(F32)
-    centred = tokens - jnp.mean(tokens, axis=-1, keepdims=True)
-    inv = lax.rsqrt(jnp.mean(centred * centred, axis=-1, keepdims=True) + EPSILON)
-    unit = centred * inv
-    unit1[...] = unit
-    inv1[...] = jnp.broadcast_to(inv, (TOK, 128))
-    n1[zp, c] = unit.astype(BF)
-    seg_buf[zp, c] = jnp.broadcast_to(seg_in[...].astype(F32), (8, TOK))
-    cot[zp, c] = cot_in[...]
     wide[0:256] = wo_flat[...].astype(F32)
     for j in range(8):
         wo_in[:, pl.ds(j * 128, 128)] = wide[pl.ds(j, 32, stride=8), :].astype(BF)
-    on["seg"] = [go_copy(seg_buf.at[zp, c], seg_buf.at[zp, c], dev) for dev, _, _ in others]
     g_o.start()
-    g_o.across()
+    g_d.own_first()
     in_rows = 2 * FF // TOK
     lines[...] = wi_flat[...].astype(F32)
     gain = column(gain2_in)
@@ -1146,49 +1137,63 @@
             tile = moved(in_moves(r, u), lambda t: wide[pl.ds(t * 32, 32), :])
             wi_in[r, :, pl.ds(u * 128, 128)] = tile.astype(BF)
     wi[z, y, x, c] = wi_in[role]
+    g_o.across()
     on["s_i"] = spread(wi_in, wi)
-    g_d.own_second()
+    tokens = x_ref[...].astype(F32)
+    centred = tokens - jnp.mean(tokens, axis=-1, keepdims=True)
+    inv = lax.rsqrt(jnp.mean(centred * centred, axis=-1, keepdims=True) + EPSILON)
+    unit = centred * inv
+    unit1[...] = unit
+    inv1[...] = jnp.broadcast_to(inv, (TOK, 128))
+    n1[zp, c] = unit.astype(BF)
+    seg_buf[zp, c] = jnp.broadcast_to(seg_in[...].astype(F32), (8, TOK))
+    cot[zp, c] = cot_in[...]
     for cp in on["s_q"]:
         cp.wait_recv()
+    g_q.across()
     g_q.own_first()
-    g_q.across()
     on["n1"] = Share(n1)
+    g_d.own_second()
+    g_o.first()
+    for cp in on["s_i"]:
+        cp.wait_recv()
+    on["seg"] = [go_copy(seg_buf.at[zp, c], seg_buf.at[zp, c], dev) for dev, _, _ in others]
+    g_q.own_second()
+    g_q.far_first()
+    g_o.second()
+    g_i.across()
+    on["cot"] = Share(cot)
+    g_q.far_second()
+    g_i.own_first()
+    g_j.own_first()
+    g_j.across()
+    on["n1"].forward()
+    g_q.done()
+    g_i.far_first()
+    on["n1"].core()
+    on["cot"].core()
     for cp in on["seg"]:
         cp.wait_recv()
-    g_d.across()
-    g_o.first()
-    g_q.own_second()
-    g_o.second()
-    for cp in on["s_i"]:
-        cp.wait_recv()
-    g_q.far_first()
-    g_i.across()
     g_o.done()
-    on["cot"] = Share(cot)
-    g_i.own_first()
-    g_q.far_second()
-    g_j.own_first()
-    on["n1"].forward()
-    g_i.own_second()
     on["n1"].done()
-    on["n1"].core()
-    g_q.done()
     lax.fori_loop(1 - zp, 2 - zp, qkv_step, 0)
-    lax.fori_loop(zp, zp + 1, qkv_step, 0)
-    g_j.own_second()
-    g_j.across()
-    g_i.far_first()
-    g_d.far_first()
     lax.fori_loop(2 * (1 - zp), 2 * (1 - zp) + 2, attend, 0)
-    on["cot"].core()
-    lax.fori_loop(2 * zp, 2 * zp + 2, attend, 0)
     lax.fori_loop(1 - zp, 2 - zp, branch, 0)
     red[0].far_terms()
+    g_i.own_second()
+    lax.fori_loop(zp, zp + 1, qkv_step, 0)
+    g_i.far_second()
     red[0].cross()
+    g_d.across()
+    lax.fori_loop(2 * zp, 2 * zp + 2, attend, 0)
+    on["cot"].forward()
     g_j.far_first()
-    g_i.far_second()
+    g_j.own_second()
     lax.fori_loop(zp, zp + 1, branch, 0)
     red[0].near_terms()
+    on["cot"].done()
+    g_d.far_first()
+    g_j.far_second()
     mid = x_ref[...].astype(F32) + red[0].total()
     middle[...] = mid
     centred = mid - jnp.mean(mid, axis=-1, keepdims=True)
@@ -1198,36 +1203,35 @@
     inv2[...] = jnp.broadcast_to(inv, (TOK, 128))
     n2[zp, c] = unit.astype(BF)
     on["n2"] = Share(n2)
-    on["cot"].forward()
-    g_j.far_second()
-    on["cot"].done()
+    g_i.done()
+    on["n2"].forward()
+    g_d.far_second()
+    g_j.done()
     on["n2"].core()
-    g_i.done()
-    g_d.far_second()
-    on["n2"].forward()
-    g_j.done()
+    on["n2"].done()
     on["mark"] = len(sent)
     upper_for(zp)
-    on["n2"].done()
     upper_for(1 - zp)
     lax.fori_loop(0, 2, down_grad, 0)
+    r_d.first(1)
     g_d.done()
-    r_d.first(1)
-    lax.fori_loop(0, 2, hidden_grad, 0)
+    hidden_grad_for(1 - zp)
+    hidden_grad_for(zp)
+    in_grad_for(HID, 2 * (1 - zh))
+    r_j.first(1)
     normed_two_grad_for(1 - zp)
     red[1].far_terms()
-    in_grad_for(HID, 2 * (1 - zh))
-    r_j.first(1)
     red[1].cross()
+    r_d.second(1)
     in_grad_for(0, 2 * (1 - zh))
     r_i.first(1)
     normed_two_grad_for(zp)
     red[1].near_terms()
+    lax.fori_loop(zp, zp + 1, down, 0)
+    red[2].near_terms()
+    r_j.second(1)
     lax.fori_loop(1 - zp, 2 - zp, down, 0)
     red[2].far_terms()
-    r_j.second(1)
-    r_d.first(0)
-    r_d.second(1)
     settle(on["mark"])
     e = red[1].total()
     n = unit2[...]
@@ -1239,23 +1243,30 @@
     dmid[...] = d_middle
     db[zp, c] = d_middle.astype(BF)
     on["db"] = Share(db)
-    r_j.third(1)
-    in_grad_for(HID, 2 * zh)
-    r_d.second(0)
-    r_i.second(1)
+    r_d.first(0)
     red[2].cross()
-    on["db"].forward()
-    r_j.first(0)
     in_grad_for(0, 2 * zh)
-    on["db"].done()
     r_d.third(1)
     r_i.first(0)
+    r_i.second(1)
     on["db"].core()
-    lax.fori_loop(zp, zp + 1, attended_grad, 0)
+    in_grad_for(HID, 2 * zh)
+    r_j.third(1)
+    r_j.first(0)
+    on["db"].forward()
+    on["db"].done()
     lax.fori_loop(1 - zp, 2 - zp, attended_grad, 0)
     lax.fori_loop(2 * (1 - zp), 2 * (1 - zp) + 2, attend_back, 0)
+    lax.fori_loop(zp, zp + 1, attended_grad, 0)
+    lax.fori_loop(2 * zp, 2 * zp + 2, attend_back, 0)
     first_grads_for(1 - zp)
     red[3].far_terms()
+    lax.fori_loop(2 * (1 - zh), 2 * (1 - zh) + 2, qkv_grad, 0)
+    r_q.first(1)
+    r_i.second(0)
+    out_vm[...] = (middle[...] + red[2].total()).astype(BF)
+    emit(0, out_vm, out_ref)
+    r_i.third(1)
     lhs = att
     for j in range(2):
         for half in range(2):
@@ -1263,31 +1274,23 @@
             go[j, :, :, :, pl.ds(half * 512, 512)] = (
                 matmul_tn(lhs[:, j].reshape(512, 128), rhs).astype(BF).reshape(2, 2, 32, 512)
             )
-    r_i.third(1)
-    lax.fori_loop(2 * zp, 2 * zp + 2, attend_back, 0)
+    red[3].cross()
     lax.fori_loop(2 * zh, 2 * zh + 2, qkv_grad, 0)
-    r_o.first()
-    r_d.third(0)
-    red[3].cross()
-    lax.fori_loop(2 * (1 - zh), 2 * (1 - zh) + 2, qkv_grad, 0)
-    r_q.first(1)
-    lax.fori_loop(zp, zp + 1, down, 0)
-    red[2].near_terms()
-    r_o.second()
-    r_i.second(0)
     r_q.second(1)
-    r_d.fourth(gd_vm)
-    emit(2, gd_vm, gd_ref)
-    r_o.third()
+    r_j.second(0)
+    r_i.third(0)
     first_grads_for(zp)
     red[3].near_terms()
-    r_i.third(0)
+    r_o.first()
+    r_q.third(1)
+    r_j.third(0)
     r_q.first(0)
-    r_j.second(0)
+    r_j.fourth(gi_vm)
+    r_o.second()
     r_i.fourth(gi_vm)
-    r_q.third(1)
     r_q.second(0)
-    r_j.third(0)
+    r_d.second(0)
+    r_o.third()
     e = red[3].total()
     n = unit1[...]
     ig_vm[...] = dmid[...] + inv1[:, 0:1] * (
@@ -1296,18 +1299,14 @@
         - n * jnp.mean(e * n, axis=-1, keepdims=True)
     )
     emit(1, ig_vm, ig_ref)
-    out_vm[...] = (middle[...] + red[2].total()).astype(BF)
-    emit(0, out_vm, out_ref)
+    r_q.third(0)
+    r_q.fourth(gq_vm)
+    r_i.done()
+    r_d.third(0)
     r_o.fourth(go_vm)
-    r_j.fourth(gi_vm)
-    r_i.done()
-    r_q.third(0)
-    r_o.done()
-    emit(4, go_vm, go_ref)
-    r_q.fourth(gq_vm)
-    r_q.done()
-    emit(5, gq_vm, gq_ref)
     r_j.done()
+    r_d.fourth(gd_vm)
+    emit(2, gd_vm, gd_ref)
     in_rows = 2 * FF // TOK
     lines[...] = wi_flat[...].astype(F32)
     gain = column(gain2_in)
@@ -1319,6 +1318,10 @@
     sums[...] = total
     emit(3, gi_own, gi_ref)
     emit(6, sums, sums_ref)
+    r_o.done()
+    emit(4, go_vm, go_ref)
+    r_q.done()
+    emit(5, gq_vm, gq_ref)
     g_o.end()
     assert n_sems[0] == N_COPIES
     settle(len(sent))

time: 135 us -> 133 us (0.985)
  Pallas kernels: 134 us -> 132 us
    pallas_call x1, Pallas kernels: 130 us -> 128 us  [block_device(): pl.pallas_call(layer_kernel, out_shape=(jax.ShapeDtypeStruct((TOK, WIDTH)...]
where the time goes in v5:
time: 133 us
  Pallas kernels  132 us (99%)
    pallas_call x1, Pallas kernels, block_device(): pl.pallas_call(layer_kernel, out_shape=(jax.ShapeDtypeStruct((TOK, WIDTH)...  128 us
    pallas_call x1, Pallas kernels, block_device(): pl.pallas_call(finish_kernel, out_shape=(jax.ShapeDtypeStruct((TOK, WIDTH...  3.87 us

profile of v5, /device:TPU:0, one launch (start us, length us, event | category | flops | bytes accessed | tf_op | source)
XLA Modules:
  0.0 132.9 jit_solution(17371246134968318048)
XLA Ops:
  0.6 128.2 %shard_map.170 = (bf16[128,1024]{1,0:T(8,128)(2,1)}, f32[128,1024]{1,0:T(8,128)}, bf16[4,32,768]{2,1,0:T(8,128)(2,1)}, bf16[32,1024]{1,0:T(8,128)(2,1)}, f32[131...) custom-call(bf16[128,1024]{1,0:T(8,128)(2,1)} %bitcast.19, bf16[128,1024]{1,0:T(8,128)(2,1)} %bitcast.20, ...), custom_call_target="tpu_custom_call" | custom-call | tf_op jit(solution)/shard_map/pallas_call | solution.py:1346
  128.8 3.9 %shard_map.171 = (bf16[128,1024]{1,0:T(8,128)(2,1)}, f32[128,1024]{1,0:T(8,128)}, f32[1,32]{1,0:T(1,128)}, f32[768,128]{1,0:T(8,128)}, f32[256,128]{1,0:T(8,128)...) custom-call(bf16[4,32,768]{2,1,0:T(8,128)(2,1)} %get-tuple-element.23.gq_in, ...), custom_call_target="tpu_custom_call" | custom-call | tf_op jit(solution)/shard_map/pallas_call | solution.py:1440

commit v6 on v5

--- a/solution.py
+++ b/solution.py
@@ -1118,14 +1118,14 @@
 
     pl.semaphore_wait(barrier, 6)
     on["s_q"] = spread(wq_in, wq)
+    wide[0:256] = wo_flat[...].astype(F32)
+    for j in range(8):
+        wo_in[:, pl.ds(j * 128, 128)] = wide[pl.ds(j, 32, stride=8), :].astype(BF)
+    g_o.start()
     wide[0 : 8 * PART] = wd_flat[...].astype(F32)
     wide[8 * PART : 8 * PAD] = jnp.zeros((8 * (PAD - PART), TOK), F32)
     for j in range(8):
         wd[zh, y, x, :, pl.ds(j * 128, 128)] = wide[pl.ds(j, PAD, stride=8), :].astype(BF)
-    wide[0:256] = wo_flat[...].astype(F32)
-    for j in range(8):
-        wo_in[:, pl.ds(j * 128, 128)] = wide[pl.ds(j, 32, stride=8), :].astype(BF)
-    g_o.start()
     g_d.own_first()
     in_rows = 2 * FF // TOK
     lines[...] = wi_flat[...].astype(F32)
@@ -1137,8 +1137,6 @@
             tile = moved(in_moves(r, u), lambda t: wide[pl.ds(t * 32, 32), :])
             wi_in[r, :, pl.ds(u * 128, 128)] = tile.astype(BF)
     wi[z, y, x, c] = wi_in[role]
-    g_o.across()
-    on["s_i"] = spread(wi_in, wi)
     tokens = x_ref[...].astype(F32)
     centred = tokens - jnp.mean(tokens, axis=-1, keepdims=True)
     inv = lax.rsqrt(jnp.mean(centred * centred, axis=-1, keepdims=True) + EPSILON)
@@ -1150,50 +1148,50 @@
     cot[zp, c] = cot_in[...]
     for cp in on["s_q"]:
         cp.wait_recv()
+    g_q.own_first()
+    g_o.across()
+    on["s_i"] = spread(wi_in, wi)
+    g_o.first()
     g_q.across()
-    g_q.own_first()
     on["n1"] = Share(n1)
     g_d.own_second()
-    g_o.first()
+    g_q.own_second()
+    on["seg"] = [go_copy(seg_buf.at[zp, c], seg_buf.at[zp, c], dev) for dev, _, _ in others]
+    g_q.far_first()
+    g_o.second()
     for cp in on["s_i"]:
         cp.wait_recv()
-    on["seg"] = [go_copy(seg_buf.at[zp, c], seg_buf.at[zp, c], dev) for dev, _, _ in others]
-    g_q.own_second()
-    g_q.far_first()
-    g_o.second()
     g_i.across()
-    on["cot"] = Share(cot)
     g_q.far_second()
     g_i.own_first()
-    g_j.own_first()
+    on["cot"] = Share(cot)
     g_j.across()
     on["n1"].forward()
+    on["n1"].core()
+    g_j.own_first()
     g_q.done()
+    on["n1"].done()
     g_i.far_first()
-    on["n1"].core()
-    on["cot"].core()
     for cp in on["seg"]:
         cp.wait_recv()
-    g_o.done()
-    on["n1"].done()
     lax.fori_loop(1 - zp, 2 - zp, qkv_step, 0)
     lax.fori_loop(2 * (1 - zp), 2 * (1 - zp) + 2, attend, 0)
+    g_o.done()
+    lax.fori_loop(zp, zp + 1, qkv_step, 0)
     lax.fori_loop(1 - zp, 2 - zp, branch, 0)
     red[0].far_terms()
     g_i.own_second()
-    lax.fori_loop(zp, zp + 1, qkv_step, 0)
+    red[0].cross()
+    g_j.far_first()
     g_i.far_second()
-    red[0].cross()
     g_d.across()
     lax.fori_loop(2 * zp, 2 * zp + 2, attend, 0)
-    on["cot"].forward()
-    g_j.far_first()
     g_j.own_second()
     lax.fori_loop(zp, zp + 1, branch, 0)
     red[0].near_terms()
-    on["cot"].done()
     g_d.far_first()
-    g_j.far_second()
+    on["cot"].forward()
+    g_i.done()
     mid = x_ref[...].astype(F32) + red[0].total()
     middle[...] = mid
     centred = mid - jnp.mean(mid, axis=-1, keepdims=True)
@@ -1203,14 +1201,16 @@
     inv2[...] = jnp.broadcast_to(inv, (TOK, 128))
     n2[zp, c] = unit.astype(BF)
     on["n2"] = Share(n2)
-    g_i.done()
+    g_j.far_second()
+    g_d.far_second()
+    on["n2"].core()
+    on["cot"].core()
     on["n2"].forward()
-    g_d.far_second()
     g_j.done()
-    on["n2"].core()
-    on["n2"].done()
+    on["cot"].done()
     on["mark"] = len(sent)
     upper_for(zp)
+    on["n2"].done()
     upper_for(1 - zp)
     lax.fori_loop(0, 2, down_grad, 0)
     r_d.first(1)
@@ -1225,13 +1225,12 @@
     r_d.second(1)
     in_grad_for(0, 2 * (1 - zh))
     r_i.first(1)
+    lax.fori_loop(1 - zp, 2 - zp, down, 0)
+    red[2].far_terms()
     normed_two_grad_for(zp)
     red[1].near_terms()
-    lax.fori_loop(zp, zp + 1, down, 0)
-    red[2].near_terms()
     r_j.second(1)
-    lax.fori_loop(1 - zp, 2 - zp, down, 0)
-    red[2].far_terms()
+    in_grad_for(HID, 2 * zh)
     settle(on["mark"])
     e = red[1].total()
     n = unit2[...]
@@ -1243,30 +1242,29 @@
     dmid[...] = d_middle
     db[zp, c] = d_middle.astype(BF)
     on["db"] = Share(db)
-    r_d.first(0)
     red[2].cross()
+    lax.fori_loop(zp, zp + 1, down, 0)
+    red[2].near_terms()
+    r_d.third(1)
     in_grad_for(0, 2 * zh)
-    r_d.third(1)
+    on["db"].core()
     r_i.first(0)
     r_i.second(1)
-    on["db"].core()
-    in_grad_for(HID, 2 * zh)
+    r_j.first(0)
     r_j.third(1)
-    r_j.first(0)
+    lax.fori_loop(zp, zp + 1, attended_grad, 0)
+    r_d.first(0)
+    lax.fori_loop(2 * zp, 2 * zp + 2, attend_back, 0)
     on["db"].forward()
     on["db"].done()
     lax.fori_loop(1 - zp, 2 - zp, attended_grad, 0)
     lax.fori_loop(2 * (1 - zp), 2 * (1 - zp) + 2, attend_back, 0)
-    lax.fori_loop(zp, zp + 1, attended_grad, 0)
-    lax.fori_loop(2 * zp, 2 * zp + 2, attend_back, 0)
+    lax.fori_loop(2 * (1 - zh), 2 * (1 - zh) + 2, qkv_grad, 0)
+    first_grads_for(zp)
+    red[3].near_terms()
     first_grads_for(1 - zp)
     red[3].far_terms()
-    lax.fori_loop(2 * (1 - zh), 2 * (1 - zh) + 2, qkv_grad, 0)
-    r_q.first(1)
-    r_i.second(0)
-    out_vm[...] = (middle[...] + red[2].total()).astype(BF)
-    emit(0, out_vm, out_ref)
-    r_i.third(1)
+    r_j.second(0)
     lhs = att
     for j in range(2):
         for half in range(2):
@@ -1275,22 +1273,17 @@
                 matmul_tn(lhs[:, j].reshape(512, 128), rhs).astype(BF).reshape(2, 2, 32, 512)
             )
     red[3].cross()
+    r_i.third(1)
+    r_q.first(1)
+    r_i.second(0)
+    r_j.third(0)
     lax.fori_loop(2 * zh, 2 * zh + 2, qkv_grad, 0)
     r_q.second(1)
-    r_j.second(0)
+    r_o.first()
+    r_q.first(0)
+    r_q.third(1)
     r_i.third(0)
-    first_grads_for(zp)
-    red[3].near_terms()
-    r_o.first()
-    r_q.third(1)
-    r_j.third(0)
-    r_q.first(0)
-    r_j.fourth(gi_vm)
     r_o.second()
-    r_i.fourth(gi_vm)
-    r_q.second(0)
-    r_d.second(0)
-    r_o.third()
     e = red[3].total()
     n = unit1[...]
     ig_vm[...] = dmid[...] + inv1[:, 0:1] * (
@@ -1299,14 +1292,17 @@
         - n * jnp.mean(e * n, axis=-1, keepdims=True)
     )
     emit(1, ig_vm, ig_ref)
+    r_i.fourth(gi_vm)
+    r_j.fourth(gi_vm)
+    r_q.second(0)
+    out_vm[...] = (middle[...] + red[2].total()).astype(BF)
+    emit(0, out_vm, out_ref)
+    r_o.third()
+    r_i.done()
+    r_d.second(0)
     r_q.third(0)
     r_q.fourth(gq_vm)
-    r_i.done()
-    r_d.third(0)
-    r_o.fourth(go_vm)
     r_j.done()
-    r_d.fourth(gd_vm)
-    emit(2, gd_vm, gd_ref)
     in_rows = 2 * FF // TOK
     lines[...] = wi_flat[...].astype(F32)
     gain = column(gain2_in)
@@ -1318,10 +1314,14 @@
     sums[...] = total
     emit(3, gi_own, gi_ref)
     emit(6, sums, sums_ref)
+    r_o.fourth(go_vm)
+    r_d.third(0)
+    r_d.fourth(gd_vm)
+    emit(2, gd_vm, gd_ref)
+    r_q.done()
+    emit(5, gq_vm, gq_ref)
     r_o.done()
     emit(4, go_vm, go_ref)
-    r_q.done()
-    emit(5, gq_vm, gq_ref)
     g_o.end()
     assert n_sems[0] == N_COPIES
     settle(len(sent))

time: 133 us -> 132 us (level)
  no operation moved by 1% of the time
where the time goes in v6:
time: 132 us
  Pallas kernels  131 us (99%)
    pallas_call x1, Pallas kernels, block_device(): pl.pallas_call(layer_kernel, out_shape=(jax.ShapeDtypeStruct((TOK, WIDTH)...  127 us
    pallas_call x1, Pallas kernels, block_device(): pl.pallas_call(finish_kernel, out_shape=(jax.ShapeDtypeStruct((TOK, WIDTH...  3.87 us

profile of v6, /device:TPU:0, one launch (start us, length us, event | category | flops | bytes accessed | tf_op | source)
XLA Modules:
  0.0 131.9 jit_solution(12072602590163258722)
XLA Ops:
  0.6 127.2 %shard_map.170 = (bf16[128,1024]{1,0:T(8,128)(2,1)}, f32[128,1024]{1,0:T(8,128)}, bf16[4,32,768]{2,1,0:T(8,128)(2,1)}, bf16[32,1024]{1,0:T(8,128)(2,1)}, f32[131...) custom-call(bf16[128,1024]{1,0:T(8,128)(2,1)} %bitcast.19, bf16[128,1024]{1,0:T(8,128)(2,1)} %bitcast.20, ...), custom_call_target="tpu_custom_call" | custom-call | tf_op jit(solution)/shard_map/pallas_call | solution.py:1346
  127.9 3.9 %shard_map.171 = (bf16[128,1024]{1,0:T(8,128)(2,1)}, f32[128,1024]{1,0:T(8,128)}, f32[1,32]{1,0:T(1,128)}, f32[768,128]{1,0:T(8,128)}, f32[256,128]{1,0:T(8,128)...) custom-call(bf16[4,32,768]{2,1,0:T(8,128)(2,1)} %get-tuple-element.23.gq_in, ...), custom_call_target="tpu_custom_call" | custom-call | tf_op jit(solution)/shard_map/pallas_call | solution.py:1440

commit v7 on v6

--- a/solution.py
+++ b/solution.py
@@ -620,6 +620,7 @@
             cp.wait_send()
             free.append(k)
         del sent[:first]
+        free.sort()
 
     def go_copy(src, dst, dev):
         cp = copy_to(src, dst, dev)
@@ -1475,7 +1476,7 @@
 
 
 N_COPIES = 142
-N_SENDS = 100
+N_SENDS = 89
 PIECES = 2
 
 

time: 132 us -> 132 us (level)
  no operation moved by 1% of the time
where the time goes in v7:
time: 132 us
  Pallas kernels  131 us (99%)
    pallas_call x1, Pallas kernels, block_device(): pl.pallas_call(layer_kernel, out_shape=(jax.ShapeDtypeStruct((TOK, WIDTH)...  127 us
    pallas_call x1, Pallas kernels, block_device(): pl.pallas_call(finish_kernel, out_shape=(jax.ShapeDtypeStruct((TOK, WIDTH...  3.87 us

profile of v7, /device:TPU:0, one launch (start us, length us, event | category | flops | bytes accessed | tf_op | source)
XLA Modules:
  0.0 131.8 jit_solution(14613359819868091708)
XLA Ops:
  0.6 127.1 %shard_map.170 = (bf16[128,1024]{1,0:T(8,128)(2,1)}, f32[128,1024]{1,0:T(8,128)}, bf16[4,32,768]{2,1,0:T(8,128)(2,1)}, bf16[32,1024]{1,0:T(8,128)(2,1)}, f32[131...) custom-call(bf16[128,1024]{1,0:T(8,128)(2,1)} %bitcast.19, bf16[128,1024]{1,0:T(8,128)(2,1)} %bitcast.20, ...), custom_call_target="tpu_custom_call" | custom-call | tf_op jit(solution)/shard_map/pallas_call | solution.py:1347
  127.8 3.9 %shard_map.171 = (bf16[128,1024]{1,0:T(8,128)(2,1)}, f32[128,1024]{1,0:T(8,128)}, f32[1,32]{1,0:T(1,128)}, f32[768,128]{1,0:T(8,128)}, f32[256,128]{1,0:T(8,128)...) custom-call(bf16[4,32,768]{2,1,0:T(8,128)(2,1)} %get-tuple-element.23.gq_in, ...), custom_call_target="tpu_custom_call" | custom-call | tf_op jit(solution)/shard_map/pallas_call | solution.py:1441
